TPU v7x, 32 devices: a whole 2x2x4 slice. The times are simulated.
32 devices in a mesh: blk: 2 (over core), cells: 16 (over z, y, x).
Axes of the slice: x: 2, y: 2, z: 4, core: 2. Of those that a mesh axis runs over, the one named last changes fastest.
Arguments:
- tokens: bfloat16 [1024, 32, 1120], P('blk', 'cells'), may hold values from -6 to 6
- lengths: int32 [32], P('cells'), may hold values from 512 to 1024, as said below
- attn_gain: float32 [1120], replicated, may hold values from 0.5 to 1.5
- attn_bias: float32 [1120], replicated, may hold values from -1.75 to 1.75
- w_qkv: bfloat16 [1120, 3360], replicated, may hold values from -0.1875 to 0.1875
- w_out: bfloat16 [1120, 1120], replicated, may hold values from -2 to 2
- mlp_gain: float32 [1120], replicated, may hold values from 0.5 to 1.5
- mlp_bias: float32 [1120], replicated, may hold values from -1.75 to 1.75
- w_up: bfloat16 [1120, 4480], replicated, may hold values from -0.1875 to 0.1875
- w_down: bfloat16 [4480, 1120], replicated, may hold values from -0.09375 to 0.09375
- cotangent: bfloat16 [1024, 32, 1120], P('blk', 'cells'), may hold values from -6 to 6
Outputs:
- mixed: bfloat16 [1024, 32, 1120], P('blk', 'cells')
- tokens_grad: bfloat16 [1024, 32, 1120], P('blk', 'cells')
- attn_gain_grad: float32 [1120], replicated
- attn_bias_grad: float32 [1120], replicated
- w_qkv_grad: float32 [1120, 3360], P('cells', 'blk')
- w_out_grad: float32 [1120, 1120], P('cells', 'blk')
- mlp_gain_grad: float32 [1120], replicated
- mlp_bias_grad: float32 [1120], replicated
- w_up_grad: float32 [1120, 4480], P('cells', 'blk')
- w_down_grad: float32 [4480, 1120], P('cells', 'blk')
Inputs may be any that keep to these rules, and one draw needn't show every extreme that they name: `lengths`: in every aligned group of 2 cells one cell, drawn at random, has length 1024.
All inputs are finite; a program needn't handle non-finite values.
Results may differ from a plain program's by a relative error of at most 0.017.
Values may be sent and summed in bfloat16 or wider, within the bound.
No kernel may reach another device: no remote copies, remote signals or barrier semaphores. Data moves between devices by JAX's collectives and lax.ppermute only.
A program may use at most 384 MiB of HBM per device.

v0:
```python
import jax
import jax.numpy as jnp
from jax import lax
from jax.sharding import PartitionSpec as P

D = 1120
HEADS = 20
HD = 56


EPSILON = 1e-05
MASKED = -1e30


def norm_forward(values_in, gain_vec, bias_vec):
    centred = values_in - jnp.mean(values_in, axis=-1, keepdims=True)
    inverse = lax.rsqrt(jnp.mean(centred * centred, axis=-1, keepdims=True) + EPSILON)
    normed = centred * inverse
    return (normed, inverse, normed * gain_vec + bias_vec)


def norm_backward(grad_in, normed, inverse, gain_vec):
    scaled = grad_in * gain_vec
    grad_out = inverse * (
        scaled
        - jnp.mean(scaled, axis=-1, keepdims=True)
        - normed * jnp.mean(scaled * normed, axis=-1, keepdims=True)
    )
    return (grad_out, jnp.sum(grad_in * normed, axis=(0, 1)), jnp.sum(grad_in, axis=(0, 1)))


def key_scores(query_heads, key_piece, query_pos, key_start, lengths):
    key_count = key_piece.shape[0]
    key_heads = key_piece.reshape(key_count, key_piece.shape[1], HEADS, HD)
    scores = jnp.einsum(
        "qchd,kchd->chqk", query_heads, key_heads, preferred_element_type=jnp.float32
    ) * HD ** (-0.5)
    key_pos = key_start + jnp.arange(key_count, dtype=jnp.int32)
    allowed = (key_pos[None, None, :] <= query_pos[None, :, None]) & (
        key_pos[None, None, :] < lengths[:, None, None]
    )
    allowed = allowed[:, None, :, :]
    return (jnp.where(allowed, scores, MASKED), allowed)


def key_sweep(step_fn, initial, pieces, row_count, block_turns):

    def one_turn(turn_index, state_in):
        row_start = turn_index * row_count
        taken = tuple(
            (lax.dynamic_slice_in_dim(full_array, row_start, row_count, 0) for full_array in pieces)
        )
        return step_fn(state_in, taken, row_start)

    return lax.fori_loop(0, block_turns, one_turn, initial)


def per_device(
    tokens, lengths, attn_gain, attn_bias, w_qkv, w_out, mlp_gain, mlp_bias, w_up, w_down, cotangent
):
    row_count = tokens.shape[0]
    cell_count = tokens.shape[1]
    block_turns = lax.axis_size("blk")
    score_scale = HD ** (-0.5)
    query_pos = lax.axis_index("blk") * row_count + jnp.arange(row_count, dtype=jnp.int32)
    inputs = tokens.astype(jnp.float32)
    normed_one, inverse_one, pre_one = norm_forward(inputs, attn_gain, attn_bias)
    normed_low = pre_one.astype(jnp.bfloat16)
    qkv_vals = jnp.einsum(
        "rcd,de->rce", normed_low, w_qkv, preferred_element_type=jnp.float32
    ).astype(jnp.bfloat16)
    key_vals = qkv_vals[..., D : 2 * D]
    value_vals = qkv_vals[..., 2 * D :]
    query_heads = qkv_vals[..., :D].reshape(row_count, cell_count, HEADS, HD)
    start_max = jnp.full((cell_count, HEADS, row_count), MASKED, jnp.float32)
    start_sum = jnp.zeros((cell_count, HEADS, row_count), jnp.float32)
    start_out = jnp.zeros((row_count, cell_count, HEADS, HD), jnp.float32)
    scores, allowed = key_scores(
        query_heads,
        (lax.all_gather(key_vals, "blk", axis=0, tiled=True),)[0],
        query_pos,
        jnp.int32(0),
        lengths,
    )
    new_max = jnp.maximum(start_max, jnp.max(scores, axis=-1))
    weights = jnp.where(allowed, jnp.exp(scores - new_max[..., None]), 0.0)
    run_sum = jnp.sum(weights, axis=-1)
    log_total = new_max + jnp.log(run_sum)

    def probabilities(key_piece, key_start):
        scores, allowed = key_scores(query_heads, key_piece, query_pos, key_start, lengths)
        return jnp.where(allowed, jnp.exp(scores - log_total[..., None]), 0.0)

    pieces = (
        lax.all_gather(key_vals, "blk", axis=0, tiled=True),
        lax.all_gather(value_vals, "blk", axis=0, tiled=True),
    )
    prob_vals = probabilities(pieces[0], jnp.int32(0)).astype(jnp.bfloat16)
    value_heads = pieces[1].reshape(pieces[1].shape[0], cell_count, HEADS, HD)
    out_acc = jnp.einsum(
        "chqk,kchd->qchd", prob_vals, value_heads, preferred_element_type=jnp.float32
    )
    attended = out_acc.reshape(row_count, cell_count, D).astype(jnp.bfloat16)
    hidden = inputs + jnp.einsum("rcd,de->rce", attended, w_out, preferred_element_type=jnp.float32)
    normed_two, inverse_two, pre_two = norm_forward(hidden, mlp_gain, mlp_bias)
    normed_mlp = pre_two.astype(jnp.bfloat16)
    upward = jnp.einsum("rcd,df->rcf", normed_mlp, w_up, preferred_element_type=jnp.float32)
    activated_full, gelu_back = jax.vjp(
        lambda value_in: jax.nn.gelu(value_in, approximate=True), upward
    )
    activated = activated_full.astype(jnp.bfloat16)
    mixed = (
        hidden + jnp.einsum("rcf,fd->rcd", activated, w_down, preferred_element_type=jnp.float32)
    ).astype(jnp.bfloat16)
    valid_rows = (query_pos[:, None] < lengths[None, :]).astype(jnp.float32)
    grad_out = cotangent.astype(jnp.float32) * valid_rows[..., None]
    grad_low = grad_out.astype(jnp.bfloat16)
    w_down_grad = jnp.einsum("rcf,rcd->fd", activated, grad_low, preferred_element_type=jnp.float32)
    grad_act = jnp.einsum("rcd,fd->rcf", grad_low, w_down, preferred_element_type=jnp.float32)
    grad_upward = gelu_back(grad_act)[0].astype(jnp.bfloat16)
    w_up_grad = jnp.einsum(
        "rcd,rcf->df", normed_mlp, grad_upward, preferred_element_type=jnp.float32
    )
    grad_normed_two = jnp.einsum(
        "rcf,df->rcd", grad_upward, w_up, preferred_element_type=jnp.float32
    )
    grad_hidden_ln, mlp_gain_grad, mlp_bias_grad = norm_backward(
        grad_normed_two, normed_two, inverse_two, mlp_gain
    )
    grad_hidden = grad_out + grad_hidden_ln
    grad_branch = grad_hidden.astype(jnp.bfloat16)
    w_out_grad = jnp.einsum(
        "rce,rcd->ed", attended, grad_branch, preferred_element_type=jnp.float32
    )
    grad_attended = jnp.einsum(
        "rcd,ed->rce", grad_branch, w_out, preferred_element_type=jnp.float32
    ).astype(jnp.bfloat16)
    grad_heads = grad_attended.reshape(row_count, cell_count, HEADS, HD)
    whole_keys, whole_values = (
        lax.all_gather(key_vals, "blk", axis=0, tiled=True),
        lax.all_gather(value_vals, "blk", axis=0, tiled=True),
    )

    def attention_grads(key_piece, value_piece, key_start):
        prob_full = probabilities(key_piece, key_start)
        value_heads = value_piece.reshape(value_piece.shape[0], cell_count, HEADS, HD)
        dprobs = jnp.einsum(
            "qchd,kchd->chqk", grad_heads, value_heads, preferred_element_type=jnp.float32
        )
        return (prob_full, dprobs)

    def delta_step(state_in, pieces, key_start):
        prob_full, dprobs = attention_grads(pieces[0], pieces[1], key_start)
        return state_in + jnp.sum(prob_full * dprobs, axis=-1)

    row_delta = key_sweep(delta_step, start_sum, (whole_keys, whole_values), row_count, block_turns)

    def query_step(state_in, pieces, key_start):
        prob_full, dprobs = attention_grads(pieces[0], pieces[1], key_start)
        dscore = (prob_full * (dprobs - row_delta[..., None])).astype(jnp.bfloat16)
        key_heads = pieces[0].reshape(pieces[0].shape[0], cell_count, HEADS, HD)
        return state_in + jnp.einsum(
            "chqk,kchd->qchd", dscore, key_heads, preferred_element_type=jnp.float32
        )

    query_acc = key_sweep(query_step, start_out, (whole_keys, whole_values), row_count, block_turns)
    grad_queries = (query_acc * score_scale).reshape(row_count, cell_count, D).astype(jnp.bfloat16)
    key_piece = whole_keys
    value_piece = whole_values
    prob_full, dprobs = attention_grads(key_piece, value_piece, jnp.int32(0))
    dscore = (prob_full * (dprobs - row_delta[..., None])).astype(jnp.bfloat16)
    grad_keys = (
        jnp.einsum("chqk,qchd->kchd", dscore, query_heads, preferred_element_type=jnp.float32)
        * score_scale
    )
    grad_values = jnp.einsum(
        "chqk,qchd->kchd",
        prob_full.astype(jnp.bfloat16),
        grad_heads,
        preferred_element_type=jnp.float32,
    )
    kv_summed = lax.psum_scatter(
        jnp.concatenate(
            [
                grad_keys.reshape(row_count * lax.axis_size("blk"), cell_count, D),
                grad_values.reshape(row_count * lax.axis_size("blk"), cell_count, D),
            ],
            axis=-1,
        ),
        "blk",
        scatter_dimension=0,
        tiled=True,
    )
    grad_qkv = jnp.concatenate([grad_queries, kv_summed.astype(jnp.bfloat16)], axis=-1)
    w_qkv_grad = jnp.einsum("rcd,rce->de", normed_low, grad_qkv, preferred_element_type=jnp.float32)
    grad_normed_one = jnp.einsum("rce,de->rcd", grad_qkv, w_qkv, preferred_element_type=jnp.float32)
    grad_inputs_ln, attn_gain_grad, attn_bias_grad = norm_backward(
        grad_normed_one, normed_one, inverse_one, attn_gain
    )
    tokens_grad = (grad_hidden + grad_inputs_ln).astype(jnp.bfloat16)
    norm_sums = lax.psum(
        (attn_gain_grad, attn_bias_grad, mlp_gain_grad, mlp_bias_grad), ("blk", "cells")
    )
    shares = (
        lax.psum_scatter(
            w_qkv_grad.astype(jnp.bfloat16), "cells", scatter_dimension=0, tiled=True
        ).astype(jnp.float32),
        lax.psum_scatter(
            w_out_grad.astype(jnp.bfloat16), "cells", scatter_dimension=0, tiled=True
        ).astype(jnp.float32),
        lax.psum_scatter(
            w_up_grad.astype(jnp.bfloat16), "cells", scatter_dimension=0, tiled=True
        ).astype(jnp.float32),
        lax.psum_scatter(
            w_down_grad.astype(jnp.bfloat16), "cells", scatter_dimension=0, tiled=True
        ).astype(jnp.float32),
    )
    summed = (
        lax.psum_scatter(
            shares[0].astype(jnp.bfloat16), "blk", scatter_dimension=1, tiled=True
        ).astype(jnp.float32),
        lax.psum_scatter(
            shares[1].astype(jnp.bfloat16), "blk", scatter_dimension=1, tiled=True
        ).astype(jnp.float32),
        lax.psum_scatter(
            shares[2].astype(jnp.bfloat16), "blk", scatter_dimension=1, tiled=True
        ).astype(jnp.float32),
        lax.psum_scatter(
            shares[3].astype(jnp.bfloat16), "blk", scatter_dimension=1, tiled=True
        ).astype(jnp.float32),
    )
    return (
        mixed,
        tokens_grad,
        norm_sums[0],
        norm_sums[1],
        summed[0],
        summed[1],
        norm_sums[2],
        norm_sums[3],
        summed[2],
        summed[3],
    )


def solution(mesh):
    placed = (
        P("blk", "cells", None),
        P("cells"),
        P(),
        P(),
        P(),
        P(),
        P(),
        P(),
        P(),
        P(),
        P("blk", "cells", None),
    )
    return jax.shard_map(
        per_device,
        mesh=mesh,
        in_specs=placed,
        out_specs=(
            P("blk", "cells", None),
            P("blk", "cells", None),
            P(),
            P(),
            P("cells", "blk"),
            P("cells", "blk"),
            P(),
            P(),
            P("cells", "blk"),
            P("cells", "blk"),
        ),
        check_vma=False,
    )
```

profile of v0, /device:TPU:0, one launch (start us, length us, event | category | flops | bytes accessed | tf_op | source)
XLA Modules:
  0.0 1227.0 jit_solution(11404623908044035054)
XLA Ops:
  11.8 12.9 %fusion.52 = bf16[512,2,3360]{0,2,1:T(8,128)(2,1)S(1)} fusion(bf16[1120,3360]{1,0:T(8,128)(2,1)} %param.19, bf16[512,2,1120]{0,2,1:T(8,128)(2,1)S(1)} %copy-done.5, f32[1120]{0:T(1024)S(1)} %copy-done.36, f32[1120]{0:T(1024)S(1)} %copy-done.29, f32[512,2]{0,1:T(2,128)S(1)} %add_rsqrt_fusion.1, f32[512,2]{0,1:T(2,128)S(1)} %broadcast_multiply_fusion.6), kind=kOutput, calls=%fused_computation.74 | convolution fusion | flops 7717355520 | bytes 16718592 | tf_op jit(solution)/shard_map/rcd,de->rce/dot_general | solution.py:69
  24.7 3.1 fusion.95
  30.8 14.1 %all-gather.5.cloned.1.call-done = bf16[1024,2,1120]{0,2,1:T(8,128)(2,1)} async-done(((bf16[512,2,1120]{0,2,1:T(8,128)(2,1)}), bf16[1024,2,1120]{0,2,1:T(8,128)(2,1)}) %all-gather.5.cloned.1.call-update) | async-done | bytes 4587536 | tf_op jit(solution)/shard_map/all_gather | solution.py:95
  44.9 36.2 %fusion.26 = (f32[2,20,512]{2,1,0:T(8,128)S(1)}, f32[2,20,512,1024]{3,2,1,0:T(8,128)}) fusion(pred[2,512,1024]{2,1,0:T(8,128)(4,1)} %broadcast_and_fusion.2, bf16[512,2,20,56]{0,3,2,1:T(8,128)(2,1)} %bitcast.181, bf16[1024,2,20,56]{0,3,2,1:T(8,128)(2,1)} %bitcast.186), kind=kOutput, calls=%fused_computation.41 | convolution fusion | flops 2411704320 | bytes 91897856 | tf_op jit(solution)/shard_map/qchd,kchd->chqk/dot_general | solution.py:35
  81.1 37.0 %select_reduce_fusion = f32[2,20,512]{2,1,0:T(8,128)S(1)} fusion(f32[2,20,512,1024]{3,2,1,0:T(8,128)} %get-tuple-element.492, f32[2,20,512]{2,1,0:T(8,128)S(1)} %broadcast_maximum_fusion, pred[2,512,1024]{2,1,0:T(8,128)(4,1)} %broadcast_and_fusion.2), kind=kLoop, calls=%fused_computation.38 | loop fusion | flops 104837120 | bytes 85098496 | tf_op jit(solution)/shard_map/reduce_sum | solution.py:87
  118.2 34.9 %convolution_convert_fusion.1 = bf16[2,20,56,512]{3,2,1,0:T(8,128)(2,1)} fusion(bf16[1024,2,20,56]{0,3,2,1:T(8,128)(2,1)} %bitcast.187, f32[2,20,512,1024]{3,2,1,0:T(8,128)} %get-tuple-element.492, f32[2,20,512]{2,1,0:T(8,128)S(1)} %log_add_fusion, pred[2,512,1024]{2,1,0:T(8,128)(4,1)} %broadcast_and_fusion.2), kind=kOutput, calls=%fused_computation.114 | convolution fusion | flops 2454814720 | bytes 91897856 | tf_op jit(solution)/shard_map/chqk,kchd->qchd/dot_general | solution.py:100
  153.1 5.8 fusion.96
  161.1 19.7 %fusion.46 = f32[512,2,4480]{2,0,1:T(8,128)} fusion(bf16[1120,4480]{1,0:T(8,128)(2,1)} %param.23, f32[512,2,1120]{0,2,1:T(8,128)S(1)} %get-tuple-element.494, f32[1120]{0:T(1024)S(1)} %copy-done.34, f32[1120]{0:T(1024)S(1)} %copy-done.27, f32[512,2]{0,1:T(2,128)S(1)} %add_rsqrt_fusion, f32[512,2]{0,1:T(2,128)S(1)} %broadcast_multiply_fusion.5), kind=kOutput, calls=%fused_computation.67 | convolution fusion | flops 10281779200 | bytes 32989952 | tf_op jit(solution)/shard_map/rcd,df->rcf/dot_general | solution.py:107
  180.8 23.3 %fusion.30 = bf16[4480,1120]{1,0:T(8,128)(2,1)} fusion(bf16[512,2,1120]{0,2,1:T(8,128)(2,1)S(1)} %copy-done.12, f32[512,2]{0,1:T(2,128)S(1)} %compare_convert_fusion, f32[512,2,4480]{2,0,1:T(8,128)} %fusion.46), kind=kOutput, calls=%fused_computation.49 | convolution fusion | flops 10325790720 | bytes 30683136 | tf_op jit(solution)/shard_map/rcf,rcd->fd/dot_general | solution.py:118
  204.1 30.4 %fusion.37 = bf16[512,2,4480]{2,0,1:T(8,128)(2,1)} fusion(f32[512,2,4480]{2,0,1:T(8,128)} %fusion.46, bf16[4480,1120]{0,1:T(8,128)(2,1)} %param.24, bf16[512,2,1120]{0,2,1:T(8,128)(2,1)} %param.25, f32[512,2]{0,1:T(2,128)S(1)} %compare_convert_fusion), kind=kOutput, calls=%fused_computation.56 | convolution fusion | flops 10371235840 | bytes 39858176 | tf_op jit(solution)/shard_map/rcd,fd->rcf/dot_general | solution.py:119
  234.6 20.8 %multiply_reduce_fusion = (f32[1120]{0:T(1024)}, f32[512,2]{0,1:T(2,128)S(1)}, f32[512,2]{0,1:T(2,128)S(1)}, f32[1120]{0:T(1024)}, f32[512,2,1120]{0,2,1:T(8,128)S(1)}) fusion(f32[512,2,1120]{0,2,1:T(8,128)} %copy-done.9, f32[512,2]{0,1:T(2,128)S(1)} %add_rsqrt_fusion, f32[512,2]{0,1:T(2,128)S(1)} %broadcast_multiply_fusion.5, f32[1120]{0:T(1024)S(1)} %copy-done.27, ...), kind=kOutput, calls=%fused_computation.96 | convolution fusion | flops 10286362624 | bytes 28415104 | tf_op jit(solution)/shard_map/rcf,df->rcd/dot_general | solution.py:124
  255.4 3.6 multiply_add_fusion
  259.1 4.4 convolution_convert_fusion
  263.5 86.8 %while.28 = (s32[]{:T(128)}, f32[2,20,512]{2,1,0:T(8,128)S(1)}, s32[2]{0:T(128)S(1)}, bf16[1024,2,1120]{0,2,1:T(8,128)(2,1)}, bf16[512,2,20,56]{0,3,2,1:T(8,128)...) while((s32[]{:T(128)}, f32[2,20,512]{2,1,0:T(8,128)S(1)}, ...), condition=%wide.region_10.11_spmd.clone, body=%wide.region_8.0_spmd.clone.sunk | while | flops 2412533760 | bytes 113406184 | solution.py:55
  264.4 4.3 constant_dynamic-slice_fusion.9
  268.7 17.0 %fusion.141 = f32[2,20,512,512]{3,2,1,0:T(8,128)} fusion(bf16[512,2,20,56]{0,3,2,1:T(8,128)(2,1)S(1)} %bitcast.185, bf16[512,2,20,56]{0,3,2,1:T(8,128)(2,1)S(1)} %copy-done.2), kind=kOutput, calls=%fused_computation.141.clone.1 | convolution fusion | flops 1174405120 | bytes 46530560 | tf_op jit(solution)/shard_map/while/body/eval_jaxpr/qchd,kchd->chqk/dot_general | solution.py:35
  285.7 21.5 %fusion.142 = f32[2,20,512]{2,1,0:T(8,128)S(1)} fusion(f32[2,20,512,512]{3,2,1,0:T(8,128)} %fusion.141, f32[2,20,512]{2,1,0:T(8,128)S(1)} %get-tuple-element.662, pred[2,512,512]{1,2,0:T(8,128)(4,1)S(1)} %broadcast_and_fusion.5, bf16[512,2,20,56]{0,3,2,1:T(8,128)(2,1)} %bitcast.190, bf16[512,2,20,56]{0,3,2,1:T(8,128)(2,1)} %get-tuple-element.664), kind=kOutput, calls=%fused_computation.3.clone.1 | convolution fusion | flops 1237299200 | bytes 47218688 | tf_op jit(solution)/shard_map/while/body/eval_jaxpr/qchd,kchd->chqk/dot_general | solution.py:147
  307.9 4.3 constant_dynamic-slice_fusion.9
  312.2 16.7 %fusion.141 = f32[2,20,512,512]{3,2,1,0:T(8,128)} fusion(bf16[512,2,20,56]{0,3,2,1:T(8,128)(2,1)S(1)} %bitcast.185, bf16[512,2,20,56]{0,3,2,1:T(8,128)(2,1)S(1)} %copy-done.2), kind=kOutput, calls=%fused_computation.141.clone.1 | convolution fusion | flops 1174405120 | bytes 46530560 | tf_op jit(solution)/shard_map/while/body/eval_jaxpr/qchd,kchd->chqk/dot_general | solution.py:35
  328.9 21.3 %fusion.142 = f32[2,20,512]{2,1,0:T(8,128)S(1)} fusion(f32[2,20,512,512]{3,2,1,0:T(8,128)} %fusion.141, f32[2,20,512]{2,1,0:T(8,128)S(1)} %get-tuple-element.662, pred[2,512,512]{1,2,0:T(8,128)(4,1)S(1)} %broadcast_and_fusion.5, bf16[512,2,20,56]{0,3,2,1:T(8,128)(2,1)} %bitcast.190, bf16[512,2,20,56]{0,3,2,1:T(8,128)(2,1)} %get-tuple-element.664), kind=kOutput, calls=%fused_computation.3.clone.1 | convolution fusion | flops 1237299200 | bytes 47218688 | tf_op jit(solution)/shard_map/while/body/eval_jaxpr/qchd,kchd->chqk/dot_general | solution.py:147
  350.3 36.2 %fusion.91 = f32[2,20,56,1024]{3,2,1,0:T(8,128)} fusion(bf16[512,2,20,56]{0,3,2,1:T(8,128)(2,1)} %get-tuple-element.753, f32[2,20,512,1024]{3,2,1,0:T(8,128)} %get-tuple-element.492, f32[2,20,512]{2,1,0:T(8,128)S(1)} %get-tuple-element.751, pred[2,512,1024]{2,1,0:T(8,128)(4,1)} %broadcast_and_fusion.2), kind=kOutput, calls=%fused_computation.138 | convolution fusion | flops 2453667840 | bytes 96485376 | tf_op jit(solution)/shard_map/chqk,qchd->kchd/dot_general | solution.py:176
  386.5 44.0 %broadcast_multiply_fusion = f32[2,20,56,1024]{3,2,1,0:T(8,128)} fusion(bf16[512,2,20,56]{0,3,2,1:T(8,128)(2,1)S(1)} %copy-done.3, f32[2,20,512,1024]{3,2,1,0:T(8,128)} %get-tuple-element.492, f32[2,20,512]{2,1,0:T(8,128)S(1)} %get-tuple-element.678, f32[2,20,512]{2,1,0:T(8,128)S(1)} %get-tuple-element.751, pred[2,512,1024]{2,1,0:T(8,128)(4,1)} %broadcast_and_fusion.2, ...), kind=kOutput, calls=%fused_computation.97 | convolution fusion | flops 4846714880 | bytes 103448576 | tf_op jit(solution)/shard_map/chqk,qchd->kchd/dot_general | solution.py:173
  430.5 12.6 %pad_maximum_fusion = f32[1024,2,2240]{0,2,1:T(8,128)} fusion(f32[1024,2,1120]{0,2,1:T(8,128)} %bitcast.193, f32[1024,2,1120]{0,2,1:T(8,128)} %bitcast.194), kind=kLoop, calls=%fused_computation.57 | loop fusion | flops 4587520 | bytes 36700160 | tf_op jit(solution)/shard_map/concatenate | solution.py:183
  444.9 101.3 %while.29 = (s32[]{:T(128)}, f32[512,2,20,56]{0,3,2,1:T(8,128)}, bf16[1024,2,1120]{0,2,1:T(8,128)(2,1)}, s32[2]{0:T(128)S(1)}, bf16[512,2,20,56]{0,3,2,1:T(8,128...) while((s32[]{:T(128)}, f32[512,2,20,56]{0,3,2,1:T(8,128)}, ...), condition=%wide.region_12.13_spmd.clone, body=%wide.region_11.12_spmd.clone.sunk | while | flops 3599697920 | bytes 124629240 | solution.py:55
  445.8 4.2 constant_dynamic-slice_fusion.10
  451.4 23.8 %fusion.149 = f32[2,20,512,512]{3,2,1,0:T(8,128)} fusion(bf16[512,2,20,56]{0,3,2,1:T(8,128)(2,1)S(1)} %bitcast.183, bf16[512,2,20,56]{0,3,2,1:T(8,128)(2,1)S(1)} %get-tuple-element.702), kind=kOutput, calls=%fused_computation.142.clone.1 | convolution fusion | flops 1174405120 | bytes 46530560 | tf_op jit(solution)/shard_map/while/body/eval_jaxpr/qchd,kchd->chqk/dot_general | solution.py:35
  475.2 24.0 %bitcast_add_fusion.2 = f32[512,2,20,56]{0,3,2,1:T(8,128)} fusion(f32[512,2,20,56]{0,3,2,1:T(8,128)} %get-tuple-element.685, pred[]{:T(512)S(6)} %compare.7, bf16[512,2,20,56]{0,3,2,1:T(8,128)(2,1)} %bitcast.184, f32[2,20,512,512]{3,2,1,0:T(8,128)} %fusion.149, f32[2,20,512]{2,1,0:T(8,128)S(1)} %get-tuple-element.706, ...), kind=kOutput, calls=%fused_computation.25.clone.1 | convolution fusion | flops 2424504320 | bytes 58687488 | tf_op jit(solution)/shard_map/while/body/eval_jaxpr/chqk,kchd->qchd/dot_general | solution.py:162
  499.8 4.2 constant_dynamic-slice_fusion.10
  505.5 16.2 %fusion.149 = f32[2,20,512,512]{3,2,1,0:T(8,128)} fusion(bf16[512,2,20,56]{0,3,2,1:T(8,128)(2,1)S(1)} %bitcast.183, bf16[512,2,20,56]{0,3,2,1:T(8,128)(2,1)S(1)} %get-tuple-element.702), kind=kOutput, calls=%fused_computation.142.clone.1 | convolution fusion | flops 1174405120 | bytes 46530560 | tf_op jit(solution)/shard_map/while/body/eval_jaxpr/qchd,kchd->chqk/dot_general | solution.py:35
  521.6 24.6 %bitcast_add_fusion.2 = f32[512,2,20,56]{0,3,2,1:T(8,128)} fusion(f32[512,2,20,56]{0,3,2,1:T(8,128)} %get-tuple-element.685, pred[]{:T(512)S(6)} %compare.7, bf16[512,2,20,56]{0,3,2,1:T(8,128)(2,1)} %bitcast.184, f32[2,20,512,512]{3,2,1,0:T(8,128)} %fusion.149, f32[2,20,512]{2,1,0:T(8,128)S(1)} %get-tuple-element.706, ...), kind=kOutput, calls=%fused_computation.25.clone.1 | convolution fusion | flops 2424504320 | bytes 58687488 | tf_op jit(solution)/shard_map/while/body/eval_jaxpr/chqk,kchd->qchd/dot_general | solution.py:162
  546.3 4.5 multiply_convert_fusion.3
  551.3 4.5 fusion.55
  556.3 13.9 %fusion.29 = bf16[1120,4480]{1,0:T(8,128)(2,1)} fusion(bf16[512,2,4480]{2,0,1:T(8,128)(2,1)S(1)} %bitcast.209, f32[512,2,1120]{0,2,1:T(8,128)S(1)} %bitcast.192, f32[1120]{0:T(1024)S(1)} %copy-done.35, f32[1120]{0:T(1024)S(1)} %copy-done.28, f32[512,2]{0,1:T(2,128)S(1)} %copy-done.26, f32[512,2]{0,1:T(2,128)S(1)} %copy-done.22), kind=kOutput, calls=%fused_computation.48 | convolution fusion | flops 10286796800 | bytes 23814912 | tf_op jit(solution)/shard_map/rcd,rcf->df/dot_general | solution.py:121
  572.7 4.4 convert_element_type.126
  579.3 12.7 %fusion.40 = bf16[1120,3360]{1,0:T(8,128)(2,1)} fusion(bf16[512,2,2240]{0,2,1:T(8,128)(2,1)S(1)} %convert_element_type.126, bf16[512,2,1120]{0,2,1:T(8,128)(2,1)S(1)} %bitcast.199, bf16[512,2,1120]{0,2,1:T(8,128)(2,1)S(1)} %copy-done.6, f32[1120]{0:T(1024)S(1)} %copy-done.37, f32[1120]{0:T(1024)S(1)} %copy-done.30, f32[512,2]{0,1:T(2,128)S(1)} %copy-done.24, ...), kind=kOutput, calls=%fused_computation.61 | convolution fusion | flops 7731440640 | bytes 16718592 | tf_op jit(solution)/shard_map/rcd,rce->de/dot_general | solution.py:195
  591.9 478.1 %fusion.94 = (bf16[80,3360]{1,0:T(8,128)(2,1)}, bf16[80,1120]{1,0:T(8,128)(2,1)S(1)}, bf16[80,4480]{1,0:T(8,128)(2,1)S(1)}) fusion(bf16[1120,3360]{1,0:T(8,128)(2,1)} %fusion.40, bf16[1120,1120]{1,0:T(8,128)(2,1)} %fusion.55, bf16[1120,4480]{1,0:T(8,128)(2,1)} %fusion.29), kind=kCustom, calls=%all-reduce-scatter.3 | all-reduce-scatter fusion | flops 11468801 | bytes 21504512
  1074.3 3.4 collective-permute-start
  1077.7 4.1 collective-permute-start.3
  1081.9 2.4 collective-permute-start.1
  1084.3 19.8 %fusion.75 = bf16[512,2,1120]{0,2,1:T(8,128)(2,1)} fusion(f32[512,2,1120]{0,2,1:T(8,128)} %copy-done.9, bf16[4480,1120]{0,1:T(8,128)(2,1)} %param.24, f32[512,2,4480]{2,0,1:T(8,128)} %fusion.46), kind=kOutput, calls=%fused_computation.108 | convolution fusion | flops 10319626240 | bytes 35266560 | tf_op jit(solution)/shard_map/rcf,fd->rcd/dot_general | solution.py:113
  1108.9 5.0 collective-permute-start.4
  1116.0 4.6 concatenate.9
  1122.6 11.8 concatenate.8
  1136.3 2.3 copy.42
  1138.6 16.2 %fusion.72 = (f32[1120]{0:T(1024)S(1)}, f32[512,2]{0,1:T(2,128)S(1)}, f32[512,2]{0,1:T(2,128)S(1)}, f32[1120]{0:T(1024)S(1)}, f32[512,2,1120]{0,2,1:T(8,128)}) fusion(bf16[512,2,1120]{0,2,1:T(8,128)(2,1)S(1)} %copy-done.6, f32[512,2]{0,1:T(2,128)S(1)} %copy-done.24, f32[512,2]{0,1:T(2,128)S(1)} %copy-done.20, f32[1120]{0:T(1024)S(1)} %copy-done.30, ...), kind=kOutput, calls=%fused_computation.94 | convolution fusion | flops 7732260864 | bytes 21318784 | tf_op jit(solution)/shard_map/rce,de->rcd/dot_general | solution.py:196
  1154.9 11.7 concatenate.10
  1168.4 38.9 %all-reduce.7 = (f32[1120]{0:T(1024)}, f32[1120]{0:T(1024)}, f32[1120]{0:T(1024)}, f32[1120]{0:T(1024)}) all-reduce(f32[1120]{0:T(1024)S(1)} %get-tuple-element.426, f32[1120]{0:T(1024)S(1)} %get-tuple-element.431, f32[1120]{0:T(1024)S(1)} %copy-done.31, f32[1120]{0:T(1024)S(1)} %copy-done.32), channel_id=1, replica_groups=mesh['blk'=2,'cells'=16] {'blk','cells'}, use_global_device_ids=true, to_apply=%region_17.18 | all-reduce | flops 4480 | bytes 35840 | tf_op jit(solution)/shard_map/psum | solution.py:201
  1207.2 6.4 fusion.71
  (180 shorter events, 44.8 us)
Async XLA Ops:
  7.2 145.9 %copy-start = (bf16[1120,1120]{1,0:T(8,128)(2,1)S(1)}, bf16[1120,1120]{1,0:T(8,128)(2,1)}, u32[]{:S(2)}) copy-start(bf16[1120,1120]{1,0:T(8,128)(2,1)} %param.20) | copy-start | bytes 7526404
  7.2 4.5 copy-start.29
  7.2 4.5 copy-start.36
  7.2 37.7 %all-gather.5.cloned.1.call-start = ((), (), s32[]{:S(2)}) async-start(), calls=%async_computation.7 | async-start | bytes 6881280 | tf_op jit(solution)/shard_map/all_gather | solution.py:95
  7.3 4.5 copy-start.5
  9.5 15.2 %copy-start.19 = (f32[512,2]{0,1:T(2,128)}, f32[512,2]{0,1:T(2,128)S(1)}, u32[]{:S(2)}) copy-start(f32[512,2]{0,1:T(2,128)S(1)} %broadcast_multiply_fusion.6) | copy-start | bytes 12292
  11.8 12.9 %copy-start.23 = (f32[512,2]{0,1:T(2,128)}, f32[512,2]{0,1:T(2,128)S(1)}, u32[]{:S(2)}) copy-start(f32[512,2]{0,1:T(2,128)S(1)} %add_rsqrt_fusion.1) | copy-start | bytes 12292
  27.8 90.4 %all-gather.3.cloned.1.call-start = ((), (), s32[]{:S(2)}) async-start(), calls=%async_computation.6 | async-start | bytes 6881280 | tf_op jit(solution)/shard_map/all_gather | solution.py:96
  28.6 541.6 %reduce-scatter.33.cloned.1.call-start = ((), (), s32[]{:S(2)}) async-start(), calls=%async_computation.13 | async-start | bytes 10967040
  118.2 34.9 %copy-start.15 = (f32[2,20,512]{2,1,0:T(8,128)}, f32[2,20,512]{2,1,0:T(8,128)S(1)}, u32[]{:S(2)}) copy-start(f32[2,20,512]{2,1,0:T(8,128)S(1)} %log_add_fusion) | copy-start | bytes 245764
  158.9 96.4 %copy-start.21 = (f32[512,2]{0,1:T(2,128)}, f32[512,2]{0,1:T(2,128)S(1)}, u32[]{:S(2)}) copy-start(f32[512,2]{0,1:T(2,128)S(1)} %broadcast_multiply_fusion.5) | copy-start | bytes 12292
  161.1 94.3 %copy-start.25 = (f32[512,2]{0,1:T(2,128)}, f32[512,2]{0,1:T(2,128)S(1)}, u32[]{:S(2)}) copy-start(f32[512,2]{0,1:T(2,128)S(1)} %add_rsqrt_fusion) | copy-start | bytes 12292
  161.1 19.7 %copy-start.12 = (bf16[512,2,1120]{0,2,1:T(8,128)(2,1)S(1)}, bf16[512,2,1120]{0,2,1:T(8,128)(2,1)}, u32[]{:S(2)}) copy-start(bf16[512,2,1120]{0,2,1:T(8,128)(2,1)} %param.25) | copy-start | bytes 6881284
  234.5 338.1 %reduce-scatter.23.cloned.1.call-start = ((), (), s32[]{:S(2)}) async-start(), calls=%async_computation.8 | async-start | bytes 27525120 | tf_op jit(solution)/shard_map/reduce_scatter | solution.py:182
  234.6 20.8 %copy-start.13 = (bf16[512,2,1120]{0,2,1:T(8,128)(2,1)S(1)}, bf16[512,2,1120]{0,2,1:T(8,128)(2,1)}, u32[]{:S(2)}) copy-start(bf16[512,2,1120]{0,2,1:T(8,128)(2,1)} %param.25) | copy-start | bytes 6881284
  259.0 4.4 copy-start.7
  259.0 4.4 copy-start.11
  350.3 36.2 %copy-start.3 = (bf16[512,2,20,56]{0,3,2,1:T(8,128)(2,1)S(1)}, bf16[512,2,20,56]{0,3,2,1:T(8,128)(2,1)}, u32[]{:S(2)}) copy-start(bf16[512,2,20,56]{0,3,2,1:T(8,128)(2,1)} %get-tuple-element.720) | copy-start | bytes 6881284
  443.1 661.0 %reduce-scatter.31.cloned.1.call-start = ((), (), s32[]{:S(2)}) async-start(), calls=%async_computation.12 | async-start | bytes 1290240
  546.2 4.5 copy-start.8
  546.2 5.0 copy-start.38
  546.3 9.6 slice-start
  546.3 9.6 slice-start.2
  551.3 4.6 slice-start.1
  551.3 4.6 copy-start.22
  551.3 4.6 copy-start.26
  551.3 4.6 copy-start.28
  551.3 4.6 copy-start.35
  551.3 4.6 slice-start.3
  551.3 5.0 slice-start.4
  572.5 6.7 copy-start.6
  572.5 6.7 copy-start.20
  572.5 6.7 copy-start.24
  572.6 6.7 copy-start.30
  572.6 6.7 copy-start.37
  572.6 641.0 %reduce-scatter.27.cloned.1.call-start = ((), (), s32[]{:S(2)}) async-start(), calls=%async_computation.10 | async-start | bytes 430080
  572.7 6.6 copy-start.14
  1070.7 45.3 %collective-permute-start.2 = (bf16[80,1120]{1,0:T(8,128)(2,1)S(1)}, bf16[80,1120]{1,0:T(8,128)(2,1)S(1)}, u32[]{:S(2)}, u32[]{:S(2)}) collective-permute-start(bf16[80,1120]{1,0:T(8,128)(2,1)S(1)} %get-tuple-element.478), channel_id=1, source_target_pairs={{0,1},{1,2},{2,3},{3,4},{4,5},{5,6},{6,7},{7,8},{8,9},{9,10},{10,1... | collective-permute-start | bytes 537608
  1074.3 48.3 %collective-permute-start = (bf16[80,3360]{1,0:T(8,128)(2,1)}, bf16[80,3360]{1,0:T(8,128)(2,1)}, u32[]{:S(2)}, u32[]{:S(2)}) collective-permute-start(bf16[80,3360]{1,0:T(8,128)(2,1)} %get-tuple-element.477), channel_id=1, source_target_pairs={{0,1},{1,2},{2,3},{3,4},{4,5},{5,6},{6,7},{7,8},{8,9},{9,10},{10,1... | collective-permute-start | bytes 1612808
  1077.7 36.1 %collective-permute-start.3 = (bf16[70,1120]{1,0:T(8,128)(2,1)}, bf16[70,1120]{1,0:T(8,128)(2,1)}, u32[]{:S(2)}, u32[]{:S(2)}) collective-permute-start(bf16[70,1120]{1,0:T(8,128)(2,1)} %slice.16), channel_id=1, source_target_pairs={{0,2},{1,3},{2,4},{3,5},{4,6},{5,7},{6,8},{7,9},{8,10},{9,11},{10,... | collective-permute-start | bytes 470408
  1081.9 40.7 %collective-permute-start.1 = (bf16[70,3360]{1,0:T(8,128)(2,1)}, bf16[70,3360]{1,0:T(8,128)(2,1)}, u32[]{:S(2)}, u32[]{:S(2)}) collective-permute-start(bf16[70,3360]{1,0:T(8,128)(2,1)} %slice.15), channel_id=1, source_target_pairs={{0,2},{1,3},{2,4},{3,5},{4,6},{5,7},{6,8},{7,9},{8,10},{9,11},{10,... | collective-permute-start | bytes 1411208
  1108.9 46.1 %collective-permute-start.4 = (bf16[80,4480]{1,0:T(8,128)(2,1)S(1)}, bf16[80,4480]{1,0:T(8,128)(2,1)}, u32[]{:S(2)}, u32[]{:S(2)}) collective-permute-start(bf16[80,4480]{1,0:T(8,128)(2,1)S(1)} %get-tuple-element.479), channel_id=1, source_target_pairs={{0,1},{1,2},{2,3},{3,4},{4,5},{5,6},{6,7},{7,8},{8,9},{9,10},{10,1... | collective-permute-start | bytes 2150408
  1113.9 41.0 %collective-permute-start.5 = (bf16[70,4480]{1,0:T(8,128)(2,1)}, bf16[70,4480]{1,0:T(8,128)(2,1)}, u32[]{:S(2)}, u32[]{:S(2)}) collective-permute-start(bf16[70,4480]{1,0:T(8,128)(2,1)} %slice.17), channel_id=1, source_target_pairs={{0,2},{1,3},{2,4},{3,5},{4,6},{5,7},{6,8},{7,9},{8,10},{9,11},{10,... | collective-permute-start | bytes 1881608
  1122.5 92.9 %reduce-scatter.25.cloned.1.call-start = ((), (), s32[]{:S(2)}) async-start(), calls=%async_computation.9 | async-start | bytes 1290240
  1138.6 78.9 %reduce-scatter.29.cloned.1.call-start = ((), (), s32[]{:S(2)}) async-start(), calls=%async_computation.11 | async-start | bytes 1720320
  1154.9 13.5 %copy-start.31 = (f32[1120]{0:T(1024)S(1)}, f32[1120]{0:T(1024)}, u32[]{:S(2)}) copy-start(f32[1120]{0:T(1024)} %get-tuple-element.424) | copy-start | bytes 13444
  1154.9 13.5 %copy-start.32 = (f32[1120]{0:T(1024)S(1)}, f32[1120]{0:T(1024)}, u32[]{:S(2)}) copy-start(f32[1120]{0:T(1024)} %get-tuple-element.430) | copy-start | bytes 13444
  1207.2 12.4 %copy-start.1 = (bf16[1120,1120]{1,0:T(8,128)(2,1)S(1)}, bf16[1120,1120]{1,0:T(8,128)(2,1)}, u32[]{:S(2)}) copy-start(bf16[1120,1120]{1,0:T(8,128)(2,1)} %param.20) | copy-start | bytes 7526404
  (12 other events, 30.8 us)
Sparse Core Ops, SparseCore 0:
  27.9 16.9 all-gather.4
  46.5 15.4 all-gather.2
  234.6 178.2 reduce-scatter.32
  443.2 29.3 reduce-scatter.22
  572.6 9.7 reduce-scatter.30
  1122.6 5.8 reduce-scatter.26
  1138.7 6.4 reduce-scatter.24
  1168.5 6.5 reduce-scatter.28
where the time goes:
time: 1230 us
  blocking collectives  517 us (42%)
  matrix products  501 us (41%)
  other arithmetic  82.3 us (7%)
  local copies, waits for them, and re-layouts  76.2 us (6%)
  starting transfers between devices  19.3 us (2%)
  between operations  16 us (1%)
  waiting for transfers between devices  15 us (1%)
    unnamed x1, blocking collectives  478 us
    dot_general x5, matrix products, key_scores(): jnp.einsum('qchd,kchd->chqk', query_heads, key_heads, preferred_element_t...  110 us
    unnamed x102, local copies, waits for them, and re-layouts  53.2 us
    dot_general x2, matrix products, query_step(): jnp.einsum('chqk,kchd->qchd', dscore, key_heads, preferred_element_type=j...  48.6 us
    dot_general x1, matrix products, per_device(): jnp.einsum('chqk,qchd->kchd', dscore, query_heads, preferred_element_type...  44 us
    dot_general x2, matrix products, attention_grads(): jnp.einsum('qchd,kchd->chqk', grad_heads, value_heads, preferred_element_...  42.7 us
    psum x1, blocking collectives, per_device(): lax.psum((attn_gain_grad, attn_bias_grad, mlp_gain_grad, mlp_bias_grad),...  38.9 us
    reduce_sum x1, other arithmetic, per_device(): run_sum = jnp.sum(weights, axis=-1)  37 us
  transfers between devices with their start and end apart: 14, of which 1 were waited for; matrix products, arithmetic and copies ran while one was open for 81% of the time, Pallas kernels for 0%

commit v1 on v0

--- a/solution.py
+++ b/solution.py
@@ -1,6 +1,10 @@
+import functools
+
 import jax
 import jax.numpy as jnp
 from jax import lax
+from jax.experimental import pallas as pl
+from jax.experimental.pallas import tpu as pltpu
 from jax.sharding import PartitionSpec as P
 
 D = 1120
@@ -10,6 +14,16 @@
 
 EPSILON = 1e-05
 MASKED = -1e30
+LOG2E = 1.4426950408889634
+LANES = 128
+WIDTH = 1152
+WINDOW = 256
+TILE = 256
+BF16 = jnp.bfloat16
+F32 = jnp.float32
+NN = (((1,), (0,)), ((), ()))
+NT = (((1,), (1,)), ((), ()))
+TN = (((0,), (0,)), ((), ()))
 
 
 def norm_forward(values_in, gain_vec, bias_vec):
@@ -55,7 +69,7 @@
     return lax.fori_loop(0, block_turns, one_turn, initial)
 
 
-def per_device(
+def position_split(
     tokens, lengths, attn_gain, attn_bias, w_qkv, w_out, mlp_gain, mlp_bias, w_up, w_down, cotangent
 ):
     row_count = tokens.shape[0]
@@ -243,6 +257,440 @@
     )
 
 
+def dot(left, right, dims=NN):
+    return lax.dot_general(left, right, dims, preferred_element_type=F32)
+
+
+def head_lanes(head, width):
+    start = jnp.minimum(head * HD // LANES, (width - WINDOW) // LANES) * LANES
+    start = pl.multiple_of(start, LANES)
+    lane = lax.broadcasted_iota(jnp.int32, (1, WINDOW), 1)
+    offset = lane + (start - head * HD)
+    own = (offset >= 0) & (offset < HD)
+    spare = lane == jnp.where(start == head * HD, WINDOW - 1, 0)
+    return start, own, spare
+
+
+def key_bias(len_ref, seq):
+    rows = lax.broadcasted_iota(jnp.int32, (seq, 1), 0)
+    return jnp.where(rows < len_ref[0], 0.0, MASKED).astype(BF16)
+
+
+def masked_query(q_ref, win, own, spare):
+    return jnp.where(own, q_ref[:, win], jnp.where(spare, 1.0, 0.0).astype(BF16))
+
+
+def causal_tile():
+    key_row = lax.broadcasted_iota(jnp.int32, (TILE, TILE), 0)
+    query_lane = lax.broadcasted_iota(jnp.int32, (TILE, TILE), 1)
+    return key_row <= query_lane
+
+
+def staggered(jobs, begin, middle, end):
+    started = begin(jobs[0])
+    waiting = None
+    for index, job in enumerate(jobs):
+        current = started
+        if index + 1 < len(jobs):
+            started = begin(jobs[index + 1])
+        result = middle(job, *current)
+        if waiting is not None:
+            end(*waiting)
+        waiting = (job, *result)
+    end(*waiting)
+
+
+def attention_forward_kernel(per, len_ref, q_ref, k_ref, v_ref, o_ref, lse_ref):
+    step = pl.program_id(0)
+    seq, width = q_ref.shape
+
+    @pl.when(step == 0)
+    def _():
+        o_ref[...] = jnp.zeros_like(o_ref)
+
+    bias = key_bias(len_ref, seq)
+    keep = causal_tile()
+    scale = LOG2E * HD ** (-0.5)
+    jobs = []
+    for slot in range(per):
+        start, own, spare = head_lanes(step * per + slot, width)
+        win = pl.ds(start, WINDOW)
+        k_win = jnp.where(spare, bias, k_ref[:, win])
+        q_win = masked_query(q_ref, win, own, spare)
+        v_turned = jnp.transpose(v_ref[:, win])
+        for turn in range(seq // TILE):
+            jobs.append((slot, turn * TILE, win, own, k_win, q_win, v_turned))
+
+    def begin(job):
+        _, low, _, _, k_win, q_win, _ = job
+        return (dot(k_win[: low + TILE], q_win[low : low + TILE], NT),)
+
+    def middle(job, scores):
+        slot, low = job[:2]
+        edge = jnp.where(keep, scores[low:], MASKED)
+        scores = edge if low == 0 else jnp.concatenate([scores[:low], edge], axis=0)
+        peak = jnp.max(scores, axis=0, keepdims=True) * scale
+        weights = jnp.exp2(scores * scale - peak)
+        total = jnp.sum(weights, axis=0, keepdims=True)
+        lse_ref[slot, :, low : low + TILE] = jnp.broadcast_to(peak + jnp.log2(total), (8, TILE))
+        return weights.astype(BF16), total
+
+    def end(job, weights, total):
+        _, low, win, own, _, _, v_turned = job
+        out = dot(v_turned[:, : low + TILE], weights) * (1.0 / total)
+        rows = slice(low, low + TILE)
+        o_ref[rows, win] = jnp.where(own, jnp.transpose(out).astype(BF16), o_ref[rows, win])
+
+    staggered(jobs, begin, middle, end)
+
+
+def attention_backward_kernel(
+    per, len_ref, q_ref, k_ref, v_ref, o_ref, do_ref, lse_ref, grad_ref, delta_ref, acc_ref
+):
+    step = pl.program_id(0)
+    seq, width = q_ref.shape
+
+    @pl.when(step == 0)
+    def _():
+        grad_ref[...] = jnp.zeros_like(grad_ref)
+        lane = lax.broadcasted_iota(jnp.int32, (delta_ref.shape[0], width), 1)
+        first = lax.broadcasted_iota(jnp.int32, (delta_ref.shape[0], width), 0) * HD
+        pick = jnp.where((lane >= first) & (lane < first + HD), 1.0, 0.0).astype(BF16)
+        for turn in range(seq // TILE):
+            rows = slice(turn * TILE, (turn + 1) * TILE)
+            product = o_ref[rows].astype(F32) * do_ref[rows].astype(F32)
+            upper = product.astype(BF16)
+            lower = (product - upper.astype(F32)).astype(BF16)
+            delta_ref[:, rows] = dot(pick, upper, NT) + dot(pick, lower, NT)
+
+    bias = key_bias(len_ref, seq)
+    keep = causal_tile()
+    scale = LOG2E * HD ** (-0.5)
+    turns = seq // TILE
+    jobs = []
+    for slot in range(per):
+        head = step * per + slot
+        start, own, spare = head_lanes(head, width)
+        win = pl.ds(start, WINDOW)
+        k_win = jnp.where(spare, bias, k_ref[:, win])
+        q_win = masked_query(q_ref, win, own, spare)
+        do_win = jnp.where(own, do_ref[:, win], jnp.zeros((), BF16))
+        v_win = v_ref[:, win]
+        lse = lse_ref[slot, 0:1, :]
+        delta = delta_ref[pl.ds(head, 1), :]
+        for turn in range(turns):
+            jobs.append((slot, turn, start, own, k_win, q_win, do_win, v_win, lse, delta))
+
+    def begin(job):
+        _, turn, _, _, k_win, q_win, do_win, v_win, _, _ = job
+        low = turn * TILE
+        rows = slice(low, low + TILE)
+        return dot(k_win[rows], q_win[low:], NT), dot(v_win[rows], do_win[low:], NT)
+
+    def middle(job, scores, dprobs):
+        turn, lse, delta = job[1], job[8], job[9]
+        low = turn * TILE
+        probs = jnp.exp2(scores * scale - lse[:, low:])
+        edge = jnp.where(keep, probs[:, :TILE], 0.0)
+        if turn + 1 < turns:
+            edge = jnp.concatenate([edge, probs[:, TILE:]], axis=1)
+        dscores = (edge * (dprobs - delta[:, low:])).astype(BF16)
+        return edge.astype(BF16), dscores
+
+    def end(job, probs, dscores):
+        slot, turn, start, own, k_win, q_win, do_win = job[:7]
+        low = turn * TILE
+        rows = slice(low, low + TILE)
+
+        def put(place, where, value):
+            lanes = pl.ds(start + place * width, WINDOW)
+            grad_ref[where, lanes] = jnp.where(own, value.astype(BF16), grad_ref[where, lanes])
+
+        put(2, rows, dot(probs, do_win[low:]))
+        put(1, rows, dot(dscores, q_win[low:]) * HD ** (-0.5))
+        part = dot(dscores, k_win[rows], TN)
+        if turn == 0:
+            acc_ref[slot] = part
+        else:
+            acc_ref[slot, low:, :] += part
+        if turn + 1 == turns:
+            put(0, slice(0, seq), acc_ref[slot] * HD ** (-0.5))
+
+    staggered(jobs, begin, middle, end)
+
+
+def resident(shape, place=0):
+    return pl.BlockSpec(shape, lambda step, *_: (0, place), pipeline_mode=pl.Buffered(1))
+
+
+def attention_forward(qkv, length, per=2):
+    seq, width = qkv.shape[0], qkv.shape[1] // 3
+    return pl.pallas_call(
+        functools.partial(attention_forward_kernel, per),
+        grid_spec=pltpu.PrefetchScalarGridSpec(
+            num_scalar_prefetch=1,
+            grid=(HEADS // per,),
+            in_specs=[resident((seq, width), place) for place in range(3)],
+            out_specs=[
+                resident((seq, width)),
+                pl.BlockSpec((per, 8, seq), lambda step, *_: (step, 0, 0)),
+            ],
+        ),
+        out_shape=[
+            jax.ShapeDtypeStruct((seq, width), BF16),
+            jax.ShapeDtypeStruct((HEADS, 8, seq), F32),
+        ],
+        compiler_params=pltpu.CompilerParams(vmem_limit_bytes=56 << 20),
+        cost_estimate=pl.CostEstimate(
+            flops=2 * 2 * HEADS * seq * seq * WINDOW * 5 // 8,
+            bytes_accessed=8 * seq * width,
+            transcendentals=HEADS * seq * seq * 5 // 8,
+        ),
+        name="attention_forward",
+    )(length, qkv, qkv, qkv)
+
+
+def attention_backward(qkv, attended, grad_attended, lse, length, per=2):
+    seq, width = qkv.shape[0], qkv.shape[1] // 3
+    return pl.pallas_call(
+        functools.partial(attention_backward_kernel, per),
+        grid_spec=pltpu.PrefetchScalarGridSpec(
+            num_scalar_prefetch=1,
+            grid=(HEADS // per,),
+            in_specs=[resident((seq, width), place) for place in (0, 1, 2, 0, 0)]
+            + [pl.BlockSpec((per, 8, seq), lambda step, *_: (step, 0, 0))],
+            out_specs=resident((seq, 3 * width)),
+            scratch_shapes=[
+                pltpu.VMEM((-(-HEADS // 16) * 16, seq), F32),
+                pltpu.VMEM((per, seq, WINDOW), F32),
+            ],
+        ),
+        out_shape=jax.ShapeDtypeStruct((seq, 3 * width), BF16),
+        compiler_params=pltpu.CompilerParams(vmem_limit_bytes=58 << 20),
+        cost_estimate=pl.CostEstimate(
+            flops=5 * 2 * HEADS * seq * seq * WINDOW * 5 // 8,
+            bytes_accessed=16 * seq * width,
+            transcendentals=HEADS * seq * seq * 5 // 8,
+        ),
+        name="attention_backward",
+    )(length, qkv, qkv, qkv, attended, grad_attended, lse)
+
+
+def swap_cores(value):
+    return lax.ppermute(value, "blk", [(0, 1), (1, 0)])
+
+
+def swap_chips(value, bit):
+    count = lax.axis_size("cells")
+    return lax.ppermute(value, "cells", [(place, place ^ bit) for place in range(count)])
+
+
+def scatter_part(grads, axes):
+    place = lax.axis_index("cells")
+    count = grads.ndim - 2
+    kept = grads
+    got = None
+    for axis in axes:
+        bit = 1 << (count - 1 - axis)
+        side = (place // bit) % 2
+
+        def half(value, which):
+            return lax.dynamic_index_in_dim(value, which, axis, keepdims=True)
+
+        def both(which):
+            if got is None:
+                return half(kept, which)
+            return (half(kept, which).astype(F32) + half(got, which).astype(F32)).astype(BF16)
+
+        sent, stays = both(1 - side), both(side)
+        got = swap_chips(sent, bit)
+        kept = stays
+    total = kept.astype(F32) + got.astype(F32)
+    return total.reshape(total.shape[-2:])
+
+
+def chip_sum(features, theirs, ours):
+    sent = dot(features, theirs).astype(BF16)
+    return (dot(features, ours) + swap_cores(sent).astype(F32)).astype(BF16)
+
+
+def scatter(grads, rows, cuts):
+    count = lax.axis_size("cells")
+    bits = count.bit_length() - 1
+    shaped = grads.reshape((2,) * bits + (rows, grads.shape[1]))
+    first = [bits - 1 - turn for turn in range(bits)]
+    orders = [first, [first[1], first[0]] + first[2:], first[2:] + first[:2]]
+    begin = 0
+    parts = []
+    for size, order in zip(cuts, orders):
+        piece = lax.slice_in_dim(shaped, begin, begin + size, axis=bits + 1)
+        parts.append(scatter_part(piece, order))
+        begin += size
+    return jnp.concatenate(parts, axis=-1) if len(parts) > 1 else parts[0]
+
+
+def columns(value, first, size):
+    return lax.dynamic_slice_in_dim(value, first, size, axis=1)
+
+
+def cell_split(
+    tokens, lengths, attn_gain, attn_bias, w_qkv, w_out, mlp_gain, mlp_bias, w_up, w_down, cotangent
+):
+    row_count = tokens.shape[0]
+    seq = 2 * row_count
+    core = lax.axis_index("blk")
+    chips = lax.axis_size("cells")
+
+    def to_cell(value):
+        mine = jnp.where(core == 0, value[:, 0], value[:, 1])
+        other = swap_cores(jnp.where(core == 0, value[:, 1], value[:, 0]))
+        return jnp.concatenate(
+            [jnp.where(core == 0, mine, other), jnp.where(core == 0, other, mine)], axis=0
+        )
+
+    def to_rows(value):
+        first, second = value[:row_count], value[row_count:]
+        mine = jnp.where(core == 0, first, second)
+        other = swap_cores(jnp.where(core == 0, second, first))
+        return jnp.stack(
+            [jnp.where(core == 0, mine, other), jnp.where(core == 0, other, mine)], axis=1
+        )
+
+    length = jnp.where(core == 0, lengths[0], lengths[1])
+    inputs = to_cell(tokens).astype(F32)
+    cell_cotangent = to_cell(cotangent)
+    w_wide = jnp.pad(w_qkv.reshape(D, 3, D), ((0, 0), (0, 0), (0, WIDTH - D))).reshape(D, 3 * WIDTH)
+    w_out_tall = jnp.pad(w_out, ((0, WIDTH - D), (0, 0)))
+
+    def norm_grads(grad_in, normed, inverse, gain_vec):
+        scaled = grad_in * gain_vec
+        grad_out = inverse * (
+            scaled
+            - jnp.mean(scaled, axis=-1, keepdims=True)
+            - normed * jnp.mean(scaled * normed, axis=-1, keepdims=True)
+        )
+        return grad_out, jnp.sum(grad_in * normed, axis=0), jnp.sum(grad_in, axis=0)
+
+    normed_one, inverse_one, pre_one = norm_forward(inputs, attn_gain, attn_bias)
+    normed_low = pre_one.astype(BF16)
+    qkv = dot(normed_low, w_wide).astype(BF16)
+    attended, lse = attention_forward(qkv, length.reshape(1))
+    hidden = inputs + dot(attended, w_out_tall)
+    normed_two, inverse_two, pre_two = norm_forward(hidden, mlp_gain, mlp_bias)
+    normed_mlp = pre_two.astype(BF16)
+    upward = dot(normed_mlp, w_up)
+    activated_full, gelu_back = jax.vjp(
+        lambda value_in: jax.nn.gelu(value_in, approximate=True), upward
+    )
+    activated = activated_full.astype(BF16)
+    mixed = (hidden + dot(activated, w_down)).astype(BF16)
+    valid = jnp.arange(seq, dtype=jnp.int32)[:, None] < length
+    grad_low = jnp.where(valid, cell_cotangent, jnp.zeros((), BF16))
+    grad_out = grad_low.astype(F32)
+
+    rows_pad = -(-(D // chips) // 8) * 8
+    place = jnp.arange(chips * rows_pad, dtype=jnp.int32)
+    source = jnp.where(place % rows_pad < D // chips, place // rows_pad * (D // chips) + place % rows_pad, -1)
+    spread = (source[:, None] == jnp.arange(D, dtype=jnp.int32)[None, :]).astype(BF16)
+
+    def spread_rows(value):
+        return dot(spread, value, NT).astype(BF16)
+
+    half = D // 2
+    down_sent = lax.dot_general(activated, columns(grad_low, (1 - core) * half, half), TN, preferred_element_type=F32)
+    down_kept = lax.dot_general(activated, columns(grad_low, core * half, half), TN, preferred_element_type=F32)
+    down_sum = (down_kept + swap_cores(down_sent.astype(BF16)).astype(F32)).astype(BF16)
+    w_down_share = scatter(down_sum, w_down.shape[0] // chips, (256, 256, half - 512))
+
+    grad_act = dot(grad_low, w_down, NT)
+    grad_upward = gelu_back(grad_act)[0].astype(BF16)
+    up_all = w_up.shape[1]
+    up_window = -(-up_all // 2 // LANES) * LANES
+    up_starts = (0, up_all - up_window)
+    up_start = jnp.where(core == 0, up_starts[0], up_starts[1])
+    up_other = jnp.where(core == 0, up_starts[1], up_starts[0])
+    up_sum = chip_sum(
+        spread_rows(normed_mlp),
+        columns(grad_upward, up_other, up_window),
+        columns(grad_upward, up_start, up_window),
+    )
+    up_share = scatter(up_sum, rows_pad, (896, 896, up_window - 1792))
+
+    grad_normed_two = dot(grad_upward, w_up, NT)
+    grad_hidden_ln, mlp_gain_grad, mlp_bias_grad = norm_grads(
+        grad_normed_two, normed_two, inverse_two, mlp_gain
+    )
+    grad_hidden = grad_out + grad_hidden_ln
+    grad_branch = grad_hidden.astype(BF16)
+    out_sum = chip_sum(
+        spread_rows(attended[:, :D]),
+        columns(grad_branch, (1 - core) * half, half),
+        columns(grad_branch, core * half, half),
+    )
+    w_out_share = scatter(out_sum, rows_pad, (half,))
+
+    grad_attended = dot(grad_branch, w_out_tall, NT).astype(BF16)
+    grad_qkv = attention_backward(qkv, attended, grad_attended, lse, length.reshape(1))
+    qkv_window = 14 * LANES
+    qkv_starts = (0, 3 * WIDTH - qkv_window)
+    qkv_start = jnp.where(core == 0, qkv_starts[0], qkv_starts[1])
+    qkv_other = jnp.where(core == 0, qkv_starts[1], qkv_starts[0])
+    qkv_sum = chip_sum(
+        spread_rows(normed_low),
+        columns(grad_qkv, qkv_other, qkv_window),
+        columns(grad_qkv, qkv_start, qkv_window),
+    )
+    qkv_share = scatter(qkv_sum, rows_pad, (640, 640, qkv_window - 1280))
+
+    grad_normed_one = dot(grad_qkv, w_wide, NT)
+    grad_inputs_ln, attn_gain_grad, attn_bias_grad = norm_grads(
+        grad_normed_one, normed_one, inverse_one, attn_gain
+    )
+    tokens_grad = (grad_hidden + grad_inputs_ln).astype(BF16)
+    norm_sums = lax.psum(
+        (attn_gain_grad, attn_bias_grad, mlp_gain_grad, mlp_bias_grad), ("blk", "cells")
+    )
+
+    rows = D // chips
+    first_share = jnp.concatenate(
+        [qkv_share[:rows, :D], qkv_share[:rows, WIDTH : WIDTH + half]], axis=1
+    )
+    shift = WIDTH + half - qkv_starts[1]
+    second_share = jnp.concatenate(
+        [
+            qkv_share[:rows, shift : shift + half],
+            qkv_share[:rows, 2 * WIDTH - qkv_starts[1] : 2 * WIDTH - qkv_starts[1] + D],
+        ],
+        axis=1,
+    )
+    w_qkv_share = jnp.where(core == 0, first_share, second_share)
+    up_shift = up_all // 2 - up_starts[1]
+    w_up_share = jnp.where(
+        core == 0,
+        up_share[:rows, : up_all // 2],
+        up_share[:rows, up_shift : up_shift + up_all // 2],
+    )
+    return (
+        to_rows(mixed),
+        to_rows(tokens_grad),
+        norm_sums[0],
+        norm_sums[1],
+        w_qkv_share,
+        w_out_share[:rows],
+        norm_sums[2],
+        norm_sums[3],
+        w_up_share,
+        w_down_share,
+    )
+
+
+def per_device(mesh, tokens, *rest):
+    chips = mesh.shape["cells"]
+    if mesh.shape["blk"] == 2 and tokens.shape[1] == 2 and chips & (chips - 1) == 0 and chips >= 8:
+        return cell_split(tokens, *rest)
+    return position_split(tokens, *rest)
+
+
 def solution(mesh):
     placed = (
         P("blk", "cells", None),
@@ -258,7 +706,7 @@
         P("blk", "cells", None),
     )
     return jax.shard_map(
-        per_device,
+        functools.partial(per_device, mesh),
         mesh=mesh,
         in_specs=placed,
         out_specs=(

time: 1230 us -> 600 us (0.49)
  blocking collectives: 517 us -> 44.8 us
  matrix products: 501 us -> 203 us
  waiting for transfers between devices: 15 us -> 118 us
  Pallas kernels: 0 us -> 81.6 us
  other arithmetic: 82.3 us -> 41.7 us
  starting transfers between devices: 19.3 us -> 48.8 us
  local copies, waits for them, and re-layouts: 76.2 us -> 50.6 us
  between operations: 16 us -> 3.07 us
    unnamed x1 -> x0, blocking collectives: 478 us -> none
    dot_general x24 -> x19, matrix products: 501 us -> 203 us  [the longest x17 187 us: dot(): return lax.dot_general(left, right, dims, preferred_element_type=F32)]
    ppermute x0 -> x48, waiting for transfers between devices: none -> 118 us  [the longest x40 118 us: swap_chips(): lax.ppermute(value, 'cells', [(place, place ^ bit) for place in range(cou...]
    pallas_call x0 -> x2, Pallas kernels: none -> 81.6 us  [the longest x1 50.5 us: attention_backward(): pl.pallas_call(functools.partial(attention_backward_kernel, per), grid_sp...]
    ppermute x0 -> x48, starting transfers between devices: none -> 48.8 us  [the longest x40 46.3 us: swap_chips(): lax.ppermute(value, 'cells', [(place, place ^ bit) for place in range(cou...]
    reduce_sum x1 -> x0, other arithmetic: 37 us -> none  [per_device(): run_sum = jnp.sum(weights, axis=-1)]
    unnamed x102 -> x93, local copies, waits for them, and re-layouts: 53.2 us -> 19.6 us
    unnamed x11 -> x0, starting transfers between devices: 19.1 us -> none
  transfers between devices with their start and end apart: 14 -> 48, of which waited for: 1 -> 20; matrix products, arithmetic and copies ran while one was open for 81% -> 38% of each run, Pallas kernels for 0% -> 14%
where the time goes in v1:
time: 600 us; the launch traced here: 593 us
  matrix products  203 us (34%)
  waiting for transfers between devices  118 us (20%)
  Pallas kernels  81.6 us (14%)
  local copies, waits for them, and re-layouts  50.6 us (8%)
  starting transfers between devices  48.8 us (8%)
  blocking collectives  44.8 us (7%)
  other arithmetic  41.7 us (7%)
    dot_general x17, matrix products, dot(): return lax.dot_general(left, right, dims, preferred_element_type=F32)  187 us
    ppermute x40, waiting for transfers between devices, swap_chips(): lax.ppermute(value, 'cells', [(place, place ^ bit) for place in range(cou...  118 us
    pallas_call x1, Pallas kernels, attention_backward(): pl.pallas_call(functools.partial(attention_backward_kernel, per), grid_sp...  50.5 us
    ppermute x40, starting transfers between devices, swap_chips(): lax.ppermute(value, 'cells', [(place, place ^ bit) for place in range(cou...  46.3 us
    psum x1, blocking collectives, cell_split(): lax.psum((attn_gain_grad, attn_bias_grad, mlp_gain_grad, mlp_bias_grad),...  44.8 us
    pallas_call x1, Pallas kernels, attention_forward(): pl.pallas_call(functools.partial(attention_forward_kernel, per), grid_spe...  31.1 us
    unnamed x93, local copies, waits for them, and re-layouts  19.6 us
  transfers between devices with their start and end apart: 48, of which 20 were waited for; matrix products, arithmetic and copies ran while one was open for 38% of the time, Pallas kernels for 14%

profile of v1, /device:TPU:0, one launch (start us, length us, event | category | flops | bytes accessed | tf_op | source)
XLA Modules:
  0.0 592.6 jit_solution(11390715573716542348)
XLA Ops:
  4.6 11.3 %copy.30 = bf16[1120,3360]{0,1:T(8,128)(2,1)} copy(bf16[1120,3360]{1,0:T(8,128)(2,1)} %param.15) | data formatting | bytes 15052800 | tf_op args[4]
  15.9 6.9 %pad.8 = bf16[1120,3,1152]{0,2,1:T(8,128)(2,1)} pad(bf16[1120,3,1120]{0,2,1:T(8,128)(2,1)} %bitcast.67, bf16[]{:T(256)} %constant.1150.clone.1), padding=0_0x0_0x0_32 | pad | bytes 15267842 | tf_op jit(solution)/shard_map/jit(_pad)/pad | solution.py:562
  29.8 13.8 %convolution_convert_fusion.3.q_ref.k_ref.v_ref = bf16[1024,3456]{1,0:T(8,128)(2,1)} fusion(bf16[1120,3456]{0,1:T(8,128)(2,1)S(1)} %bitcast.71, f32[1120]{0:T(1024)S(1)} %copy-done.31, f32[1120]{0:T(1024)S(1)} %copy-done.27, f32[1024]{0:T(1024)S(1)} %add_rsqrt_fusion.1, f32[1024]{0:T(1024)S(1)} %broadcast_multiply_fusion.5, ...), kind=kOutput, calls=%fused_computation.16 | convolution fusion | flops 7941095424 | bytes 17130240 | tf_op jit(solution)/shard_map/dot_general | solution.py:261
  43.7 31.1 %attention_forward.1 = (bf16[1024,1152]{1,0:T(8,128)(2,1)}, f32[20,8,1024]{2,1,0:T(8,128)}) custom-call(s32[1]{0:T(128)} %bitcast.4.len_ref, bf16[1024,3456]{1,0:T(8,128)(2,1)} %convolution_convert_fusion.3.q_ref.k_ref.v_ref, bf16[1024,3456]{1,0:T(8,128)(2,1)} %convolution_convert_fusion.3.q_ref.k_ref.v_ref, ...), custom_call_target="tpu_custom_call" | custom-call | flops 13421772800 | bytes 9437184 | tf_op jit(solution)/shard_map/attention_forward/pallas_call | solution.py:428
  74.8 5.7 fusion.88
  81.1 4.9 fusion.31
  86.0 19.6 %fusion.83 = f32[1024,4480]{1,0:T(8,128)} fusion(bf16[1120,4480]{1,0:T(8,128)(2,1)} %param.19, f32[1024,1120]{0,1:T(8,128)S(1)} %get-tuple-element.87, f32[1120]{0:T(1024)S(1)} %copy-done.32, f32[1120]{0:T(1024)S(1)} %copy-done.24, f32[1024]{0:T(1024)S(1)} %add_rsqrt_fusion, f32[1024]{0:T(1024)S(1)} %broadcast_multiply_fusion.4), kind=kOutput, calls=%fused_computation.222 | convolution fusion | flops 10281779200 | bytes 32989952 | tf_op jit(solution)/shard_map/dot_general | solution.py:261
  105.6 5.0 fusion.32
  110.6 4.9 fusion.33
  117.6 33.1 %fusion.6 = (bf16[1024,4480]{1,0:T(8,128)(2,1)}, bf16[1024,4480]{1,0:T(8,128)(2,1)}) fusion(f32[1024,4480]{1,0:T(8,128)} %fusion.83, bf16[1024,1120]{0,1:T(8,128)(2,1)S(1)} %maximum_select_fusion, bf16[4480,1120]{0,1:T(8,128)(2,1)} %param.20), kind=kOutput, calls=%fused_computation.8 | convolution fusion | flops 10376970240 | bytes 49029120 | tf_op jit(solution)/shard_map/dot_general | solution.py:261
  150.7 17.8 %fusion.30 = bf16[1024,1120]{0,1:T(8,128)(2,1)} fusion(f32[1024,1120]{0,1:T(8,128)S(1)} %get-tuple-element.87, bf16[1024,4480]{1,0:T(8,128)(2,1)} %get-tuple-element.27, bf16[4480,1120]{0,1:T(8,128)(2,1)} %param.20), kind=kOutput, calls=%fused_computation.51 | convolution fusion | flops 10278338560 | bytes 26091520 | tf_op jit(solution)/shard_map/dot_general | solution.py:261
  168.5 7.3 %convolution_convert_fusion.1 = bf16[4480,560]{0,1:T(8,128)(2,1)} fusion(bf16[1024,4480]{1,0:T(8,128)(2,1)S(1)} %copy-done.35, bf16[1024,1120]{0,1:T(8,128)(2,1)S(1)} %maximum_select_fusion, s32[]{:T(128)S(6)} %select_n.563), kind=kOutput, calls=%fused_computation.14 | convolution fusion | flops 5140531200 | bytes 15339524 | tf_op jit(solution)/shard_map/dot_general | solution.py:600
  175.9 18.5 %multiply_reduce_fusion = (f32[1120]{0:T(1024)S(1)}, f32[1024]{0:T(1024)S(1)}, f32[1024]{0:T(1024)S(1)}, f32[1120]{0:T(1024)S(1)}, f32[1024,1120]{0,1:T(8,128)S(1)}) fusion(f32[1024,1120]{0,1:T(8,128)S(1)} %get-tuple-element.87, f32[1024]{0:T(1024)S(1)} %add_rsqrt_fusion, f32[1024]{0:T(1024)S(1)} %broadcast_multiply_fusion.4, f32[1120]{0:T(1024)S(1)} %copy-done.24, ...), kind=kOutput, calls=%fused_computation.43 | convolution fusion | flops 10286362624 | bytes 28415104 | tf_op jit(solution)/shard_map/dot_general | solution.py:261
  197.9 5.0 convolution_convert_fusion.4.do_ref
  202.9 2.8 convolution_convert_fusion.5
  206.1 50.5 %attention_backward.1 = bf16[1024,3456]{1,0:T(8,128)(2,1)} custom-call(s32[1]{0:T(128)} %bitcast.4.len_ref, bf16[1024,3456]{1,0:T(8,128)(2,1)} %convolution_convert_fusion.3.q_ref.k_ref.v_ref, bf16[1024,3456]{1,0:T(8,128)(2,1)} %convolution_convert_fusion.3.q_ref.k_ref.v_ref, bf16[1024,3456]{1,0:T(8,128)(2,1)} %convolution_convert_fusion.3.q_ref.k_ref.v_ref, ...), custom_call_target="tpu_custom_call" | custom-call | flops 33554432000 | bytes 18874368 | tf_op jit(solution)/shard_map/attention_backward/pallas_call | solution.py:455
  256.6 17.0 %fusion.28 = (f32[1120]{0:T(1024)S(1)}, f32[1024]{0:T(1024)S(1)}, f32[1024]{0:T(1024)S(1)}, f32[1120]{0:T(1024)S(1)}, f32[1024,1120]{0,1:T(8,128)}) fusion(f32[1024]{0:T(1024)S(1)} %copy-done.26, f32[1024]{0:T(1024)S(1)} %copy-done.23, bf16[512,1120]{0,1:T(8,128)(2,1)} %copy-done.7, bf16[512,1120]{0,1:T(8,128)(2,1)S(1)} %copy-done.6, ...), kind=kOutput, calls=%fused_computation.41 | convolution fusion | flops 7942139904 | bytes 21730432 | tf_op jit(solution)/shard_map/dot_general | solution.py:261
  273.7 9.3 %convolution_convert_fusion.2 = bf16[1152,1792]{1,0:T(8,128)(2,1)} fusion(bf16[1152,1024]{1,0:T(8,128)(2,1)} %fusion.31, bf16[1024,3456]{1,0:T(8,128)(2,1)} %attention_backward.1, s32[]{:T(128)S(6)} %select_n.538), kind=kOutput, calls=%fused_computation.15 | convolution fusion | flops 4229922816 | bytes 10158084 | tf_op jit(solution)/shard_map/dot_general | solution.py:261
  283.1 3.7 fusion.27
  287.4 9.3 %convolution_convert_fusion = bf16[1152,2304]{1,0:T(8,128)(2,1)} fusion(bf16[1152,1024]{1,0:T(8,128)(2,1)} %fusion.33, bf16[1024,4480]{1,0:T(8,128)(2,1)S(1)} %bitcast.81, s32[]{:T(128)S(6)} %select_n.566), kind=kOutput, calls=%fused_computation.10 | convolution fusion | flops 5438472192 | bytes 12386308 | tf_op jit(solution)/shard_map/dot_general | solution.py:261
  297.3 44.8 %all-reduce.2 = (f32[1120]{0:T(1024)}, f32[1120]{0:T(1024)}, f32[1120]{0:T(1024)}, f32[1120]{0:T(1024)}) all-reduce(f32[1120]{0:T(1024)S(1)} %get-tuple-element.16, f32[1120]{0:T(1024)S(1)} %get-tuple-element.21, f32[1120]{0:T(1024)S(1)} %get-tuple-element.14, ...), channel_id=1, replica_groups=mesh['blk'=2,'cells'=16] {'blk','cells'}, use_global_device_ids=true, to_apply=%region_9.10 | all-reduce | flops 4480 | bytes 35840 | tf_op jit(solution)/shard_map/psum | solution.py:650
  342.1 2.9 broadcast_select_fusion.4
  347.5 4.1 add_convert_fusion.4
  351.6 2.7 copy.31
  359.5 15.7 %collective-permute-done.18 = bf16[2,2,2,1,72,560]{5,4,3,2,1,0:T(8,128)(2,1)S(1)} collective-permute-done((bf16[2,2,2,1,72,560]{5,4,3,2,1,0:T(8,128)(2,1)S(1)}, bf16[2,2,2,1,72,560]{5,4,3,2,1,0:T(8,128)(2,1)S(1)}, u32[]{:S(2)}, u32[]{:S(2)}) %collective-permute-start.18) | collective-permute-done | bytes 645152 | tf_op jit(solution)/shard_map/ppermute | solution.py:485
  378.7 7.1 %collective-permute-done.19 = bf16[2,2,1,1,72,560]{5,4,3,2,1,0:T(8,128)(2,1)S(1)} collective-permute-done((bf16[2,2,1,1,72,560]{5,4,3,2,1,0:T(8,128)(2,1)S(1)}, bf16[2,2,1,1,72,560]{5,4,3,2,1,0:T(8,128)(2,1)S(1)}, u32[]{:S(2)}, u32[]{:S(2)}) %collective-permute-start.19) | collective-permute-done | bytes 322592 | tf_op jit(solution)/shard_map/ppermute | solution.py:485
  386.4 7.5 %add_convert_fusion.2 = bf16[1152,1792]{1,0:T(8,128)(2,1)S(1)} fusion(bf16[1152,1792]{1,0:T(8,128)(2,1)} %collective-permute-done.4, bf16[1152,1024]{1,0:T(8,128)(2,1)S(1)} %copy-done.38, bf16[1024,3456]{1,0:T(8,128)(2,1)} %attention_backward.1, s32[]{:T(128)S(6)} %select_n.537), kind=kOutput, calls=%fused_computation.13 | convolution fusion | flops 4234051584 | bytes 14286852 | tf_op jit(solution)/shard_map/dot_general | solution.py:261
  400.0 8.2 %collective-permute-done.13 = bf16[2,1,2,2,72,512]{5,4,3,2,1,0:T(8,128)(2,1)S(1)} collective-permute-done((bf16[2,1,2,2,72,512]{5,4,3,2,1,0:T(8,128)(2,1)S(1)}, bf16[2,1,2,2,72,512]{5,4,3,2,1,0:T(8,128)(2,1)S(1)}, u32[]{:S(2)}, u32[]{:S(2)}) %collective-permute-start.13) | collective-permute-done | bytes 589856 | tf_op jit(solution)/shard_map/ppermute | solution.py:485
  410.0 3.6 collective-permute-done.21
  420.1 7.2 %collective-permute-done.14 = bf16[1,1,2,2,72,512]{5,4,3,2,1,0:T(8,128)(2,1)S(1)} collective-permute-done((bf16[1,1,2,2,72,512]{5,4,3,2,1,0:T(8,128)(2,1)S(1)}, bf16[1,1,2,2,72,512]{5,4,3,2,1,0:T(8,128)(2,1)S(1)}, u32[]{:S(2)}, u32[]{:S(2)}) %collective-permute-start.14) | collective-permute-done | bytes 294944 | tf_op jit(solution)/shard_map/ppermute | solution.py:485
  429.4 8.9 %add_convert_fusion.1 = bf16[4480,560]{0,1:T(8,128)(2,1)} fusion(bf16[4480,560]{0,1:T(8,128)(2,1)} %collective-permute-done.35, bf16[1024,4480]{1,0:T(8,128)(2,1)S(1)} %bitcast.79, bf16[1024,1120]{0,1:T(8,128)(2,1)S(1)} %copy-done.2, s32[]{:T(128)S(6)} %select_n.562), kind=kOutput, calls=%fused_computation.12 | convolution fusion | flops 5145548800 | bytes 20357124 | tf_op jit(solution)/shard_map/dot_general | solution.py:601
  438.3 8.4 %copy.32 = bf16[4480,560]{1,0:T(8,128)(2,1)} copy(bf16[4480,560]{0,1:T(8,128)(2,1)} %add_convert_fusion.1) | data formatting | bytes 10035200 | tf_op jit(solution)/shard_map/convert_element_type | solution.py:602
  458.9 5.7 collective-permute-done.44
  478.6 9.0 %add_convert_fusion = bf16[1152,2304]{1,0:T(8,128)(2,1)S(1)} fusion(bf16[1152,2304]{1,0:T(8,128)(2,1)} %collective-permute-done.22, bf16[1152,1024]{1,0:T(8,128)(2,1)S(1)} %copy-done.37, bf16[1024,4480]{1,0:T(8,128)(2,1)} %get-tuple-element.26, s32[]{:T(128)S(6)} %select_n.565), kind=kOutput, calls=%fused_computation.11 | convolution fusion | flops 5443780608 | bytes 17694724 | tf_op jit(solution)/shard_map/dot_general | solution.py:261
  489.4 4.2 collective-permute-done.46
  498.6 3.0 collective-permute-done.47
  502.5 6.0 %collective-permute-done.12 = bf16[1,1,1,1,72,640]{5,4,3,2,1,0:T(8,128)(2,1)S(1)} collective-permute-done((bf16[1,1,1,1,72,640]{5,4,3,2,1,0:T(8,128)(2,1)S(1)}, bf16[1,1,1,1,72,640]{5,4,3,2,1,0:T(8,128)(2,1)S(1)}, u32[]{:S(2)}, u32[]{:S(2)}) %collective-permute-start.12) | collective-permute-done | bytes 92192 | tf_op jit(solution)/shard_map/ppermute | solution.py:485
  508.5 3.4 collective-permute-start.8
  512.0 7.5 %collective-permute-done.8 = bf16[1,1,1,1,72,640]{5,4,3,2,1,0:T(8,128)(2,1)S(1)} collective-permute-done((bf16[1,1,1,1,72,640]{5,4,3,2,1,0:T(8,128)(2,1)S(1)}, bf16[1,1,1,1,72,640]{5,4,3,2,1,0:T(8,128)(2,1)S(1)}, u32[]{:S(2)}, u32[]{:S(2)}) %collective-permute-start.8) | collective-permute-done | bytes 92192 | tf_op jit(solution)/shard_map/ppermute | solution.py:485
  524.6 6.4 %collective-permute-done.32 = bf16[1,1,2,2,72,512]{5,4,3,2,1,0:T(8,128)(2,1)S(1)} collective-permute-done((bf16[1,1,2,2,72,512]{5,4,3,2,1,0:T(8,128)(2,1)S(1)}, bf16[1,1,2,2,72,512]{5,4,3,2,1,0:T(8,128)(2,1)S(1)}, u32[]{:S(2)}, u32[]{:S(2)}) %collective-permute-start.32) | collective-permute-done | bytes 294944 | tf_op jit(solution)/shard_map/ppermute | solution.py:485
  534.8 3.1 collective-permute-done.33
  538.9 6.3 %collective-permute-done.27 = bf16[2,2,1,2,72,896]{5,4,3,2,1,0:T(8,128)(2,1)S(1)} collective-permute-done((bf16[2,2,1,2,72,896]{5,4,3,2,1,0:T(8,128)(2,1)S(1)}, bf16[2,2,1,2,72,896]{5,4,3,2,1,0:T(8,128)(2,1)S(1)}, u32[]{:S(2)}, u32[]{:S(2)}) %collective-permute-start.27) | collective-permute-done | bytes 1032224 | tf_op jit(solution)/shard_map/ppermute | solution.py:485
  546.0 11.9 %collective-permute-done.34 = bf16[1,1,1,1,72,512]{5,4,3,2,1,0:T(8,128)(2,1)S(1)} collective-permute-done((bf16[1,1,1,1,72,512]{5,4,3,2,1,0:T(8,128)(2,1)S(1)}, bf16[1,1,1,1,72,512]{5,4,3,2,1,0:T(8,128)(2,1)S(1)}, u32[]{:S(2)}, u32[]{:S(2)}) %collective-permute-start.34) | collective-permute-done | bytes 73760 | tf_op jit(solution)/shard_map/ppermute | solution.py:485
  562.9 7.5 %collective-permute-done.38 = bf16[2,1,1,1,280,256]{5,4,3,2,1,0:T(8,128)(2,1)S(1)} collective-permute-done((bf16[2,1,1,1,280,256]{5,4,3,2,1,0:T(8,128)(2,1)S(1)}, bf16[2,1,1,1,280,256]{5,4,3,2,1,0:T(8,128)(2,1)S(1)}, u32[]{:S(2)}, u32[]{:S(2)}) %collective-permute-start.38) | collective-permute-done | bytes 286752 | tf_op jit(solution)/shard_map/ppermute | solution.py:485
  570.5 2.9 collective-permute-done.42
  573.5 3.2 collective-permute-start.43
  576.7 4.0 collective-permute-done.25
  585.2 4.6 collective-permute-done.26
  (258 shorter events, 102.1 us)
Async XLA Ops:
  2.5 22.2 %collective-permute-start = (bf16[512,1120]{0,1:T(8,128)(2,1)S(1)}, bf16[512,1120]{0,1:T(8,128)(2,1)}, u32[]{:S(2)}, u32[]{:S(2)}) collective-permute-start(bf16[512,1120]{0,1:T(8,128)(2,1)S(1)} %select_bitcast_fusion.5), channel_id=1, source_target_pairs={{0,16},{16,0},{1,17},{17,1},{2,18},{18,2},{3,19},{19,3},{4,20},{20... | collective-permute-start | bytes 3440648 | tf_op jit(solution)/shard_map/ppermute | solution.py:480
  4.2 111.3 %collective-permute-start.2 = (bf16[512,1120]{0,1:T(8,128)(2,1)}, bf16[512,1120]{0,1:T(8,128)(2,1)}, u32[]{:S(2)}, u32[]{:S(2)}) collective-permute-start(bf16[512,1120]{0,1:T(8,128)(2,1)} %select_bitcast_fusion.2), channel_id=1, source_target_pairs={{0,16},{16,0},{1,17},{17,1},{2,18},{18,2},{3,19},{19,3},{4,20},{20... | collective-permute-start | bytes 3440648 | tf_op jit(solution)/shard_map/ppermute | solution.py:480
  175.8 253.6 %collective-permute-start.35 = (bf16[4480,560]{0,1:T(8,128)(2,1)}, bf16[4480,560]{0,1:T(8,128)(2,1)}, u32[]{:S(2)}, u32[]{:S(2)}) collective-permute-start(bf16[4480,560]{0,1:T(8,128)(2,1)} %convolution_convert_fusion.1), channel_id=1, source_target_pairs={{0,16},{16,0},{1,17},{17,1},{2,18},{18,2},{3,19},{19,3},{4,20},{20... | collective-permute-start | bytes 15052808 | tf_op jit(solution)/shard_map/ppermute | solution.py:480
  205.7 141.8 %collective-permute-start.17 = (bf16[1152,560]{0,1:T(8,128)(2,1)}, bf16[1152,560]{0,1:T(8,128)(2,1)}, u32[]{:S(2)}, u32[]{:S(2)}) collective-permute-start(bf16[1152,560]{0,1:T(8,128)(2,1)} %convolution_convert_fusion.5), channel_id=1, source_target_pairs={{0,16},{16,0},{1,17},{17,1},{2,18},{18,2},{3,19},{19,3},{4,20},{20... | collective-permute-start | bytes 3870728 | tf_op jit(solution)/shard_map/ppermute | solution.py:480
  282.9 103.5 %collective-permute-start.4 = (bf16[1152,1792]{1,0:T(8,128)(2,1)}, bf16[1152,1792]{1,0:T(8,128)(2,1)}, u32[]{:S(2)}, u32[]{:S(2)}) collective-permute-start(bf16[1152,1792]{1,0:T(8,128)(2,1)} %convolution_convert_fusion.2), channel_id=1, source_target_pairs={{0,16},{16,0},{1,17},{17,1},{2,18},{18,2},{3,19},{19,3},{4,20},{20... | collective-permute-start | bytes 12386312 | tf_op jit(solution)/shard_map/ppermute | solution.py:480
  287.0 58.0 %collective-permute-start.3 = (bf16[512,1120]{0,1:T(8,128)(2,1)S(1)}, bf16[512,1120]{0,1:T(8,128)(2,1)}, u32[]{:S(2)}, u32[]{:S(2)}) collective-permute-start(bf16[512,1120]{0,1:T(8,128)(2,1)S(1)} %broadcast_select_fusion.2), channel_id=1, source_target_pairs={{0,16},{16,0},{1,17},{17,1},{2,18},{18,2},{3,19},{19,3},{4,20},{20... | collective-permute-start | bytes 3440648 | tf_op jit(solution)/shard_map/ppermute | solution.py:480
  296.8 181.4 %collective-permute-start.22 = (bf16[1152,2304]{1,0:T(8,128)(2,1)}, bf16[1152,2304]{1,0:T(8,128)(2,1)}, u32[]{:S(2)}, u32[]{:S(2)}) collective-permute-start(bf16[1152,2304]{1,0:T(8,128)(2,1)} %convolution_convert_fusion), channel_id=1, source_target_pairs={{0,16},{16,0},{1,17},{17,1},{2,18},{18,2},{3,19},{19,3},{4,20},{20... | collective-permute-start | bytes 15925256 | tf_op jit(solution)/shard_map/ppermute | solution.py:480
  345.0 13.0 %collective-permute-start.1 = (bf16[512,1120]{0,1:T(8,128)(2,1)}, bf16[512,1120]{0,1:T(8,128)(2,1)}, u32[]{:S(2)}, u32[]{:S(2)}) collective-permute-start(bf16[512,1120]{0,1:T(8,128)(2,1)} %broadcast_select_fusion.4), channel_id=1, source_target_pairs={{0,16},{16,0},{1,17},{17,1},{2,18},{18,2},{3,19},{19,3},{4,20},{20... | collective-permute-start | bytes 3440648 | tf_op jit(solution)/shard_map/ppermute | solution.py:480
  355.6 19.5 %collective-permute-start.18 = (bf16[2,2,2,1,72,560]{5,4,3,2,1,0:T(8,128)(2,1)S(1)}, bf16[2,2,2,1,72,560]{5,4,3,2,1,0:T(8,128)(2,1)S(1)}, u32[]{:S(2)}, u32[]{:S(2)}) collective-permute-start(bf16[2,2,2,1,72,560]{5,4,3,2,1,0:T(8,128)(2,1)S(1)} %constant_dynamic-slice_fusion.4), channel_id=1, source_target_pairs={{0,1},{1,0},{2,3},{3,2},{4,5},{5,4},{6,7},{7,6},{8,9},{9,8},{10,11... | collective-permute-start | bytes 1935368 | tf_op jit(solution)/shard_map/ppermute | solution.py:485
  375.3 10.5 %collective-permute-start.19 = (bf16[2,2,1,1,72,560]{5,4,3,2,1,0:T(8,128)(2,1)S(1)}, bf16[2,2,1,1,72,560]{5,4,3,2,1,0:T(8,128)(2,1)S(1)}, u32[]{:S(2)}, u32[]{:S(2)}) collective-permute-start(bf16[2,2,1,1,72,560]{5,4,3,2,1,0:T(8,128)(2,1)S(1)} %get-tuple-element.51), channel_id=1, source_target_pairs={{0,2},{1,3},{2,0},{3,1},{4,6},{5,7},{6,4},{7,5},{8,10},{9,11},{10,... | collective-permute-start | bytes 967688 | tf_op jit(solution)/shard_map/ppermute | solution.py:485
  385.9 11.8 %collective-permute-start.20 = (bf16[2,1,1,1,72,560]{5,4,3,2,1,0:T(8,128)(2,1)S(1)}, bf16[2,1,1,1,72,560]{5,4,3,2,1,0:T(8,128)(2,1)S(1)}, u32[]{:S(2)}, u32[]{:S(2)}) collective-permute-start(bf16[2,1,1,1,72,560]{5,4,3,2,1,0:T(8,128)(2,1)S(1)} %get-tuple-element.71), channel_id=1, source_target_pairs={{0,4},{1,5},{2,6},{3,7},{4,0},{5,1},{6,2},{7,3},{8,12},{9,13},{10,... | collective-permute-start | bytes 483848 | tf_op jit(solution)/shard_map/ppermute | solution.py:485
  394.1 14.1 %collective-permute-start.13 = (bf16[2,1,2,2,72,512]{5,4,3,2,1,0:T(8,128)(2,1)S(1)}, bf16[2,1,2,2,72,512]{5,4,3,2,1,0:T(8,128)(2,1)S(1)}, u32[]{:S(2)}, u32[]{:S(2)}) collective-permute-start(bf16[2,1,2,2,72,512]{5,4,3,2,1,0:T(8,128)(2,1)S(1)} %constant_dynamic-slice_fusion.7), channel_id=1, source_target_pairs={{0,4},{1,5},{2,6},{3,7},{4,0},{5,1},{6,2},{7,3},{8,12},{9,13},{10,... | collective-permute-start | bytes 1769480 | tf_op jit(solution)/shard_map/ppermute | solution.py:485
  396.1 20.0 %collective-permute-start.9 = (bf16[2,2,1,2,72,640]{5,4,3,2,1,0:T(8,128)(2,1)S(1)}, bf16[2,2,1,2,72,640]{5,4,3,2,1,0:T(8,128)(2,1)S(1)}, u32[]{:S(2)}, u32[]{:S(2)}) collective-permute-start(bf16[2,2,1,2,72,640]{5,4,3,2,1,0:T(8,128)(2,1)S(1)} %constant_dynamic-slice_fusion.9), channel_id=1, source_target_pairs={{0,2},{1,3},{2,0},{3,1},{4,6},{5,7},{6,4},{7,5},{8,10},{9,11},{10,... | collective-permute-start | bytes 2211848 | tf_op jit(solution)/shard_map/ppermute | solution.py:485
  397.8 20.7 %collective-permute-start.5 = (bf16[2,2,2,1,72,640]{5,4,3,2,1,0:T(8,128)(2,1)S(1)}, bf16[2,2,2,1,72,640]{5,4,3,2,1,0:T(8,128)(2,1)S(1)}, u32[]{:S(2)}, u32[]{:S(2)}) collective-permute-start(bf16[2,2,2,1,72,640]{5,4,3,2,1,0:T(8,128)(2,1)S(1)} %constant_dynamic-slice_fusion.11), channel_id=1, source_target_pairs={{0,1},{1,0},{2,3},{3,2},{4,5},{5,4},{6,7},{7,6},{8,9},{9,8},{10,11... | collective-permute-start | bytes 2211848 | tf_op jit(solution)/shard_map/ppermute | solution.py:485
  408.2 5.5 collective-permute-start.21
  413.6 13.7 %collective-permute-start.14 = (bf16[1,1,2,2,72,512]{5,4,3,2,1,0:T(8,128)(2,1)S(1)}, bf16[1,1,2,2,72,512]{5,4,3,2,1,0:T(8,128)(2,1)S(1)}, u32[]{:S(2)}, u32[]{:S(2)}) collective-permute-start(bf16[1,1,2,2,72,512]{5,4,3,2,1,0:T(8,128)(2,1)S(1)} %get-tuple-element.59), channel_id=1, source_target_pairs={{0,8},{1,9},{2,10},{3,11},{4,12},{5,13},{6,14},{7,15},{8,0},{9,1},... | collective-permute-start | bytes 884744 | tf_op jit(solution)/shard_map/ppermute | solution.py:485
  417.1 56.2 %collective-permute-start.10 = (bf16[2,2,1,1,72,640]{5,4,3,2,1,0:T(8,128)(2,1)}, bf16[2,2,1,1,72,640]{5,4,3,2,1,0:T(8,128)(2,1)}, u32[]{:S(2)}, u32[]{:S(2)}) collective-permute-start(bf16[2,2,1,1,72,640]{5,4,3,2,1,0:T(8,128)(2,1)} %get-tuple-element.55), channel_id=1, source_target_pairs={{0,1},{1,0},{2,3},{3,2},{4,5},{5,4},{6,7},{7,6},{8,9},{9,8},{10,11... | collective-permute-start | bytes 1105928 | tf_op jit(solution)/shard_map/ppermute | solution.py:485
  419.6 55.5 %collective-permute-start.6 = (bf16[2,2,1,1,72,640]{5,4,3,2,1,0:T(8,128)(2,1)}, bf16[2,2,1,1,72,640]{5,4,3,2,1,0:T(8,128)(2,1)}, u32[]{:S(2)}, u32[]{:S(2)}) collective-permute-start(bf16[2,2,1,1,72,640]{5,4,3,2,1,0:T(8,128)(2,1)} %get-tuple-element.53), channel_id=1, source_target_pairs={{0,2},{1,3},{2,0},{3,1},{4,6},{5,7},{6,4},{7,5},{8,10},{9,11},{10,... | collective-permute-start | bytes 1105928 | tf_op jit(solution)/shard_map/ppermute | solution.py:485
  428.1 29.0 %collective-permute-start.15 = (bf16[1,1,2,1,72,512]{5,4,3,2,1,0:T(8,128)(2,1)}, bf16[1,1,2,1,72,512]{5,4,3,2,1,0:T(8,128)(2,1)}, u32[]{:S(2)}, u32[]{:S(2)}) collective-permute-start(bf16[1,1,2,1,72,512]{5,4,3,2,1,0:T(8,128)(2,1)} %get-tuple-element.79), channel_id=1, source_target_pairs={{0,1},{1,0},{2,3},{3,2},{4,5},{5,4},{6,7},{7,6},{8,9},{9,8},{10,11... | collective-permute-start | bytes 442376 | tf_op jit(solution)/shard_map/ppermute | solution.py:485
  456.0 8.5 %collective-permute-start.44 = (bf16[2,1,2,2,280,48]{4,5,3,2,1,0:T(8,128)(2,1)}, bf16[2,1,2,2,280,48]{4,5,3,2,1,0:T(8,128)(2,1)S(1)}, u32[]{:S(2)}, u32[]{:S(2)}) collective-permute-start(bf16[2,1,2,2,280,48]{4,5,3,2,1,0:T(8,128)(2,1)} %copy.33), channel_id=1, source_target_pairs={{0,4},{1,5},{2,6},{3,7},{4,0},{5,1},{6,2},{7,3},{8,12},{9,13},{10,... | collective-permute-start | bytes 645128 | tf_op jit(solution)/shard_map/ppermute | solution.py:485
  457.1 65.0 %collective-permute-start.36 = (bf16[2,2,2,1,280,256]{5,4,3,2,1,0:T(8,128)(2,1)}, bf16[2,2,2,1,280,256]{5,4,3,2,1,0:T(8,128)(2,1)}, u32[]{:S(2)}, u32[]{:S(2)}) collective-permute-start(bf16[2,2,2,1,280,256]{5,4,3,2,1,0:T(8,128)(2,1)} %constant_dynamic-slice_fusion.5), channel_id=1, source_target_pairs={{0,1},{1,0},{2,3},{3,2},{4,5},{5,4},{6,7},{7,6},{8,9},{9,8},{10,11... | collective-permute-start | bytes 3440648 | tf_op jit(solution)/shard_map/ppermute | solution.py:485
  464.6 6.3 %collective-permute-start.16 = (bf16[1,1,1,1,72,512]{5,4,3,2,1,0:T(8,128)(2,1)S(1)}, bf16[1,1,1,1,72,512]{5,4,3,2,1,0:T(8,128)(2,1)}, u32[]{:S(2)}, u32[]{:S(2)}) collective-permute-start(bf16[1,1,1,1,72,512]{5,4,3,2,1,0:T(8,128)(2,1)S(1)} %add_convert_fusion.61), channel_id=1, source_target_pairs={{0,2},{1,3},{2,0},{3,1},{4,6},{5,7},{6,4},{7,5},{8,10},{9,11},{10,... | collective-permute-start | bytes 221192 | tf_op jit(solution)/shard_map/ppermute | solution.py:485
  470.9 60.8 %collective-permute-start.40 = (bf16[2,2,1,2,280,256]{5,4,3,2,1,0:T(8,128)(2,1)}, bf16[2,2,1,2,280,256]{5,4,3,2,1,0:T(8,128)(2,1)S(1)}, u32[]{:S(2)}, u32[]{:S(2)}) collective-permute-start(bf16[2,2,1,2,280,256]{5,4,3,2,1,0:T(8,128)(2,1)} %constant_dynamic-slice_fusion.1), channel_id=1, source_target_pairs={{0,2},{1,3},{2,0},{3,1},{4,6},{5,7},{6,4},{7,5},{8,10},{9,11},{10,... | collective-permute-start | bytes 3440648 | tf_op jit(solution)/shard_map/ppermute | solution.py:485
  473.4 14.9 %collective-permute-start.45 = (bf16[1,1,2,2,280,48]{5,4,3,2,1,0:T(8,128)(2,1)S(1)}, bf16[1,1,2,2,280,48]{5,4,3,2,1,0:T(8,128)(2,1)S(1)}, u32[]{:S(2)}, u32[]{:S(2)}) collective-permute-start(bf16[1,1,2,2,280,48]{5,4,3,2,1,0:T(8,128)(2,1)S(1)} %get-tuple-element.65), channel_id=1, source_target_pairs={{0,8},{1,9},{2,10},{3,11},{4,12},{5,13},{6,14},{7,15},{8,0},{9,1},... | collective-permute-start | bytes 322568 | tf_op jit(solution)/shard_map/ppermute | solution.py:485
  475.1 19.3 %collective-permute-start.11 = (bf16[2,1,1,1,72,640]{5,4,3,2,1,0:T(8,128)(2,1)S(1)}, bf16[2,1,1,1,72,640]{5,4,3,2,1,0:T(8,128)(2,1)S(1)}, u32[]{:S(2)}, u32[]{:S(2)}) collective-permute-start(bf16[2,1,1,1,72,640]{5,4,3,2,1,0:T(8,128)(2,1)S(1)} %get-tuple-element.75), channel_id=1, source_target_pairs={{0,4},{1,5},{2,6},{3,7},{4,0},{5,1},{6,2},{7,3},{8,12},{9,13},{10,... | collective-permute-start | bytes 552968 | tf_op jit(solution)/shard_map/ppermute | solution.py:485
  478.2 19.0 %collective-permute-start.7 = (bf16[2,1,1,1,72,640]{5,4,3,2,1,0:T(8,128)(2,1)S(1)}, bf16[2,1,1,1,72,640]{5,4,3,2,1,0:T(8,128)(2,1)S(1)}, u32[]{:S(2)}, u32[]{:S(2)}) collective-permute-start(bf16[2,1,1,1,72,640]{5,4,3,2,1,0:T(8,128)(2,1)S(1)} %get-tuple-element.73), channel_id=1, source_target_pairs={{0,4},{1,5},{2,6},{3,7},{4,0},{5,1},{6,2},{7,3},{8,12},{9,13},{10,... | collective-permute-start | bytes 552968 | tf_op jit(solution)/shard_map/ppermute | solution.py:485
  488.4 5.2 collective-permute-start.46
  493.5 40.1 %collective-permute-start.23 = (bf16[2,2,2,1,72,896]{5,4,3,2,1,0:T(8,128)(2,1)S(1)}, bf16[2,2,2,1,72,896]{5,4,3,2,1,0:T(8,128)(2,1)S(1)}, u32[]{:S(2)}, u32[]{:S(2)}) collective-permute-start(bf16[2,2,2,1,72,896]{5,4,3,2,1,0:T(8,128)(2,1)S(1)} %constant_dynamic-slice_fusion.2), channel_id=1, source_target_pairs={{0,1},{1,0},{2,3},{3,2},{4,5},{5,4},{6,7},{7,6},{8,9},{9,8},{10,11... | collective-permute-start | bytes 3096584 | tf_op jit(solution)/shard_map/ppermute | solution.py:485
  494.4 26.4 %collective-permute-start.31 = (bf16[2,1,2,2,72,512]{5,4,3,2,1,0:T(8,128)(2,1)S(1)}, bf16[2,1,2,2,72,512]{5,4,3,2,1,0:T(8,128)(2,1)S(1)}, u32[]{:S(2)}, u32[]{:S(2)}) collective-permute-start(bf16[2,1,2,2,72,512]{5,4,3,2,1,0:T(8,128)(2,1)S(1)} %constant_dynamic-slice_fusion.6), channel_id=1, source_target_pairs={{0,4},{1,5},{2,6},{3,7},{4,0},{5,1},{6,2},{7,3},{8,12},{9,13},{10,... | collective-permute-start | bytes 1769480 | tf_op jit(solution)/shard_map/ppermute | solution.py:485
  497.2 4.4 collective-permute-start.47
  501.6 6.9 %collective-permute-start.12 = (bf16[1,1,1,1,72,640]{5,4,3,2,1,0:T(8,128)(2,1)S(1)}, bf16[1,1,1,1,72,640]{5,4,3,2,1,0:T(8,128)(2,1)S(1)}, u32[]{:S(2)}, u32[]{:S(2)}) collective-permute-start(bf16[1,1,1,1,72,640]{5,4,3,2,1,0:T(8,128)(2,1)S(1)} %add_convert_fusion.55), channel_id=1, source_target_pairs={{0,8},{1,9},{2,10},{3,11},{4,12},{5,13},{6,14},{7,15},{8,0},{9,1},... | collective-permute-start | bytes 276488 | tf_op jit(solution)/shard_map/ppermute | solution.py:485
  508.5 11.0 %collective-permute-start.8 = (bf16[1,1,1,1,72,640]{5,4,3,2,1,0:T(8,128)(2,1)S(1)}, bf16[1,1,1,1,72,640]{5,4,3,2,1,0:T(8,128)(2,1)S(1)}, u32[]{:S(2)}, u32[]{:S(2)}) collective-permute-start(bf16[1,1,1,1,72,640]{5,4,3,2,1,0:T(8,128)(2,1)S(1)} %add_convert_fusion.57), channel_id=1, source_target_pairs={{0,8},{1,9},{2,10},{3,11},{4,12},{5,13},{6,14},{7,15},{8,0},{9,1},... | collective-permute-start | bytes 276488 | tf_op jit(solution)/shard_map/ppermute | solution.py:485
  519.5 25.7 %collective-permute-start.27 = (bf16[2,2,1,2,72,896]{5,4,3,2,1,0:T(8,128)(2,1)S(1)}, bf16[2,2,1,2,72,896]{5,4,3,2,1,0:T(8,128)(2,1)S(1)}, u32[]{:S(2)}, u32[]{:S(2)}) collective-permute-start(bf16[2,2,1,2,72,896]{5,4,3,2,1,0:T(8,128)(2,1)S(1)} %constant_dynamic-slice_fusion), channel_id=1, source_target_pairs={{0,2},{1,3},{2,0},{3,1},{4,6},{5,7},{6,4},{7,5},{8,10},{9,11},{10,... | collective-permute-start | bytes 3096584 | tf_op jit(solution)/shard_map/ppermute | solution.py:485
  521.0 10.0 %collective-permute-start.32 = (bf16[1,1,2,2,72,512]{5,4,3,2,1,0:T(8,128)(2,1)S(1)}, bf16[1,1,2,2,72,512]{5,4,3,2,1,0:T(8,128)(2,1)S(1)}, u32[]{:S(2)}, u32[]{:S(2)}) collective-permute-start(bf16[1,1,2,2,72,512]{5,4,3,2,1,0:T(8,128)(2,1)S(1)} %get-tuple-element.57), channel_id=1, source_target_pairs={{0,8},{1,9},{2,10},{3,11},{4,12},{5,13},{6,14},{7,15},{8,0},{9,1},... | collective-permute-start | bytes 884744 | tf_op jit(solution)/shard_map/ppermute | solution.py:485
  523.7 34.3 %collective-permute-start.37 = (bf16[2,2,1,1,280,256]{5,4,3,2,1,0:T(8,128)(2,1)S(1)}, bf16[2,2,1,1,280,256]{5,4,3,2,1,0:T(8,128)(2,1)S(1)}, u32[]{:S(2)}, u32[]{:S(2)}) collective-permute-start(bf16[2,2,1,1,280,256]{5,4,3,2,1,0:T(8,128)(2,1)S(1)} %get-tuple-element.35), channel_id=1, source_target_pairs={{0,2},{1,3},{2,0},{3,1},{4,6},{5,7},{6,4},{7,5},{8,10},{9,11},{10,... | collective-permute-start | bytes 1720328 | tf_op jit(solution)/shard_map/ppermute | solution.py:485
  531.1 6.9 %collective-permute-start.33 = (bf16[1,1,2,1,72,512]{5,4,3,2,1,0:T(8,128)(2,1)S(1)}, bf16[1,1,2,1,72,512]{5,4,3,2,1,0:T(8,128)(2,1)S(1)}, u32[]{:S(2)}, u32[]{:S(2)}) collective-permute-start(bf16[1,1,2,1,72,512]{5,4,3,2,1,0:T(8,128)(2,1)S(1)} %get-tuple-element.77), channel_id=1, source_target_pairs={{0,1},{1,0},{2,3},{3,2},{4,5},{5,4},{6,7},{7,6},{8,9},{9,8},{10,11... | collective-permute-start | bytes 442376 | tf_op jit(solution)/shard_map/ppermute | solution.py:485
  532.0 28.0 %collective-permute-start.41 = (bf16[2,2,1,1,280,256]{5,4,3,2,1,0:T(8,128)(2,1)S(1)}, bf16[2,2,1,1,280,256]{5,4,3,2,1,0:T(8,128)(2,1)S(1)}, u32[]{:S(2)}, u32[]{:S(2)}) collective-permute-start(bf16[2,2,1,1,280,256]{5,4,3,2,1,0:T(8,128)(2,1)S(1)} %get-tuple-element.37), channel_id=1, source_target_pairs={{0,1},{1,0},{2,3},{3,2},{4,5},{5,4},{6,7},{7,6},{8,9},{9,8},{10,11... | collective-permute-start | bytes 1720328 | tf_op jit(solution)/shard_map/ppermute | solution.py:485
  533.9 26.6 %collective-permute-start.24 = (bf16[2,2,1,1,72,896]{5,4,3,2,1,0:T(8,128)(2,1)S(1)}, bf16[2,2,1,1,72,896]{5,4,3,2,1,0:T(8,128)(2,1)S(1)}, u32[]{:S(2)}, u32[]{:S(2)}) collective-permute-start(bf16[2,2,1,1,72,896]{5,4,3,2,1,0:T(8,128)(2,1)S(1)} %get-tuple-element.47), channel_id=1, source_target_pairs={{0,2},{1,3},{2,0},{3,1},{4,6},{5,7},{6,4},{7,5},{8,10},{9,11},{10,... | collective-permute-start | bytes 1548296 | tf_op jit(solution)/shard_map/ppermute | solution.py:485
  538.0 20.0 %collective-permute-start.34 = (bf16[1,1,1,1,72,512]{5,4,3,2,1,0:T(8,128)(2,1)S(1)}, bf16[1,1,1,1,72,512]{5,4,3,2,1,0:T(8,128)(2,1)S(1)}, u32[]{:S(2)}, u32[]{:S(2)}) collective-permute-start(bf16[1,1,1,1,72,512]{5,4,3,2,1,0:T(8,128)(2,1)S(1)} %add_convert_fusion.59), channel_id=1, source_target_pairs={{0,2},{1,3},{2,0},{3,1},{4,6},{5,7},{6,4},{7,5},{8,10},{9,11},{10,... | collective-permute-start | bytes 221192 | tf_op jit(solution)/shard_map/ppermute | solution.py:485
  545.5 16.9 %collective-permute-start.28 = (bf16[2,2,1,1,72,896]{5,4,3,2,1,0:T(8,128)(2,1)S(1)}, bf16[2,2,1,1,72,896]{5,4,3,2,1,0:T(8,128)(2,1)S(1)}, u32[]{:S(2)}, u32[]{:S(2)}) collective-permute-start(bf16[2,2,1,1,72,896]{5,4,3,2,1,0:T(8,128)(2,1)S(1)} %get-tuple-element.49), channel_id=1, source_target_pairs={{0,1},{1,0},{2,3},{3,2},{4,5},{5,4},{6,7},{7,6},{8,9},{9,8},{10,11... | collective-permute-start | bytes 1548296 | tf_op jit(solution)/shard_map/ppermute | solution.py:485
  558.2 12.2 %collective-permute-start.38 = (bf16[2,1,1,1,280,256]{5,4,3,2,1,0:T(8,128)(2,1)S(1)}, bf16[2,1,1,1,280,256]{5,4,3,2,1,0:T(8,128)(2,1)S(1)}, u32[]{:S(2)}, u32[]{:S(2)}) collective-permute-start(bf16[2,1,1,1,280,256]{5,4,3,2,1,0:T(8,128)(2,1)S(1)} %get-tuple-element.61), channel_id=1, source_target_pairs={{0,4},{1,5},{2,6},{3,7},{4,0},{5,1},{6,2},{7,3},{8,12},{9,13},{10,... | collective-permute-start | bytes 860168 | tf_op jit(solution)/shard_map/ppermute | solution.py:485
  560.2 13.3 %collective-permute-start.42 = (bf16[2,1,1,1,280,256]{5,4,3,2,1,0:T(8,128)(2,1)S(1)}, bf16[2,1,1,1,280,256]{5,4,3,2,1,0:T(8,128)(2,1)S(1)}, u32[]{:S(2)}, u32[]{:S(2)}) collective-permute-start(bf16[2,1,1,1,280,256]{5,4,3,2,1,0:T(8,128)(2,1)S(1)} %get-tuple-element.63), channel_id=1, source_target_pairs={{0,4},{1,5},{2,6},{3,7},{4,0},{5,1},{6,2},{7,3},{8,12},{9,13},{10,... | collective-permute-start | bytes 860168 | tf_op jit(solution)/shard_map/ppermute | solution.py:485
  560.6 20.0 %collective-permute-start.25 = (bf16[2,1,1,1,72,896]{5,4,3,2,1,0:T(8,128)(2,1)S(1)}, bf16[2,1,1,1,72,896]{5,4,3,2,1,0:T(8,128)(2,1)S(1)}, u32[]{:S(2)}, u32[]{:S(2)}) collective-permute-start(bf16[2,1,1,1,72,896]{5,4,3,2,1,0:T(8,128)(2,1)S(1)} %get-tuple-element.67), channel_id=1, source_target_pairs={{0,4},{1,5},{2,6},{3,7},{4,0},{5,1},{6,2},{7,3},{8,12},{9,13},{10,... | collective-permute-start | bytes 774152 | tf_op jit(solution)/shard_map/ppermute | solution.py:485
  562.6 20.8 %collective-permute-start.29 = (bf16[2,1,1,1,72,896]{5,4,3,2,1,0:T(8,128)(2,1)S(1)}, bf16[2,1,1,1,72,896]{5,4,3,2,1,0:T(8,128)(2,1)S(1)}, u32[]{:S(2)}, u32[]{:S(2)}) collective-permute-start(bf16[2,1,1,1,72,896]{5,4,3,2,1,0:T(8,128)(2,1)S(1)} %get-tuple-element.69), channel_id=1, source_target_pairs={{0,4},{1,5},{2,6},{3,7},{4,0},{5,1},{6,2},{7,3},{8,12},{9,13},{10,... | collective-permute-start | bytes 774152 | tf_op jit(solution)/shard_map/ppermute | solution.py:485
  570.4 13.7 %collective-permute-start.39 = (bf16[1,1,1,1,280,256]{5,4,3,2,1,0:T(8,128)(2,1)S(1)}, bf16[1,1,1,1,280,256]{5,4,3,2,1,0:T(8,128)(2,1)S(1)}, u32[]{:S(2)}, u32[]{:S(2)}) collective-permute-start(bf16[1,1,1,1,280,256]{5,4,3,2,1,0:T(8,128)(2,1)S(1)} %add_convert_fusion.47), channel_id=1, source_target_pairs={{0,8},{1,9},{2,10},{3,11},{4,12},{5,13},{6,14},{7,15},{8,0},{9,1},... | collective-permute-start | bytes 430088 | tf_op jit(solution)/shard_map/ppermute | solution.py:485
  573.5 10.7 %collective-permute-start.43 = (bf16[1,1,1,1,280,256]{5,4,3,2,1,0:T(8,128)(2,1)S(1)}, bf16[1,1,1,1,280,256]{5,4,3,2,1,0:T(8,128)(2,1)S(1)}, u32[]{:S(2)}, u32[]{:S(2)}) collective-permute-start(bf16[1,1,1,1,280,256]{5,4,3,2,1,0:T(8,128)(2,1)S(1)} %add_convert_fusion.45), channel_id=1, source_target_pairs={{0,8},{1,9},{2,10},{3,11},{4,12},{5,13},{6,14},{7,15},{8,0},{9,1},... | collective-permute-start | bytes 430088 | tf_op jit(solution)/shard_map/ppermute | solution.py:485
  580.7 9.1 %collective-permute-start.26 = (bf16[1,1,1,1,72,896]{5,4,3,2,1,0:T(8,128)(2,1)S(1)}, bf16[1,1,1,1,72,896]{5,4,3,2,1,0:T(8,128)(2,1)S(1)}, u32[]{:S(2)}, u32[]{:S(2)}) collective-permute-start(bf16[1,1,1,1,72,896]{5,4,3,2,1,0:T(8,128)(2,1)S(1)} %add_convert_fusion.51), channel_id=1, source_target_pairs={{0,8},{1,9},{2,10},{3,11},{4,12},{5,13},{6,14},{7,15},{8,0},{9,1},... | collective-permute-start | bytes 387080 | tf_op jit(solution)/shard_map/ppermute | solution.py:485
  583.5 7.7 %collective-permute-start.30 = (bf16[1,1,1,1,72,896]{5,4,3,2,1,0:T(8,128)(2,1)S(1)}, bf16[1,1,1,1,72,896]{5,4,3,2,1,0:T(8,128)(2,1)S(1)}, u32[]{:S(2)}, u32[]{:S(2)}) collective-permute-start(bf16[1,1,1,1,72,896]{5,4,3,2,1,0:T(8,128)(2,1)S(1)} %add_convert_fusion.49), channel_id=1, source_target_pairs={{0,8},{1,9},{2,10},{3,11},{4,12},{5,13},{6,14},{7,15},{8,0},{9,1},... | collective-permute-start | bytes 387080 | tf_op jit(solution)/shard_map/ppermute | solution.py:485
  (45 other events, 994.9 us)

commit v2 on v1

--- a/solution.py
+++ b/solution.py
@@ -1,4 +1,5 @@
 import functools
+import math
 
 import jax
 import jax.numpy as jnp
@@ -423,13 +424,13 @@
     return pl.BlockSpec(shape, lambda step, *_: (0, place), pipeline_mode=pl.Buffered(1))
 
 
-def attention_forward(qkv, length, per=2):
+def attention_forward(qkv, length, heads, per=2):
     seq, width = qkv.shape[0], qkv.shape[1] // 3
     return pl.pallas_call(
         functools.partial(attention_forward_kernel, per),
         grid_spec=pltpu.PrefetchScalarGridSpec(
             num_scalar_prefetch=1,
-            grid=(HEADS // per,),
+            grid=(heads // per,),
             in_specs=[resident((seq, width), place) for place in range(3)],
             out_specs=[
                 resident((seq, width)),
@@ -438,13 +439,13 @@
         ),
         out_shape=[
             jax.ShapeDtypeStruct((seq, width), BF16),
-            jax.ShapeDtypeStruct((HEADS, 8, seq), F32),
+            jax.ShapeDtypeStruct((heads, 8, seq), F32),
         ],
         compiler_params=pltpu.CompilerParams(vmem_limit_bytes=56 << 20),
         cost_estimate=pl.CostEstimate(
-            flops=2 * 2 * HEADS * seq * seq * WINDOW * 5 // 8,
+            flops=2 * 2 * heads * seq * seq * WINDOW * 5 // 8,
             bytes_accessed=8 * seq * width,
-            transcendentals=HEADS * seq * seq * 5 // 8,
+            transcendentals=heads * seq * seq * 5 // 8,
         ),
         name="attention_forward",
     )(length, qkv, qkv, qkv)
@@ -452,28 +453,516 @@
 
 def attention_backward(qkv, attended, grad_attended, lse, length, per=2):
     seq, width = qkv.shape[0], qkv.shape[1] // 3
+    heads = lse.shape[0]
     return pl.pallas_call(
         functools.partial(attention_backward_kernel, per),
         grid_spec=pltpu.PrefetchScalarGridSpec(
             num_scalar_prefetch=1,
-            grid=(HEADS // per,),
+            grid=(heads // per,),
             in_specs=[resident((seq, width), place) for place in (0, 1, 2, 0, 0)]
             + [pl.BlockSpec((per, 8, seq), lambda step, *_: (step, 0, 0))],
             out_specs=resident((seq, 3 * width)),
             scratch_shapes=[
-                pltpu.VMEM((-(-HEADS // 16) * 16, seq), F32),
+                pltpu.VMEM((-(-heads // 16) * 16, seq), F32),
                 pltpu.VMEM((per, seq, WINDOW), F32),
             ],
         ),
         out_shape=jax.ShapeDtypeStruct((seq, 3 * width), BF16),
         compiler_params=pltpu.CompilerParams(vmem_limit_bytes=58 << 20),
         cost_estimate=pl.CostEstimate(
-            flops=5 * 2 * HEADS * seq * seq * WINDOW * 5 // 8,
+            flops=5 * 2 * heads * seq * seq * WINDOW * 5 // 8,
             bytes_accessed=16 * seq * width,
-            transcendentals=HEADS * seq * seq * 5 // 8,
+            transcendentals=heads * seq * seq * 5 // 8,
         ),
         name="attention_backward",
     )(length, qkv, qkv, qkv, attended, grad_attended, lse)
+
+
+def once(shape):
+    return pl.BlockSpec(shape, lambda step, *_: (0, 0), pipeline_mode=pl.Buffered(1))
+
+
+def lane_tiles(rows, tile):
+    return pl.BlockSpec((rows, tile), lambda step, *_: (0, step))
+
+
+def row_tiles(tile, columns):
+    return pl.BlockSpec((tile, columns), lambda step, *_: (step, 0))
+
+
+def spread_store(rows_ref, scratch_ref, value, chips):
+    depth = value.shape[0]
+    rows = depth // chips
+    padded = rows_ref.shape[0] // chips
+    scratch_ref[:depth] = value
+    for pair in range(chips // 2):
+        first = 2 * pair * rows
+        both = jnp.concatenate(
+            [
+                scratch_ref[first : first + padded],
+                scratch_ref[first + rows : first + rows + padded],
+            ],
+            axis=0,
+        )
+        rows_ref[2 * pair * padded : 2 * (pair + 1) * padded] = both.astype(BF16)
+
+
+def norm_down(value, gain, bias):
+    centred = value - jnp.mean(value, axis=0, keepdims=True)
+    inverse = lax.rsqrt(jnp.mean(centred * centred, axis=0, keepdims=True) + EPSILON)
+    return centred * inverse * gain + bias
+
+
+def cell_tile(core_ref, mine_ref, other_ref):
+    return jnp.where(pl.program_id(0) // 2 == core_ref[0], mine_ref[0], other_ref[...]).astype(F32)
+
+
+def project_kernel(
+    chips, spans, core_ref, mine_ref, other_ref, norm_ref, w_ref, *rest
+):
+    out_refs, rows_ref, wide_refs, scratch_ref = (
+        rest[: len(spans)],
+        rest[len(spans)],
+        rest[len(spans) + 1 : -1],
+        rest[-1],
+    )
+    depth = w_ref.shape[0]
+
+    @pl.when(pl.program_id(0) == 0)
+    def _():
+        scratch_ref[...] = jnp.zeros_like(scratch_ref)
+        for wide_ref, (first, size) in zip(wide_refs, spans):
+            width = wide_ref.shape[1] // 3
+            for part in range(3):
+                begin = part * depth + first
+                wide_ref[:, part * width : part * width + size] = w_ref[:, begin : begin + size]
+                if size < width:
+                    wide_ref[:, part * width + size : (part + 1) * width] = jnp.zeros(
+                        (depth, width - size), BF16
+                    )
+
+    columns = jnp.transpose(norm_ref[...])
+    normed = norm_down(cell_tile(core_ref, mine_ref, other_ref), columns[:, 0:1], columns[:, 1:2])
+    spread_store(rows_ref, scratch_ref, normed, chips)
+    left = jnp.transpose(normed.astype(BF16))
+    for out_ref, wide_ref in zip(out_refs, wide_refs):
+        out_ref[...] = dot(left, wide_ref[...]).astype(BF16)
+
+
+def cell_specs(depth, tile):
+    return [
+        pl.BlockSpec((1, depth, tile), lambda step, core, *_: (core[0], 0, step % 2)),
+        pl.BlockSpec((depth, tile), lambda step, core, *_: (0, step % 2)),
+    ]
+
+
+def project(core, turned, other, norms, w, spans, chips, rows_pad):
+    _, depth, half = turned.shape
+    tile = half // 2
+    widths = [3 * (-(-size // LANES) * LANES) for _, size in spans]
+    return pl.pallas_call(
+        functools.partial(project_kernel, chips, spans),
+        grid_spec=pltpu.PrefetchScalarGridSpec(
+            num_scalar_prefetch=1,
+            grid=(4,),
+            in_specs=cell_specs(depth, tile) + [once(norms.shape), once(w.shape)],
+            out_specs=[row_tiles(tile, width) for width in widths]
+            + [lane_tiles(chips * rows_pad, tile)]
+            + [once((depth, width)) for width in widths],
+            scratch_shapes=[pltpu.VMEM((depth + 8, tile), F32)],
+        ),
+        out_shape=[jax.ShapeDtypeStruct((2 * half, width), BF16) for width in widths]
+        + [jax.ShapeDtypeStruct((chips * rows_pad, 2 * half), BF16)]
+        + [jax.ShapeDtypeStruct((depth, width), BF16) for width in widths],
+        compiler_params=pltpu.CompilerParams(vmem_limit_bytes=56 << 20),
+        cost_estimate=pl.CostEstimate(
+            flops=2 * 2 * half * depth * sum(widths), bytes_accessed=30 << 20, transcendentals=0
+        ),
+        name="project",
+    )(core, turned, other, norms, w)
+
+
+def cell_tile_low(core_ref, mine_ref, other_ref):
+    return jnp.where(pl.program_id(0) // 2 == core_ref[0], mine_ref[0], other_ref[...])
+
+
+def valid_lanes(len_ref, tile):
+    lane = lax.broadcasted_iota(jnp.int32, (1, tile), 1) + pl.program_id(0) * tile
+    return lane < len_ref[0]
+
+
+def hand_over_kernel(core_ref, first_ref, second_ref, first_out, second_out):
+    first_out[...] = first_ref[0]
+    second_out[...] = second_ref[0]
+
+
+def hand_over(core, first, second):
+    _, depth, half = first.shape
+    tile = half // 2
+    taken = pl.BlockSpec((1, depth, tile), lambda step, core: (1 - core[0], 0, step))
+    return pl.pallas_call(
+        hand_over_kernel,
+        grid_spec=pltpu.PrefetchScalarGridSpec(
+            num_scalar_prefetch=1,
+            grid=(2,),
+            in_specs=[taken, taken],
+            out_specs=[lane_tiles(depth, tile)] * 2,
+        ),
+        out_shape=[jax.ShapeDtypeStruct((depth, half), BF16)] * 2,
+        name="hand_over",
+    )(core, first, second)
+
+
+def take_over_kernel(core_ref, got_ref, whole_ref, out_ref):
+    out_ref[0] = got_ref[...]
+
+
+def take_over(core, whole, got):
+    depth, half = got.shape
+    tile = half // 2
+    return pl.pallas_call(
+        take_over_kernel,
+        grid_spec=pltpu.PrefetchScalarGridSpec(
+            num_scalar_prefetch=1,
+            grid=(2,),
+            in_specs=[lane_tiles(depth, tile), pl.BlockSpec(memory_space=pl.ANY)],
+            out_specs=pl.BlockSpec((1, depth, tile), lambda step, core: (1 - core[0], 0, step)),
+        ),
+        out_shape=jax.ShapeDtypeStruct(whole.shape, BF16),
+        input_output_aliases={2: 0},
+        name="take_over",
+    )(core, got, whole)
+
+
+def hidden_kernel(
+    chips,
+    core_ref,
+    len_ref,
+    mine_ref,
+    other_ref,
+    mine_grad_ref,
+    other_grad_ref,
+    first_ref,
+    second_ref,
+    w_ref,
+    norm_ref,
+    hidden_ref,
+    normed_ref,
+    grad_ref,
+    rows_ref,
+    o_rows_ref,
+    w_turned_ref,
+    scratch_ref,
+):
+    depth = w_ref.shape[0]
+    tile = mine_ref.shape[2]
+
+    @pl.when(pl.program_id(0) == 0)
+    def _():
+        scratch_ref[...] = jnp.zeros_like(scratch_ref)
+        w_turned_ref[...] = jnp.transpose(w_ref[...])
+
+    attended = jnp.concatenate([first_ref[...], second_ref[...]], axis=1)
+    value = cell_tile(core_ref, mine_ref, other_ref)
+    hidden = value + dot(w_turned_ref[...], attended[:, :depth], NT)
+    hidden_ref[...] = hidden
+    grad = cell_tile_low(core_ref, mine_grad_ref, other_grad_ref)
+    grad = jnp.where(valid_lanes(len_ref, tile), grad, jnp.zeros((), BF16))
+    grad_ref[:, :depth] = jnp.transpose(grad)
+    grad_ref[:, depth:] = jnp.zeros((tile, grad_ref.shape[1] - depth), BF16)
+    columns = jnp.transpose(norm_ref[...])
+    normed = norm_down(hidden, columns[:, 2:3], columns[:, 3:4])
+    spread_store(rows_ref, scratch_ref, normed, chips)
+    normed_ref[...] = jnp.transpose(normed.astype(BF16))
+    spread_store(o_rows_ref, scratch_ref, jnp.transpose(attended).astype(F32)[:depth], chips)
+
+
+def hidden_state(core, length, cell, grad_cell, attended, w_out, norms, chips, rows_pad):
+    _, depth, half = cell[0].shape
+    tile = half // 2
+    seq = 2 * half
+    spread = jax.ShapeDtypeStruct((chips * rows_pad, seq), BF16)
+    return pl.pallas_call(
+        functools.partial(hidden_kernel, chips),
+        grid_spec=pltpu.PrefetchScalarGridSpec(
+            num_scalar_prefetch=2,
+            grid=(4,),
+            in_specs=cell_specs(depth, tile) * 2
+            + [row_tiles(tile, part.shape[1]) for part in attended]
+            + [once(w_out.shape), once(norms.shape)],
+            out_specs=[lane_tiles(depth, tile), row_tiles(tile, depth), row_tiles(tile, WIDTH)]
+            + [lane_tiles(chips * rows_pad, tile)] * 2,
+            scratch_shapes=[pltpu.VMEM((depth, depth), BF16), pltpu.VMEM((depth + 8, tile), F32)],
+        ),
+        out_shape=[
+            jax.ShapeDtypeStruct((depth, seq), F32),
+            jax.ShapeDtypeStruct((seq, depth), BF16),
+            jax.ShapeDtypeStruct((seq, WIDTH), BF16),
+            spread,
+            spread,
+        ],
+        compiler_params=pltpu.CompilerParams(vmem_limit_bytes=56 << 20),
+        cost_estimate=pl.CostEstimate(
+            flops=2 * seq * depth * depth, bytes_accessed=24 << 20, transcendentals=0
+        ),
+        name="hidden_state",
+    )(core, length, *cell, *grad_cell, *attended, w_out, norms)
+
+
+GELU = (2.0 / math.pi) ** 0.5
+
+
+def hidden_units_kernel(
+    tile, normed_ref, grad_ref, up_ref, down_ref, activated_ref, grad_upward_ref
+):
+    seq, depth = normed_ref.shape
+
+    def begin(first):
+        rows = slice(first, first + tile)
+        return dot(normed_ref[rows], up_ref[...]), dot(grad_ref[rows, :depth], down_ref[...])
+
+    def middle(first, upward, grad_activated):
+        rows = slice(first, first + tile)
+        square = upward * upward
+        gate = 0.5 * jnp.tanh(upward * (GELU + (GELU * 0.044715) * square)) + 0.5
+        activated = upward * gate
+        slope = gate + 2.0 * activated * (1.0 - gate) * (GELU + (3 * GELU * 0.044715) * square)
+        activated_ref[:, rows] = jnp.transpose(activated.astype(BF16))
+        grad_upward_ref[rows] = (grad_activated * slope).astype(BF16)
+        return ()
+
+    staggered(list(range(0, seq, tile)), begin, middle, lambda first: None)
+
+
+def hidden_units(normed, grad, w_up, w_down_turned, tile=512, rows=256):
+    seq, depth = normed.shape
+    units = w_up.shape[1]
+    return pl.pallas_call(
+        functools.partial(hidden_units_kernel, rows),
+        grid=(pl.cdiv(units, tile),),
+        in_specs=[once(normed.shape), once(grad.shape)] + [lane_tiles(depth, tile)] * 2,
+        out_specs=[row_tiles(tile, seq), lane_tiles(seq, tile)],
+        out_shape=[
+            jax.ShapeDtypeStruct((units, seq), BF16),
+            jax.ShapeDtypeStruct((seq, units), BF16),
+        ],
+        compiler_params=pltpu.CompilerParams(vmem_limit_bytes=56 << 20),
+        cost_estimate=pl.CostEstimate(
+            flops=2 * 2 * seq * depth * units,
+            bytes_accessed=4 * depth * units + 4 * seq * units,
+            transcendentals=seq * units,
+        ),
+        name="hidden_units",
+    )(normed, grad, w_up, w_down_turned)
+
+
+def norm_down_back(grad_in, value, gain, gain_ref, bias_ref):
+    centred = value - jnp.mean(value, axis=0, keepdims=True)
+    inverse = lax.rsqrt(jnp.mean(centred * centred, axis=0, keepdims=True) + EPSILON)
+    normed = centred * inverse
+    product = grad_in * normed
+    for first in range(0, value.shape[1], LANES):
+        lanes = slice(first, first + LANES)
+        gain_ref[...] += product[:, lanes]
+        bias_ref[...] += grad_in[:, lanes]
+    scaled = grad_in * gain
+    return inverse * (
+        scaled
+        - jnp.mean(scaled, axis=0, keepdims=True)
+        - normed * jnp.mean(scaled * normed, axis=0, keepdims=True)
+    )
+
+
+def clear_first(*refs):
+    @pl.when(pl.program_id(0) == 0)
+    def _():
+        for ref in refs:
+            ref[...] = jnp.zeros_like(ref)
+
+
+def hidden_grad_kernel(
+    core_ref,
+    len_ref,
+    grad_up_ref,
+    w_up_ref,
+    hidden_ref,
+    mine_grad_ref,
+    other_grad_ref,
+    w_ref,
+    norm_ref,
+    grad_hidden_ref,
+    branch_ref,
+    first_ref,
+    second_ref,
+    gain_ref,
+    bias_ref,
+):
+    clear_first(gain_ref, bias_ref)
+    depth, tile = hidden_ref.shape
+    grad = cell_tile_low(core_ref, mine_grad_ref, other_grad_ref)
+    grad = jnp.where(valid_lanes(len_ref, tile), grad, jnp.zeros((), BF16)).astype(F32)
+    grad_normed = dot(w_up_ref[...], grad_up_ref[...], NT)
+    columns = jnp.transpose(norm_ref[...])
+    grad = grad + norm_down_back(grad_normed, hidden_ref[...], columns[:, 2:3], gain_ref, bias_ref)
+    grad_hidden_ref[...] = grad
+    branch = jnp.transpose(grad.astype(BF16))
+    branch_ref[:, :depth] = branch
+    branch_ref[:, depth:] = jnp.zeros((tile, branch_ref.shape[1] - depth), BF16)
+    width = first_ref.shape[1]
+    first_ref[...] = dot(branch, w_ref[:width], NT).astype(BF16)
+    second_ref[:, : depth - width] = dot(branch, w_ref[width:], NT).astype(BF16)
+    second_ref[:, depth - width :] = jnp.zeros((tile, second_ref.shape[1] - depth + width), BF16)
+
+
+def hidden_grad(core, length, grad_upward, w_up, hidden, grad_cell, w_out, norms, widths):
+    depth, seq = hidden.shape
+    tile = seq // 4
+    units = w_up.shape[1]
+    return pl.pallas_call(
+        hidden_grad_kernel,
+        grid_spec=pltpu.PrefetchScalarGridSpec(
+            num_scalar_prefetch=2,
+            grid=(4,),
+            in_specs=[row_tiles(tile, units), once(w_up.shape), lane_tiles(depth, tile)]
+            + cell_specs(depth, tile)
+            + [once(w_out.shape), once(norms.shape)],
+            out_specs=[lane_tiles(depth, tile), row_tiles(tile, WIDTH)]
+            + [row_tiles(tile, width) for width in widths]
+            + [once((depth, LANES))] * 2,
+        ),
+        out_shape=[
+            jax.ShapeDtypeStruct((depth, seq), F32),
+            jax.ShapeDtypeStruct((seq, WIDTH), BF16),
+        ]
+        + [jax.ShapeDtypeStruct((seq, width), BF16) for width in widths]
+        + [jax.ShapeDtypeStruct((depth, LANES), F32)] * 2,
+        compiler_params=pltpu.CompilerParams(vmem_limit_bytes=58 << 20),
+        cost_estimate=pl.CostEstimate(
+            flops=2 * seq * depth * (units + depth), bytes_accessed=40 << 20, transcendentals=0
+        ),
+        name="hidden_grad",
+    )(core, length, grad_upward, w_up, hidden, *grad_cell, w_out, norms)
+
+
+def halves(depth, tile):
+    return [
+        pl.BlockSpec((depth, tile), lambda step, core, *_: (0, jnp.minimum(step, 1))),
+        pl.BlockSpec((1, depth, tile), lambda step, core, *_: (core[0], 0, jnp.maximum(step - 2, 0))),
+    ]
+
+
+def half_place(step, core):
+    return jnp.where(step < 2, 2 - 2 * core + step, 2 * core + step - 2)
+
+
+def tokens_grad_kernel(
+    core_ref,
+    first_ref,
+    second_ref,
+    wide_first_ref,
+    wide_second_ref,
+    mine_ref,
+    other_ref,
+    grad_hidden_ref,
+    norm_ref,
+    sent_ref,
+    kept_ref,
+    gain_ref,
+    bias_ref,
+):
+    clear_first(gain_ref, bias_ref)
+    step = pl.program_id(0)
+    grad_normed = dot(wide_first_ref[...], first_ref[...], NT)
+    grad_normed += dot(wide_second_ref[...], second_ref[...], NT)
+    value = jnp.where(step < 2, other_ref[...], mine_ref[0]).astype(F32)
+    columns = jnp.transpose(norm_ref[...])
+    grad = norm_down_back(grad_normed, value, columns[:, 0:1], gain_ref, bias_ref)
+    grad = (grad_hidden_ref[...] + grad).astype(BF16)
+
+    @pl.when(step < 2)
+    def _():
+        sent_ref[...] = grad
+
+    @pl.when(step >= 2)
+    def _():
+        kept_ref[0] = grad
+
+
+def tokens_gradient(core, grads, wides, cell, grad_hidden, norms):
+    depth, seq = grad_hidden.shape
+    tile = seq // 4
+    return pl.pallas_call(
+        tokens_grad_kernel,
+        grid_spec=pltpu.PrefetchScalarGridSpec(
+            num_scalar_prefetch=1,
+            grid=(4,),
+            in_specs=[
+                pl.BlockSpec((tile, part.shape[1]), lambda step, core: (half_place(step, core[0]), 0))
+                for part in grads
+            ]
+            + [once(part.shape) for part in wides]
+            + [
+                pl.BlockSpec((1, depth, tile), lambda step, core: (core[0], 0, jnp.maximum(step - 2, 0))),
+                pl.BlockSpec((depth, tile), lambda step, core: (0, jnp.minimum(step, 1))),
+                pl.BlockSpec((depth, tile), lambda step, core: (0, half_place(step, core[0]))),
+                once(norms.shape),
+            ],
+            out_specs=halves(depth, tile) + [once((depth, LANES))] * 2,
+        ),
+        out_shape=[
+            jax.ShapeDtypeStruct((depth, seq // 2), BF16),
+            jax.ShapeDtypeStruct((2, depth, seq // 2), BF16),
+        ]
+        + [jax.ShapeDtypeStruct((depth, LANES), F32)] * 2,
+        compiler_params=pltpu.CompilerParams(vmem_limit_bytes=56 << 20),
+        cost_estimate=pl.CostEstimate(
+            flops=2 * seq * depth * 3 * WIDTH, bytes_accessed=30 << 20, transcendentals=0
+        ),
+        name="tokens_gradient",
+    )(core, *grads, *wides, *cell, grad_hidden, norms)
+
+
+def mixed_sent_kernel(core_ref, activated_ref, w_ref, hidden_ref, out_ref):
+    out_ref[...] = (hidden_ref[...] + dot(w_ref[...], activated_ref[...])).astype(BF16)
+
+
+def mixed_kept_kernel(core_ref, activated_ref, w_ref, hidden_ref, out_ref):
+    out_ref[0] = (hidden_ref[...] + dot(w_ref[...], activated_ref[...])).astype(BF16)
+
+
+def mixed_half(core, activated, w_down_turned, hidden, sent):
+    depth, seq = hidden.shape
+    units = activated.shape[0]
+    tile = seq // 4
+
+    def place(step, core):
+        return 0, (2 - 2 * core[0] if sent else 2 * core[0]) + step
+
+    if sent:
+        out_spec = lane_tiles(depth, tile)
+        out_shape = jax.ShapeDtypeStruct((depth, seq // 2), BF16)
+    else:
+        out_spec = pl.BlockSpec((1, depth, tile), lambda step, core: (core[0], 0, step))
+        out_shape = jax.ShapeDtypeStruct((2, depth, seq // 2), BF16)
+    return pl.pallas_call(
+        mixed_sent_kernel if sent else mixed_kept_kernel,
+        grid_spec=pltpu.PrefetchScalarGridSpec(
+            num_scalar_prefetch=1,
+            grid=(2,),
+            in_specs=[
+                pl.BlockSpec((units, tile), place),
+                once(w_down_turned.shape),
+                pl.BlockSpec((depth, tile), place),
+            ],
+            out_specs=out_spec,
+        ),
+        out_shape=out_shape,
+        compiler_params=pltpu.CompilerParams(vmem_limit_bytes=56 << 20),
+        cost_estimate=pl.CostEstimate(
+            flops=seq * depth * units, bytes_accessed=20 << 20, transcendentals=0
+        ),
+        name="mixed_half",
+    )(core, activated, w_down_turned, hidden)
 
 
 def swap_cores(value):
@@ -485,48 +974,102 @@
     return lax.ppermute(value, "cells", [(place, place ^ bit) for place in range(count)])
 
 
-def scatter_part(grads, axes):
-    place = lax.axis_index("cells")
-    count = grads.ndim - 2
-    kept = grads
-    got = None
-    for axis in axes:
-        bit = 1 << (count - 1 - axis)
-        side = (place // bit) % 2
-
-        def half(value, which):
-            return lax.dynamic_index_in_dim(value, which, axis, keepdims=True)
-
-        def both(which):
-            if got is None:
-                return half(kept, which)
-            return (half(kept, which).astype(F32) + half(got, which).astype(F32)).astype(BF16)
-
-        sent, stays = both(1 - side), both(side)
-        got = swap_chips(sent, bit)
-        kept = stays
-    total = kept.astype(F32) + got.astype(F32)
-    return total.reshape(total.shape[-2:])
-
-
-def chip_sum(features, theirs, ours):
-    sent = dot(features, theirs).astype(BF16)
-    return (dot(features, ours) + swap_cores(sent).astype(F32)).astype(BF16)
-
-
-def scatter(grads, rows, cuts):
-    count = lax.axis_size("cells")
-    bits = count.bit_length() - 1
-    shaped = grads.reshape((2,) * bits + (rows, grads.shape[1]))
-    first = [bits - 1 - turn for turn in range(bits)]
-    orders = [first, [first[1], first[0]] + first[2:], first[2:] + first[:2]]
-    begin = 0
-    parts = []
-    for size, order in zip(cuts, orders):
-        piece = lax.slice_in_dim(shaped, begin, begin + size, axis=bits + 1)
-        parts.append(scatter_part(piece, order))
-        begin += size
-    return jnp.concatenate(parts, axis=-1) if len(parts) > 1 else parts[0]
+class Scatter:
+    def __init__(self, grads, rows, cut=None, axis=-1, late=False):
+        bits = lax.axis_size("cells").bit_length() - 1
+        place = lax.axis_index("cells")
+        self.sides = [(place >> (bits - 1 - axis)) & 1 for axis in range(bits)]
+        self.bits = bits
+        grads = grads.reshape((2,) * bits + (rows, grads.shape[1]))
+        low, next_low = bits - 1, bits - 2
+        higher = list(range(next_low - 1, -1, -1))
+        if late:
+            self.parts = [(grads, higher + [low, next_low])]
+        else:
+            first, second = jnp.split(grads, [cut], axis=axis)
+            self.parts = [(first, [low, next_low]), (second, [next_low, low])]
+            self.rest = higher
+            self.axis = axis
+        self.sent = None
+        self.got = None
+
+    def _half(self, value, axis, other):
+        side = self.sides[axis]
+        return lax.dynamic_index_in_dim(value, 1 - side if other else side, axis, keepdims=True)
+
+    def send(self):
+        if self.got is not None:
+            added = []
+            for (kept, axes), got in zip(self.parts, self.got):
+                total = self._half(kept, axes[0], False).astype(F32) + got.astype(F32)
+                added.append((total.astype(BF16), axes[1:]))
+            if len(added) == 2 and not added[0][1]:
+                joined = jnp.concatenate([added[0][0], added[1][0]], axis=self.axis)
+                added = [(joined, self.rest)]
+            self.parts = added
+        self.sent = [self._half(kept, axes[0], True) for kept, axes in self.parts]
+        return self.sent
+
+    def move(self, sent):
+        self.got = [
+            swap_chips(value, 1 << (self.bits - 1 - axes[0]))
+            for value, (_, axes) in zip(sent, self.parts)
+        ]
+        return self.got
+
+    def arrived(self, got):
+        self.got = list(got)
+
+    def result(self):
+        ((kept, axes),) = self.parts
+        total = self._half(kept, axes[0], False).astype(F32) + self.got[0].astype(F32)
+        return total.reshape(total.shape[-2:])
+
+
+def begin_with(chain, *scatters):
+    sends = [item.send() for item in scatters]
+    flat = [value for group in sends for value in group]
+    chain, *flat = lax.optimization_barrier((chain, *flat))
+    for item, group in zip(scatters, sends):
+        item.move(flat[: len(group)])
+        flat = flat[len(group) :]
+    return chain
+
+
+def finish_with(chain, *scatters):
+    groups = [item.got for item in scatters]
+    flat = [value for group in groups for value in group]
+    chain, *flat = lax.optimization_barrier((chain, *flat))
+    for item, group in zip(scatters, groups):
+        item.arrived(flat[: len(group)])
+        flat = flat[len(group) :]
+    return chain
+
+
+class AllSum:
+    def __init__(self, value):
+        self.value = value
+        self.stage = 0
+        self.got = None
+
+    def send(self):
+        if self.got is not None:
+            self.value = self.value + self.got[0]
+        return [self.value]
+
+    def move(self, sent):
+        if self.stage == 0:
+            self.got = [swap_cores(sent[0])]
+        else:
+            self.got = [swap_chips(sent[0], 1 << (self.stage - 1))]
+        self.stage += 1
+        return self.got
+
+    def arrived(self, got):
+        self.got = list(got)
+
+    def result(self):
+        return self.value + self.got[0]
 
 
 def columns(value, first, size):
@@ -540,147 +1083,162 @@
     seq = 2 * row_count
     core = lax.axis_index("blk")
     chips = lax.axis_size("cells")
-
-    def to_cell(value):
-        mine = jnp.where(core == 0, value[:, 0], value[:, 1])
-        other = swap_cores(jnp.where(core == 0, value[:, 1], value[:, 0]))
-        return jnp.concatenate(
-            [jnp.where(core == 0, mine, other), jnp.where(core == 0, other, mine)], axis=0
-        )
-
-    def to_rows(value):
-        first, second = value[:row_count], value[row_count:]
-        mine = jnp.where(core == 0, first, second)
-        other = swap_cores(jnp.where(core == 0, second, first))
-        return jnp.stack(
-            [jnp.where(core == 0, mine, other), jnp.where(core == 0, other, mine)], axis=1
-        )
-
-    length = jnp.where(core == 0, lengths[0], lengths[1])
-    inputs = to_cell(tokens).astype(F32)
-    cell_cotangent = to_cell(cotangent)
-    w_wide = jnp.pad(w_qkv.reshape(D, 3, D), ((0, 0), (0, 0), (0, WIDTH - D))).reshape(D, 3 * WIDTH)
-    w_out_tall = jnp.pad(w_out, ((0, WIDTH - D), (0, 0)))
-
-    def norm_grads(grad_in, normed, inverse, gain_vec):
-        scaled = grad_in * gain_vec
-        grad_out = inverse * (
-            scaled
-            - jnp.mean(scaled, axis=-1, keepdims=True)
-            - normed * jnp.mean(scaled * normed, axis=-1, keepdims=True)
-        )
-        return grad_out, jnp.sum(grad_in * normed, axis=0), jnp.sum(grad_in, axis=0)
-
-    normed_one, inverse_one, pre_one = norm_forward(inputs, attn_gain, attn_bias)
-    normed_low = pre_one.astype(BF16)
-    qkv = dot(normed_low, w_wide).astype(BF16)
-    attended, lse = attention_forward(qkv, length.reshape(1))
-    hidden = inputs + dot(attended, w_out_tall)
-    normed_two, inverse_two, pre_two = norm_forward(hidden, mlp_gain, mlp_bias)
-    normed_mlp = pre_two.astype(BF16)
-    upward = dot(normed_mlp, w_up)
-    activated_full, gelu_back = jax.vjp(
-        lambda value_in: jax.nn.gelu(value_in, approximate=True), upward
-    )
-    activated = activated_full.astype(BF16)
-    mixed = (hidden + dot(activated, w_down)).astype(BF16)
-    valid = jnp.arange(seq, dtype=jnp.int32)[:, None] < length
-    grad_low = jnp.where(valid, cell_cotangent, jnp.zeros((), BF16))
-    grad_out = grad_low.astype(F32)
-
-    rows_pad = -(-(D // chips) // 8) * 8
-    place = jnp.arange(chips * rows_pad, dtype=jnp.int32)
-    source = jnp.where(place % rows_pad < D // chips, place // rows_pad * (D // chips) + place % rows_pad, -1)
-    spread = (source[:, None] == jnp.arange(D, dtype=jnp.int32)[None, :]).astype(BF16)
-
-    def spread_rows(value):
-        return dot(spread, value, NT).astype(BF16)
+    rows = D // chips
+    rows_pad = -(-rows // 8) * 8
+
+    def tie(*values):
+        return lax.optimization_barrier(values)
+
+    def pick(first, second):
+        return jnp.where(core == 0, first, second)
+
+    core_index = core.reshape(1).astype(jnp.int32)
+    length = pick(lengths[0], lengths[1])
+    length = length.reshape(1)
+    turned, turned_cotangent = tokens.transpose(1, 2, 0), cotangent.transpose(1, 2, 0)
+    sent, sent_cotangent = hand_over(core_index, turned, turned_cotangent)
+    cell = (turned, swap_cores(sent))
+    grad_cell = (turned_cotangent, swap_cores(sent_cotangent))
+    norms = jnp.stack([attn_gain, attn_bias, mlp_gain, mlp_bias] * 2)
+    w_down_turned = w_down.T
+
+    big, small = 16, HEADS - 16
+    spans = ((0, big * HD), (big * HD, small * HD))
+    qkv_big, qkv_small, one_rows, wide_big, wide_small = project(
+        core_index, *cell, norms, w_qkv, spans, chips, rows_pad
+    )
+    attended_big, lse_big = attention_forward(qkv_big, length, big)
+    attended_small, lse_small = attention_forward(qkv_small, length, small)
+    hidden, normed_mlp, grad_low, mlp_rows, attended_rows = hidden_state(
+        core_index, length, cell, grad_cell, (attended_big, attended_small), w_out, norms, chips, rows_pad
+    )
+    activated, grad_upward = hidden_units(normed_mlp, grad_low, w_up, w_down_turned)
 
     half = D // 2
-    down_sent = lax.dot_general(activated, columns(grad_low, (1 - core) * half, half), TN, preferred_element_type=F32)
-    down_kept = lax.dot_general(activated, columns(grad_low, core * half, half), TN, preferred_element_type=F32)
-    down_sum = (down_kept + swap_cores(down_sent.astype(BF16)).astype(F32)).astype(BF16)
-    w_down_share = scatter(down_sum, w_down.shape[0] // chips, (256, 256, half - 512))
-
-    grad_act = dot(grad_low, w_down, NT)
-    grad_upward = gelu_back(grad_act)[0].astype(BF16)
+    window = -(-half // LANES) * LANES
+    starts = (0, WIDTH - window)
+    ours, theirs = pick(*starts), pick(*starts[::-1])
     up_all = w_up.shape[1]
     up_window = -(-up_all // 2 // LANES) * LANES
     up_starts = (0, up_all - up_window)
-    up_start = jnp.where(core == 0, up_starts[0], up_starts[1])
-    up_other = jnp.where(core == 0, up_starts[1], up_starts[0])
-    up_sum = chip_sum(
-        spread_rows(normed_mlp),
-        columns(grad_upward, up_other, up_window),
-        columns(grad_upward, up_start, up_window),
-    )
-    up_share = scatter(up_sum, rows_pad, (896, 896, up_window - 1792))
-
-    grad_normed_two = dot(grad_upward, w_up, NT)
-    grad_hidden_ln, mlp_gain_grad, mlp_bias_grad = norm_grads(
-        grad_normed_two, normed_two, inverse_two, mlp_gain
-    )
-    grad_hidden = grad_out + grad_hidden_ln
-    grad_branch = grad_hidden.astype(BF16)
-    out_sum = chip_sum(
-        spread_rows(attended[:, :D]),
-        columns(grad_branch, (1 - core) * half, half),
-        columns(grad_branch, core * half, half),
-    )
-    w_out_share = scatter(out_sum, rows_pad, (half,))
-
-    grad_attended = dot(grad_branch, w_out_tall, NT).astype(BF16)
-    grad_qkv = attention_backward(qkv, attended, grad_attended, lse, length.reshape(1))
-    qkv_window = 14 * LANES
-    qkv_starts = (0, 3 * WIDTH - qkv_window)
-    qkv_start = jnp.where(core == 0, qkv_starts[0], qkv_starts[1])
-    qkv_other = jnp.where(core == 0, qkv_starts[1], qkv_starts[0])
-    qkv_sum = chip_sum(
-        spread_rows(normed_low),
-        columns(grad_qkv, qkv_other, qkv_window),
-        columns(grad_qkv, qkv_start, qkv_window),
-    )
-    qkv_share = scatter(qkv_sum, rows_pad, (640, 640, qkv_window - 1280))
-
-    grad_normed_one = dot(grad_qkv, w_wide, NT)
-    grad_inputs_ln, attn_gain_grad, attn_bias_grad = norm_grads(
-        grad_normed_one, normed_one, inverse_one, attn_gain
-    )
-    tokens_grad = (grad_hidden + grad_inputs_ln).astype(BF16)
-    norm_sums = lax.psum(
-        (attn_gain_grad, attn_bias_grad, mlp_gain_grad, mlp_bias_grad), ("blk", "cells")
-    )
-
-    rows = D // chips
-    first_share = jnp.concatenate(
-        [qkv_share[:rows, :D], qkv_share[:rows, WIDTH : WIDTH + half]], axis=1
-    )
-    shift = WIDTH + half - qkv_starts[1]
-    second_share = jnp.concatenate(
-        [
-            qkv_share[:rows, shift : shift + half],
-            qkv_share[:rows, 2 * WIDTH - qkv_starts[1] : 2 * WIDTH - qkv_starts[1] + D],
-        ],
-        axis=1,
-    )
-    w_qkv_share = jnp.where(core == 0, first_share, second_share)
-    up_shift = up_all // 2 - up_starts[1]
-    w_up_share = jnp.where(
-        core == 0,
-        up_share[:rows, : up_all // 2],
-        up_share[:rows, up_shift : up_shift + up_all // 2],
-    )
+    up_ours, up_theirs = pick(*up_starts), pick(*up_starts[::-1])
+    big_width, small_width = qkv_big.shape[1] // 3, qkv_small.shape[1] // 3
+    big_window = big_width + -(-half // LANES) * LANES
+    big_starts = (0, 3 * big_width - big_window)
+    big_ours, big_theirs = pick(*big_starts), pick(*big_starts[::-1])
+    small_window = 2 * small_width
+    small_starts = (0, small_width)
+    small_ours, small_theirs = pick(*small_starts), pick(*small_starts[::-1])
+
+    down_sent = dot(activated, columns(grad_low, theirs, window)).astype(BF16)
+    down_got = swap_cores(down_sent)
+    up_sent = dot(mlp_rows, columns(grad_upward, up_theirs, up_window)).astype(BF16)
+    up_got = swap_cores(up_sent)
+    grad_low_d, up_sent = tie(grad_low, up_sent)
+    down_sum = dot(activated, columns(grad_low_d, ours, window)) + down_got.astype(F32)
+    down_rows = w_down.shape[0] // chips
+    down = Scatter(down_sum.astype(BF16), down_rows, down_rows // 16 * 8, axis=-2)
+    grad_upward_d = begin_with(grad_upward, down)
+    up_sum = dot(mlp_rows, columns(grad_upward_d, up_ours, up_window)) + up_got.astype(F32)
+    up_sum = up_sum.astype(BF16)
+
+    grad_hidden, grad_branch, grad_attended_big, grad_attended_small, *mlp_norms = hidden_grad(
+        core_index, length, grad_upward_d, w_up, hidden, grad_cell, w_out, norms, (big_width, small_width)
+    )
+    grad_branch, up_sum = tie(grad_branch, up_sum)
+    grad_branch = finish_with(grad_branch, down)
+    up = Scatter(up_sum, rows_pad, up_window // 2)
+    grad_branch = begin_with(grad_branch, down, up)
+    out_sent = dot(attended_rows, columns(grad_branch, theirs, window)).astype(BF16)
+    out_got = swap_cores(out_sent)
+    out_sum = dot(attended_rows, columns(grad_branch, ours, window)) + out_got.astype(F32)
+    out = Scatter(out_sum.astype(BF16), rows_pad, late=True)
+    grad_attended_big, grad_attended_small = begin_with((grad_attended_big, grad_attended_small), out)
+
+    grad_big = attention_backward(
+        qkv_big, attended_big, grad_attended_big, lse_big, length
+    )
+    grad_big = finish_with(grad_big, down, up, out)
+    big_sent = dot(one_rows, columns(grad_big, big_theirs, big_window)).astype(BF16)
+    big_got = swap_cores(big_sent)
+    grad_big, big_sent = tie(grad_big, big_sent)
+    grad_big = begin_with(grad_big, down, up, out)
+    big_sum = dot(one_rows, columns(grad_big, big_ours, big_window)) + big_got.astype(F32)
+    whole_big = Scatter(big_sum.astype(BF16), rows_pad, big_window // 2)
+    qkv_small = begin_with(qkv_small, whole_big)
+    grad_small = attention_backward(
+        qkv_small, attended_small, grad_attended_small, lse_small, length
+    )
+    small_sent = dot(one_rows, columns(grad_small, small_theirs, small_window)).astype(BF16)
+    small_got = swap_cores(small_sent)
+    grad_small, grad_big, small_sent = tie(grad_small, grad_big, small_sent)
+    grad_small, small_got, grad_big = tie(grad_small, small_got, grad_big)
+    small_sum = dot(one_rows, columns(grad_small, small_ours, small_window)) + small_got.astype(F32)
+    whole_small = Scatter(small_sum.astype(BF16), rows_pad, small_window // 2)
+    grad_big = finish_with(grad_big, down, up, out)
+    grad_big = begin_with(grad_big, whole_small, down, up, out)
+    tokens_sent, tokens_kept, *attn_norms = tokens_gradient(
+        core_index, (grad_big, grad_small), (wide_big, wide_small), cell, grad_hidden, norms
+    )
+    tokens_got = swap_cores(tokens_sent)
+    norm_sums = AllSum(jnp.stack([jnp.sum(part, axis=1) for part in (*attn_norms, *mlp_norms)] * 2))
+    activated, tokens_sent = tie(activated, tokens_sent)
+    activated = finish_with(activated, whole_big, whole_small)
+    activated = begin_with(activated, norm_sums, whole_big, whole_small)
+    mixed_sent = mixed_half(core_index, activated, w_down_turned, hidden, True)
+    mixed_got = swap_cores(mixed_sent)
+    activated, mixed_sent = tie(activated, mixed_sent)
+    activated = finish_with(activated, up, out, norm_sums, whole_big, whole_small)
+    activated = begin_with(activated, norm_sums, whole_big, whole_small, up, out)
+    mixed_kept = mixed_half(core_index, activated, w_down_turned, hidden, False)
+    mixed_kept = finish_with(mixed_kept, norm_sums, whole_big, whole_small)
+    mixed_kept = begin_with(mixed_kept, norm_sums, whole_big, whole_small)
+    w_down_share, up_share, w_out_share = down.result(), up.result(), out.result()
+    tokens_grad = take_over(core_index, tokens_kept, tokens_got)
+    mixed = take_over(core_index, mixed_kept, mixed_got)
+    mixed = finish_with(mixed, norm_sums)
+    mixed = begin_with(mixed, norm_sums)
+    big_share, small_share = whole_big.result(), whole_small.result()
+    mixed = finish_with(mixed, norm_sums)
+    mixed = begin_with(mixed, norm_sums)
+    sums = norm_sums.result()
+
+    shift = big_width + half - big_starts[1]
+    w_qkv_share = pick(
+        jnp.concatenate(
+            [
+                big_share[:rows, :big_width],
+                small_share[:rows, : small * HD],
+                big_share[:rows, big_width : big_width + half],
+            ],
+            axis=1,
+        ),
+        jnp.concatenate(
+            [
+                big_share[:rows, shift : 2 * big_width - big_starts[1]],
+                small_share[:rows, : small * HD],
+                big_share[:rows, 2 * big_width - big_starts[1] :],
+                small_share[:rows, small_width : small_width + small * HD],
+            ],
+            axis=1,
+        ),
+    )
+
+    def own_columns(share, starts, all_columns):
+        second = all_columns // 2 - starts[1]
+        return pick(share[:, : all_columns // 2], share[:, second : second + all_columns // 2])
+
     return (
-        to_rows(mixed),
-        to_rows(tokens_grad),
-        norm_sums[0],
-        norm_sums[1],
+        mixed.transpose(2, 0, 1),
+        tokens_grad.transpose(2, 0, 1),
+        sums[0],
+        sums[1],
         w_qkv_share,
-        w_out_share[:rows],
-        norm_sums[2],
-        norm_sums[3],
-        w_up_share,
-        w_down_share,
+        own_columns(w_out_share[:rows], starts, D),
+        sums[2],
+        sums[3],
+        own_columns(up_share[:rows], up_starts, up_all),
+        own_columns(w_down_share, starts, D),
     )
 
 

time: 600 us -> 483 us (0.81)
  Pallas kernels: 81.6 us -> 237 us
  matrix products: 203 us -> 73 us
  waiting for transfers between devices: 118 us -> 50.5 us
  blocking collectives: 44.8 us -> 0 us
  local copies, waits for them, and re-layouts: 50.6 us -> 36 us
  starting transfers between devices: 48.8 us -> 40.7 us
  other arithmetic: 41.7 us -> 34.1 us
    pallas_call x0 -> x10, Pallas kernels: none -> 152 us  [the longest x1 34.8 us: hidden_units(): pl.pallas_call(functools.partial(hidden_units_kernel, rows), grid=(pl.cdi...]
    dot_general x17 -> x10, matrix products: 187 us -> 73 us  [dot(): return lax.dot_general(left, right, dims, preferred_element_type=F32)]
    ppermute x40 -> x32, waiting for transfers between devices: 118 us -> 50.5 us  [swap_chips(): lax.ppermute(value, 'cells', [(place, place ^ bit) for place in range(cou...]
    psum x1 -> x0, blocking collectives: 44.8 us -> none  [cell_split(): lax.psum((attn_gain_grad, attn_bias_grad, mlp_gain_grad, mlp_bias_grad),...]
    dot_general x2 -> x0, matrix products: 16.2 us -> none  [the longest x1 8.88 us: cell_split(): lax.dot_general(activated, columns(grad_low, core * half, half), TN, pref...]
    unnamed x93 -> x98, local copies, waits for them, and re-layouts: 19.6 us -> 8.49 us
    convert_element_type x2 -> x0, local copies, waits for them, and re-layouts: 11.1 us -> none  [the longest x1 8.37 us: cell_split(): (down_kept + swap_cores(down_sent.astype(BF16)).astype(F32)).astype(BF16)]
    dynamic_slice x12 -> x23, local copies, waits for them, and re-layouts: 7.51 us -> 16.4 us  [_half(): lax.dynamic_index_in_dim(value, 1 - side if other else side, axis, keepdi...]
  transfers between devices with their start and end apart: 48 -> 42, of which waited for: 20 -> 9; matrix products, arithmetic and copies ran while one was open for 38% -> 19% of each run, Pallas kernels for 14% -> 37%
where the time goes in v2:
time: 483 us; the launch traced here: 474 us
  Pallas kernels  237 us (49%)
  matrix products  73 us (15%)
  waiting for transfers between devices  50.5 us (10%)
  starting transfers between devices  40.7 us (8%)
  local copies, waits for them, and re-layouts  36 us (7%)
  other arithmetic  34.1 us (7%)
    dot_general x10, matrix products, dot(): return lax.dot_general(left, right, dims, preferred_element_type=F32)  73 us
    pallas_call x2, Pallas kernels, attention_backward(): pl.pallas_call(functools.partial(attention_backward_kernel, per), grid_sp...  52.4 us
    ppermute x32, waiting for transfers between devices, swap_chips(): lax.ppermute(value, 'cells', [(place, place ^ bit) for place in range(cou...  50.5 us
    ppermute x32, starting transfers between devices, swap_chips(): lax.ppermute(value, 'cells', [(place, place ^ bit) for place in range(cou...  39.2 us
    pallas_call x1, Pallas kernels, hidden_units(): pl.pallas_call(functools.partial(hidden_units_kernel, rows), grid=(pl.cdi...  34.8 us
    pallas_call x2, Pallas kernels, attention_forward(): pl.pallas_call(functools.partial(attention_forward_kernel, per), grid_spe...  32.4 us
    pallas_call x1, Pallas kernels, hidden_grad(): pl.pallas_call(hidden_grad_kernel, grid_spec=pltpu.PrefetchScalarGridSpec...  31.5 us
    pallas_call x1, Pallas kernels, project(): pl.pallas_call(functools.partial(project_kernel, chips, spans), grid_spec...  23.2 us
  transfers between devices with their start and end apart: 42, of which 9 were waited for; matrix products, arithmetic and copies ran while one was open for 19% of the time, Pallas kernels for 37%

profile of v2, /device:TPU:0, one launch (start us, length us, event | category | flops | bytes accessed | tf_op | source)
XLA Modules:
  0.0 474.3 jit_solution(11501254821464577021)
XLA Ops:
  0.7 2.7 hand_over.1
  7.6 23.2 %project.1 = (bf16[1024,2688]{1,0:T(8,128)(2,1)}, bf16[1024,768]{1,0:T(8,128)(2,1)}, bf16[1152,1024]{1,0:T(8,128)(2,1)}, bf16[1120,2688]{1,0:T(8,128)(2,1)}, bf16[1120,768]{1,0:T(8,128)(2,1)}) custom-call(s32[1]{0:T(128)} %bitcast.core_ref, bf16[2,1120,512]{2,1,0:T(8,128)(2,1)} %bitcast.41, bf16[1120,512]{1,0:T(8,128)(2,1)} %copy-done.31, ...), custom_call_target="tpu_custom_call" | custom-call | flops 7927234560 | bytes 31457280 | tf_op jit(solution)/shard_map/project/pallas_call | solution.py:563
  30.8 7.4 %attention_forward.3 = (bf16[1024,256]{1,0:T(8,128)(2,1)}, f32[4,8,1024]{2,1,0:T(8,128)}) custom-call(s32[1]{0:T(128)} %bitcast.3.len_ref, bf16[1024,768]{1,0:T(8,128)(2,1)} %get-tuple-element.171.q_ref.k_ref.v_ref, bf16[1024,768]{1,0:T(8,128)(2,1)} %get-tuple-element.171.q_ref.k_ref.v_ref, bf16[1024,768]{1,0:T(8,128)(2,1)} %get-tuple-element.171.q_ref.k_ref.v_ref), custom_call_target="tpu_custom_call" | custom-call | flops 2684354560 | bytes 2097152 | tf_op jit(solution)/shard_map/attention_forward/pallas_call | solution.py:429
  38.1 25.0 %attention_forward.2 = (bf16[1024,896]{1,0:T(8,128)(2,1)}, f32[16,8,1024]{2,1,0:T(8,128)}) custom-call(s32[1]{0:T(128)} %bitcast.3.len_ref, bf16[1024,2688]{1,0:T(8,128)(2,1)} %get-tuple-element.131.q_ref.k_ref.v_ref, bf16[1024,2688]{1,0:T(8,128)(2,1)} %get-tuple-element.131.q_ref.k_ref.v_ref, bf16[1024,2688]{1,0:T(8,128)(2,1)} %get-tuple-element.131.q_ref.k_ref.v_ref), custom_call_target="tpu_custom_call" | custom-call | flops 10737418240 | bytes 7340032 | tf_op jit(solution)/shard_map/attention_forward/pallas_call | solution.py:429
  64.2 13.9 %hidden_state.1 = (f32[1120,1024]{1,0:T(8,128)}, bf16[1024,1120]{1,0:T(8,128)(2,1)}, bf16[1024,1152]{1,0:T(8,128)(2,1)}, bf16[1152,1024]{1,0:T(8,128)(2,1)}, bf16[1152,1024]{1,0:T(8,128)(2,1)}) custom-call(s32[1]{0:T(128)} %bitcast.core_ref, s32[1]{0:T(128)} %bitcast.3.len_ref, bf16[2,1120,512]{2,1,0:T(8,128)(2,1)} %bitcast.42, ...), custom_call_target="tpu_custom_call" | custom-call | flops 2569011200 | bytes 25165824 | tf_op jit(solution)/shard_map/hidden_state/pallas_call | solution.py:685
  78.2 34.8 %hidden_units.1 = (bf16[4480,1024]{1,0:T(8,128)(2,1)}, bf16[1024,4480]{1,0:T(8,128)(2,1)}) custom-call(bf16[1024,1120]{1,0:T(8,128)(2,1)} %get-tuple-element.135.normed_ref, bf16[1024,1152]{1,0:T(8,128)(2,1)} %get-tuple-element.141.grad_ref, bf16[1120,4480]{1,0:T(8,128)(2,1)} %w_up_ref.1, bf16[1120,4480]{1,0:T(8,128)(2,1)} %bitcast.34), custom_call_target="tpu_custom_call" | custom-call | flops 20552089600 | bytes 38420480 | tf_op jit(solution)/shard_map/hidden_units/pallas_call | solution.py:740
  113.0 12.5 %convolution_convert_fusion.1 = bf16[4480,640]{1,0:T(8,128)(2,1)} fusion(bf16[4480,1024]{1,0:T(8,128)(2,1)} %get-tuple-element.224.activated_ref, bf16[1024,1152]{1,0:T(8,128)(2,1)S(1)} %copy-done.44, s32[]{:T(128)S(6)} %select_n.174), kind=kOutput, calls=%fused_computation.5 | convolution fusion | flops 5874892800 | bytes 16220164 | tf_op jit(solution)/shard_map/dot_general | solution.py:262
  126.0 9.7 %convolution_convert_fusion = bf16[1152,2304]{1,0:T(8,128)(2,1)} fusion(bf16[1152,1024]{1,0:T(8,128)(2,1)S(1)} %copy-done.42, bf16[1024,4480]{1,0:T(8,128)(2,1)} %get-tuple-element.142.grad_up_ref, s32[]{:T(128)S(6)} %select_n.172), kind=kOutput, calls=%fused_computation.3 | convolution fusion | flops 5438472192 | bytes 12386308 | tf_op jit(solution)/shard_map/dot_general | solution.py:262
  135.7 11.6 %add_convert_fusion = bf16[4480,640]{1,0:T(8,128)(2,1)S(1)} fusion(bf16[4480,640]{1,0:T(8,128)(2,1)} %collective-permute-done.2, bf16[4480,1024]{1,0:T(8,128)(2,1)} %get-tuple-element.224.activated_ref, bf16[1024,1152]{1,0:T(8,128)(2,1)} %get-tuple-element.141.grad_ref, s32[]{:T(128)S(6)} %select_n.173), kind=kOutput, calls=%fused_computation.1 | convolution fusion | flops 5880627200 | bytes 21954564 | tf_op jit(solution)/shard_map/dot_general | solution.py:262
  150.3 3.0 collective-permute-start.5
  154.8 10.6 %fusion = bf16[1152,2304]{1,0:T(8,128)(2,1)} fusion(bf16[1152,1024]{1,0:T(8,128)(2,1)S(1)} %copy-done.43, bf16[1152,2304]{1,0:T(8,128)(2,1)} %collective-permute-done.3, bf16[1024,4480]{1,0:T(8,128)(2,1)} %get-tuple-element.142.grad_up_ref, s32[]{:T(128)S(6)} %select_n.177), kind=kOutput, calls=%fused_computation.2 | convolution fusion | flops 5443780608 | bytes 17694724 | tf_op jit(solution)/shard_map/dot_general | solution.py:262
  165.4 31.5 %hidden_grad.1 = (f32[1120,1024]{1,0:T(8,128)}, bf16[1024,1152]{1,0:T(8,128)(2,1)}, bf16[1024,896]{1,0:T(8,128)(2,1)}, bf16[1024,256]{1,0:T(8,128)(2,1)}, f32[1120,128]{1,0:T(8,128)}, /*index=5*/f32[1120,128]{1,0:T(8,128)}) custom-call(s32[1]{0:T(128)} %bitcast.core_ref, s32[1]{0:T(128)} %bitcast.3.len_ref, ...), custom_call_target="tpu_custom_call" | custom-call | flops 12845056000 | bytes 41943040 | tf_op jit(solution)/shard_map/hidden_grad/pallas_call | solution.py:821
  196.9 3.0 fusion.32
  201.2 1.7 constant_dynamic-slice_fusion.19
  203.1 1.7 add_convert_fusion.1
  205.9 1.8 add_convert_fusion.2
  208.8 2.0 convolution_convert_fusion.3
  211.6 1.9 collective-permute-start.8
  215.1 4.5 fusion.4
  222.1 40.7 %attention_backward.2.first_ref = bf16[1024,2688]{1,0:T(8,128)(2,1)} custom-call(s32[1]{0:T(128)} %bitcast.3.len_ref, bf16[1024,2688]{1,0:T(8,128)(2,1)} %get-tuple-element.131.q_ref.k_ref.v_ref, bf16[1024,2688]{1,0:T(8,128)(2,1)} %get-tuple-element.131.q_ref.k_ref.v_ref, bf16[1024,2688]{1,0:T(8,128)(2,1)} %get-tuple-element.131.q_ref.k_ref.v_ref, ...), custom_call_target="tpu_custom_call" | custom-call | flops 26843545600 | bytes 14680064 | tf_op jit(solution)/shard_map/attention_backward/pallas_call | solution.py:457
  262.8 9.2 %convolution_convert_fusion.2 = bf16[1152,1536]{1,0:T(8,128)(2,1)} fusion(bf16[1152,1024]{1,0:T(8,128)(2,1)} %get-tuple-element.138, bf16[1024,2688]{1,0:T(8,128)(2,1)} %attention_backward.2.first_ref, s32[]{:T(128)S(6)} %select_n.181), kind=kOutput, calls=%fused_computation.6 | convolution fusion | flops 3625648128 | bytes 9043972 | tf_op jit(solution)/shard_map/dot_general | solution.py:262
  276.5 1.6 add_convert_fusion.8
  285.1 6.4 %fusion.1 = bf16[1152,1536]{1,0:T(8,128)(2,1)S(1)} fusion(bf16[1152,1024]{1,0:T(8,128)(2,1)S(1)} %copy-done.45, bf16[1152,1536]{1,0:T(8,128)(2,1)} %collective-permute-done.12, bf16[1024,2688]{1,0:T(8,128)(2,1)} %attention_backward.2.first_ref, s32[]{:T(128)S(6)} %select_n.184), kind=kOutput, calls=%fused_computation.7 | convolution fusion | flops 3629187072 | bytes 12582916 | tf_op jit(solution)/shard_map/dot_general | solution.py:262
  293.8 11.7 %attention_backward.3.second_ref = bf16[1024,768]{1,0:T(8,128)(2,1)} custom-call(s32[1]{0:T(128)} %bitcast.3.len_ref, bf16[1024,768]{1,0:T(8,128)(2,1)} %get-tuple-element.171.q_ref.k_ref.v_ref, bf16[1024,768]{1,0:T(8,128)(2,1)} %get-tuple-element.171.q_ref.k_ref.v_ref, bf16[1024,768]{1,0:T(8,128)(2,1)} %get-tuple-element.171.q_ref.k_ref.v_ref, ...), custom_call_target="tpu_custom_call" | custom-call | flops 6710886400 | bytes 4194304 | tf_op jit(solution)/shard_map/attention_backward/pallas_call | solution.py:457
  305.5 3.7 convolution_convert_fusion.4
  310.7 3.0 collective-permute-start.17
  315.1 1.9 reduce_sum.39
  319.2 14.6 %collective-permute-done.17 = bf16[1,1,2,2,72,640]{5,4,3,2,1,0:T(8,128)(2,1)} collective-permute-done((bf16[1,1,2,2,72,640]{5,4,3,2,1,0:T(8,128)(2,1)}, bf16[1,1,2,2,72,640]{5,4,3,2,1,0:T(8,128)(2,1)}, u32[]{:S(2)}, u32[]{:S(2)}) %collective-permute-start.17) | collective-permute-done | bytes 368672 | tf_op jit(solution)/shard_map/ppermute | solution.py:974
  337.3 1.7 add_convert_fusion.13
  340.7 2.9 fusion.7
  348.8 1.9 collective-permute-start.41
  351.1 1.6 collective-permute-start.21
  352.8 18.4 %tokens_gradient.1 = (bf16[1120,512]{1,0:T(8,128)(2,1)}, bf16[2,1120,512]{2,1,0:T(8,128)(2,1)}, f32[1120,128]{1,0:T(8,128)}, f32[1120,128]{1,0:T(8,128)}) custom-call(s32[1]{0:T(128)} %bitcast.core_ref, bf16[1024,2688]{1,0:T(8,128)(2,1)} %attention_backward.2.first_ref, bf16[1024,768]{1,0:T(8,128)(2,1)} %attention_backward.3.second_ref, ...), custom_call_target="tpu_custom_call" | custom-call | flops 7927234560 | bytes 31457280 | tf_op jit(solution)/shard_map/tokens_gradient/pallas_call | solution.py:894
  371.2 1.9 reduce_sum.36
  374.4 1.9 reduce_sum.37
  387.7 11.5 %mixed_half.2 = bf16[1120,512]{1,0:T(8,128)(2,1)} custom-call(s32[1]{0:T(128)} %bitcast.core_ref, bf16[4480,1024]{1,0:T(8,128)(2,1)} %get-tuple-element.224.activated_ref, bf16[1120,4480]{1,0:T(8,128)(2,1)} %bitcast.35, f32[1120,1024]{1,0:T(8,128)} %get-tuple-element.143.hidden_ref), custom_call_target="tpu_custom_call" | custom-call | flops 5138022400 | bytes 20971520 | tf_op jit(solution)/shard_map/mixed_half/pallas_call | solution.py:947
  405.7 6.8 %collective-permute-done.28 = bf16[2,2,1,1,72,256]{5,4,3,2,1,0:T(8,128)(2,1)S(1)} collective-permute-done((bf16[2,2,1,1,72,256]{5,4,3,2,1,0:T(8,128)(2,1)S(1)}, bf16[2,2,1,1,72,256]{5,4,3,2,1,0:T(8,128)(2,1)S(1)}, u32[]{:S(2)}, u32[]{:S(2)}) %collective-permute-start.28) | collective-permute-done | bytes 147488 | tf_op jit(solution)/shard_map/ppermute | solution.py:974
  413.8 2.6 collective-permute-start.40
  417.9 11.6 %mixed_half.3.whole_ref = bf16[2,1120,512]{2,1,0:T(8,128)(2,1)} custom-call(s32[1]{0:T(128)} %bitcast.core_ref, bf16[4480,1024]{1,0:T(8,128)(2,1)} %get-tuple-element.224.activated_ref, bf16[1120,4480]{1,0:T(8,128)(2,1)} %bitcast.36, f32[1120,1024]{1,0:T(8,128)} %get-tuple-element.143.hidden_ref), custom_call_target="tpu_custom_call" | custom-call | flops 5138022400 | bytes 20971520 | tf_op jit(solution)/shard_map/mixed_half/pallas_call | solution.py:947
  429.9 1.7 collective-permute-start.32
  433.0 3.3 collective-permute-done.30
  436.3 8.4 %collective-permute-done.32 = bf16[2,1,1,1,72,512]{5,4,3,2,1,0:T(8,128)(2,1)S(1)} collective-permute-done((bf16[2,1,1,1,72,512]{5,4,3,2,1,0:T(8,128)(2,1)S(1)}, bf16[2,1,1,1,72,512]{5,4,3,2,1,0:T(8,128)(2,1)S(1)}, u32[]{:S(2)}, u32[]{:S(2)}) %collective-permute-start.32) | collective-permute-done | bytes 147488 | tf_op jit(solution)/shard_map/ppermute | solution.py:974
  446.5 2.1 take_over.3
  448.6 2.5 collective-permute-start.37
  452.5 8.8 %collective-permute-done.37 = bf16[1,1,1,1,72,1536]{5,4,3,2,1,0:T(8,128)(2,1)S(1)} collective-permute-done((bf16[1,1,1,1,72,1536]{5,4,3,2,1,0:T(8,128)(2,1)S(1)}, bf16[1,1,1,1,72,1536]{5,4,3,2,1,0:T(8,128)(2,1)S(1)}, u32[]{:S(2)}, u32[]{:S(2)}) %collective-permute-start.37) | collective-permute-done | bytes 221216 | tf_op jit(solution)/shard_map/ppermute | solution.py:974
  462.4 2.1 take_over.2
  465.1 3.4 collective-permute-done.34
  470.2 3.2 collective-permute-done.36
  (249 shorter events, 77.3 us)
Async XLA Ops:
  3.4 3.2 collective-permute-start
  3.9 59.3 %collective-permute-start.1 = (bf16[1120,512]{1,0:T(8,128)(2,1)}, bf16[1120,512]{1,0:T(8,128)(2,1)S(1)}, u32[]{:S(2)}, u32[]{:S(2)}) collective-permute-start(bf16[1120,512]{1,0:T(8,128)(2,1)} %get-tuple-element.130), channel_id=1, source_target_pairs={{0,16},{16,0},{1,17},{17,1},{2,18},{18,2},{3,19},{19,3},{4,20},{20... | collective-permute-start | bytes 3440648 | tf_op jit(solution)/shard_map/ppermute | solution.py:969
  78.2 34.8 %copy-start.44 = (bf16[1024,1152]{1,0:T(8,128)(2,1)S(1)}, bf16[1024,1152]{1,0:T(8,128)(2,1)}, u32[]{:S(2)}) copy-start(bf16[1024,1152]{1,0:T(8,128)(2,1)} %get-tuple-element.141.grad_ref) | copy-start | bytes 7077892
  125.6 10.2 %collective-permute-start.2 = (bf16[4480,640]{1,0:T(8,128)(2,1)}, bf16[4480,640]{1,0:T(8,128)(2,1)}, u32[]{:S(2)}, u32[]{:S(2)}) collective-permute-start(bf16[4480,640]{1,0:T(8,128)(2,1)} %convolution_convert_fusion.1), channel_id=1, source_target_pairs={{0,16},{16,0},{1,17},{17,1},{2,18},{18,2},{3,19},{19,3},{4,20},{20... | collective-permute-start | bytes 17203208 | tf_op jit(solution)/shard_map/ppermute | solution.py:969
  135.7 19.1 %collective-permute-start.3 = (bf16[1152,2304]{1,0:T(8,128)(2,1)}, bf16[1152,2304]{1,0:T(8,128)(2,1)}, u32[]{:S(2)}, u32[]{:S(2)}) collective-permute-start(bf16[1152,2304]{1,0:T(8,128)(2,1)} %convolution_convert_fusion), channel_id=1, source_target_pairs={{0,16},{16,0},{1,17},{17,1},{2,18},{18,2},{3,19},{19,3},{4,20},{20... | collective-permute-start | bytes 15925256 | tf_op jit(solution)/shard_map/ppermute | solution.py:969
  150.3 52.8 %collective-permute-start.5 = (bf16[2,2,1,2,144,640]{5,4,3,2,1,0:T(8,128)(2,1)}, bf16[2,2,1,2,144,640]{5,4,3,2,1,0:T(8,128)(2,1)}, u32[]{:S(2)}, u32[]{:S(2)}) collective-permute-start(bf16[2,2,1,2,144,640]{5,4,3,2,1,0:T(8,128)(2,1)} %constant_dynamic-slice_fusion.22), channel_id=1, source_target_pairs={{0,2},{1,3},{2,0},{3,1},{4,6},{5,7},{6,4},{7,5},{8,10},{9,11},{10,... | collective-permute-start | bytes 4423688 | tf_op jit(solution)/shard_map/ppermute | solution.py:974
  153.3 49.8 %collective-permute-start.4 = (bf16[2,2,2,1,136,640]{5,4,3,2,1,0:T(8,128)(2,1)}, bf16[2,2,2,1,136,640]{5,4,3,2,1,0:T(8,128)(2,1)}, u32[]{:S(2)}, u32[]{:S(2)}) collective-permute-start(bf16[2,2,2,1,136,640]{5,4,3,2,1,0:T(8,128)(2,1)} %constant_dynamic-slice_fusion.23), channel_id=1, source_target_pairs={{0,1},{1,0},{2,3},{3,2},{4,5},{5,4},{6,7},{7,6},{8,9},{9,8},{10,11... | collective-permute-start | bytes 4177928 | tf_op jit(solution)/shard_map/ppermute | solution.py:974
  210.8 4.2 collective-permute-start.6
  210.9 51.8 %collective-permute-start.10 = (bf16[2,2,1,2,72,1152]{5,4,3,2,1,0:T(8,128)(2,1)}, bf16[2,2,1,2,72,1152]{5,4,3,2,1,0:T(8,128)(2,1)S(1)}, u32[]{:S(2)}, u32[]{:S(2)}) collective-permute-start(bf16[2,2,1,2,72,1152]{5,4,3,2,1,0:T(8,128)(2,1)} %constant_dynamic-slice_fusion.18), channel_id=1, source_target_pairs={{0,2},{1,3},{2,0},{3,1},{4,6},{5,7},{6,4},{7,5},{8,10},{9,11},{10,... | collective-permute-start | bytes 3981320 | tf_op jit(solution)/shard_map/ppermute | solution.py:974
  211.5 51.2 %collective-permute-start.9 = (bf16[2,2,2,1,72,1152]{5,4,3,2,1,0:T(8,128)(2,1)S(1)}, bf16[2,2,2,1,72,1152]{5,4,3,2,1,0:T(8,128)(2,1)S(1)}, u32[]{:S(2)}, u32[]{:S(2)}) collective-permute-start(bf16[2,2,2,1,72,1152]{5,4,3,2,1,0:T(8,128)(2,1)S(1)} %copy-done.26), channel_id=1, source_target_pairs={{0,1},{1,0},{2,3},{3,2},{4,5},{5,4},{6,7},{7,6},{8,9},{9,8},{10,11... | collective-permute-start | bytes 3981320 | tf_op jit(solution)/shard_map/ppermute | solution.py:974
  211.6 51.1 %collective-permute-start.8 = (bf16[2,2,1,1,144,640]{5,4,3,2,1,0:T(8,128)(2,1)}, bf16[2,2,1,1,144,640]{5,4,3,2,1,0:T(8,128)(2,1)}, u32[]{:S(2)}, u32[]{:S(2)}) collective-permute-start(bf16[2,2,1,1,144,640]{5,4,3,2,1,0:T(8,128)(2,1)} %constant_dynamic-slice_fusion.20), channel_id=1, source_target_pairs={{0,1},{1,0},{2,3},{3,2},{4,5},{5,4},{6,7},{7,6},{8,9},{9,8},{10,11... | collective-permute-start | bytes 2211848 | tf_op jit(solution)/shard_map/ppermute | solution.py:974
  213.6 49.2 %collective-permute-start.7 = (bf16[2,2,1,1,136,640]{5,4,3,2,1,0:T(8,128)(2,1)}, bf16[2,2,1,1,136,640]{5,4,3,2,1,0:T(8,128)(2,1)}, u32[]{:S(2)}, u32[]{:S(2)}) collective-permute-start(bf16[2,2,1,1,136,640]{5,4,3,2,1,0:T(8,128)(2,1)} %constant_dynamic-slice_fusion.21), channel_id=1, source_target_pairs={{0,2},{1,3},{2,0},{3,1},{4,6},{5,7},{6,4},{7,5},{8,10},{9,11},{10,... | collective-permute-start | bytes 2088968 | tf_op jit(solution)/shard_map/ppermute | solution.py:974
  220.5 42.3 %collective-permute-start.11 = (bf16[2,1,2,2,72,640]{5,4,3,2,1,0:T(8,128)(2,1)}, bf16[2,1,2,2,72,640]{5,4,3,2,1,0:T(8,128)(2,1)}, u32[]{:S(2)}, u32[]{:S(2)}) collective-permute-start(bf16[2,1,2,2,72,640]{5,4,3,2,1,0:T(8,128)(2,1)} %constant_dynamic-slice_fusion.17), channel_id=1, source_target_pairs={{0,4},{1,5},{2,6},{3,7},{4,0},{5,1},{6,2},{7,3},{8,12},{9,13},{10,... | collective-permute-start | bytes 2211848 | tf_op jit(solution)/shard_map/ppermute | solution.py:974
  272.0 12.1 %collective-permute-start.12 = (bf16[1152,1536]{1,0:T(8,128)(2,1)}, bf16[1152,1536]{1,0:T(8,128)(2,1)}, u32[]{:S(2)}, u32[]{:S(2)}) collective-permute-start(bf16[1152,1536]{1,0:T(8,128)(2,1)} %convolution_convert_fusion.2), channel_id=1, source_target_pairs={{0,16},{16,0},{1,17},{17,1},{2,18},{18,2},{3,19},{19,3},{4,20},{20... | collective-permute-start | bytes 10616840 | tf_op jit(solution)/shard_map/ppermute | solution.py:969
  309.2 8.6 %collective-permute-start.13 = (bf16[1152,512]{1,0:T(8,128)(2,1)}, bf16[1152,512]{1,0:T(8,128)(2,1)}, u32[]{:S(2)}, u32[]{:S(2)}) collective-permute-start(bf16[1152,512]{1,0:T(8,128)(2,1)} %convolution_convert_fusion.4), channel_id=1, source_target_pairs={{0,16},{16,0},{1,17},{17,1},{2,18},{18,2},{3,19},{19,3},{4,20},{20... | collective-permute-start | bytes 3538952 | tf_op jit(solution)/shard_map/ppermute | solution.py:969
  309.6 26.3 %collective-permute-start.14 = (bf16[2,1,1,1,280,640]{5,4,3,2,1,0:T(8,128)(2,1)}, bf16[2,1,1,1,280,640]{5,4,3,2,1,0:T(8,128)(2,1)}, u32[]{:S(2)}, u32[]{:S(2)}) collective-permute-start(bf16[2,1,1,1,280,640]{5,4,3,2,1,0:T(8,128)(2,1)} %fusion.15), channel_id=1, source_target_pairs={{0,4},{1,5},{2,6},{3,7},{4,0},{5,1},{6,2},{7,3},{8,12},{9,13},{10,... | collective-permute-start | bytes 2150408 | tf_op jit(solution)/shard_map/ppermute | solution.py:974
  310.0 24.3 %collective-permute-start.15 = (bf16[2,2,1,1,72,1152]{5,4,3,2,1,0:T(8,128)(2,1)}, bf16[2,2,1,1,72,1152]{5,4,3,2,1,0:T(8,128)(2,1)}, u32[]{:S(2)}, u32[]{:S(2)}) collective-permute-start(bf16[2,2,1,1,72,1152]{5,4,3,2,1,0:T(8,128)(2,1)} %get-tuple-element.178), channel_id=1, source_target_pairs={{0,2},{1,3},{2,0},{3,1},{4,6},{5,7},{6,4},{7,5},{8,10},{9,11},{10,... | collective-permute-start | bytes 1990664 | tf_op jit(solution)/shard_map/ppermute | solution.py:974
  310.6 23.8 %collective-permute-start.16 = (bf16[2,2,1,1,72,1152]{5,4,3,2,1,0:T(8,128)(2,1)}, bf16[2,2,1,1,72,1152]{5,4,3,2,1,0:T(8,128)(2,1)}, u32[]{:S(2)}, u32[]{:S(2)}) collective-permute-start(bf16[2,2,1,1,72,1152]{5,4,3,2,1,0:T(8,128)(2,1)} %get-tuple-element.179), channel_id=1, source_target_pairs={{0,1},{1,0},{2,3},{3,2},{4,5},{5,4},{6,7},{7,6},{8,9},{9,8},{10,11... | collective-permute-start | bytes 1990664 | tf_op jit(solution)/shard_map/ppermute | solution.py:974
  310.7 23.1 %collective-permute-start.17 = (bf16[1,1,2,2,72,640]{5,4,3,2,1,0:T(8,128)(2,1)}, bf16[1,1,2,2,72,640]{5,4,3,2,1,0:T(8,128)(2,1)}, u32[]{:S(2)}, u32[]{:S(2)}) collective-permute-start(bf16[1,1,2,2,72,640]{5,4,3,2,1,0:T(8,128)(2,1)} %constant_dynamic-slice_fusion.14), channel_id=1, source_target_pairs={{0,8},{1,9},{2,10},{3,11},{4,12},{5,13},{6,14},{7,15},{8,0},{9,1},... | collective-permute-start | bytes 1105928 | tf_op jit(solution)/shard_map/ppermute | solution.py:974
  317.0 22.1 %copy-start.5 = (bf16[2,2,1,1,144,640]{5,4,3,2,1,0:T(8,128)(2,1)S(1)}, bf16[2,2,1,1,144,640]{5,4,3,2,1,0:T(8,128)(2,1)}, u32[]{:S(2)}) copy-start(bf16[2,2,1,1,144,640]{5,4,3,2,1,0:T(8,128)(2,1)} %copy-done.4) | copy-start | bytes 2211844
  317.0 22.1 %copy-start.7 = (bf16[2,2,1,1,136,640]{5,4,3,2,1,0:T(8,128)(2,1)S(1)}, bf16[2,2,1,1,136,640]{5,4,3,2,1,0:T(8,128)(2,1)}, u32[]{:S(2)}) copy-start(bf16[2,2,1,1,136,640]{5,4,3,2,1,0:T(8,128)(2,1)} %copy-done.6) | copy-start | bytes 2088964
  317.8 61.2 %collective-permute-start.18 = (bf16[2,2,2,1,72,768]{5,4,3,2,1,0:T(8,128)(2,1)}, bf16[2,2,2,1,72,768]{5,4,3,2,1,0:T(8,128)(2,1)}, u32[]{:S(2)}, u32[]{:S(2)}) collective-permute-start(bf16[2,2,2,1,72,768]{5,4,3,2,1,0:T(8,128)(2,1)} %constant_dynamic-slice_fusion.13), channel_id=1, source_target_pairs={{0,1},{1,0},{2,3},{3,2},{4,5},{5,4},{6,7},{7,6},{8,9},{9,8},{10,11... | collective-permute-start | bytes 2654216 | tf_op jit(solution)/shard_map/ppermute | solution.py:974
  333.8 46.5 %collective-permute-start.19 = (bf16[2,2,1,2,72,768]{5,4,3,2,1,0:T(8,128)(2,1)}, bf16[2,2,1,2,72,768]{5,4,3,2,1,0:T(8,128)(2,1)}, u32[]{:S(2)}, u32[]{:S(2)}) collective-permute-start(bf16[2,2,1,2,72,768]{5,4,3,2,1,0:T(8,128)(2,1)} %constant_dynamic-slice_fusion.12), channel_id=1, source_target_pairs={{0,2},{1,3},{2,0},{3,1},{4,6},{5,7},{6,4},{7,5},{8,10},{9,11},{10,... | collective-permute-start | bytes 2654216 | tf_op jit(solution)/shard_map/ppermute | solution.py:974
  348.8 51.7 %collective-permute-start.41 = (bf16[1,1,1,1,280,640]{5,4,3,2,1,0:T(8,128)(2,1)}, bf16[1,1,1,1,280,640]{5,4,3,2,1,0:T(8,128)(2,1)}, u32[]{:S(2)}, u32[]{:S(2)}) collective-permute-start(bf16[1,1,1,1,280,640]{5,4,3,2,1,0:T(8,128)(2,1)} %constant_dynamic-slice_fusion.9), channel_id=1, source_target_pairs={{0,8},{1,9},{2,10},{3,11},{4,12},{5,13},{6,14},{7,15},{8,0},{9,1},... | collective-permute-start | bytes 1075208 | tf_op jit(solution)/shard_map/ppermute | solution.py:974
  350.7 31.0 %collective-permute-start.20 = (bf16[2,2,2,1,72,256]{5,4,3,2,1,0:T(8,128)(2,1)}, bf16[2,2,2,1,72,256]{5,4,3,2,1,0:T(8,128)(2,1)}, u32[]{:S(2)}, u32[]{:S(2)}) collective-permute-start(bf16[2,2,2,1,72,256]{5,4,3,2,1,0:T(8,128)(2,1)} %constant_dynamic-slice_fusion.11), channel_id=1, source_target_pairs={{0,1},{1,0},{2,3},{3,2},{4,5},{5,4},{6,7},{7,6},{8,9},{9,8},{10,11... | collective-permute-start | bytes 884744 | tf_op jit(solution)/shard_map/ppermute | solution.py:974
  351.1 30.6 %collective-permute-start.21 = (bf16[2,2,1,2,72,256]{5,4,3,2,1,0:T(8,128)(2,1)}, bf16[2,2,1,2,72,256]{5,4,3,2,1,0:T(8,128)(2,1)}, u32[]{:S(2)}, u32[]{:S(2)}) collective-permute-start(bf16[2,2,1,2,72,256]{5,4,3,2,1,0:T(8,128)(2,1)} %constant_dynamic-slice_fusion.10), channel_id=1, source_target_pairs={{0,2},{1,3},{2,0},{3,1},{4,6},{5,7},{6,4},{7,5},{8,10},{9,11},{10,... | collective-permute-start | bytes 884744 | tf_op jit(solution)/shard_map/ppermute | solution.py:974
  379.0 34.0 %collective-permute-start.23 = (bf16[2,1,1,1,72,2304]{5,4,3,2,1,0:T(8,128)(2,1)}, bf16[2,1,1,1,72,2304]{5,4,3,2,1,0:T(8,128)(2,1)S(1)}, u32[]{:S(2)}, u32[]{:S(2)}) collective-permute-start(bf16[2,1,1,1,72,2304]{5,4,3,2,1,0:T(8,128)(2,1)} %fusion.17), channel_id=1, source_target_pairs={{0,4},{1,5},{2,6},{3,7},{4,0},{5,1},{6,2},{7,3},{8,12},{9,13},{10,... | collective-permute-start | bytes 1990664 | tf_op jit(solution)/shard_map/ppermute | solution.py:974
  380.3 21.3 %collective-permute-start.24 = (bf16[1,1,2,1,72,640]{5,4,3,2,1,0:T(8,128)(2,1)}, bf16[1,1,2,1,72,640]{5,4,3,2,1,0:T(8,128)(2,1)S(1)}, u32[]{:S(2)}, u32[]{:S(2)}) collective-permute-start(bf16[1,1,2,1,72,640]{5,4,3,2,1,0:T(8,128)(2,1)} %constant_dynamic-slice_fusion.8), channel_id=1, source_target_pairs={{0,1},{1,0},{2,3},{3,2},{4,5},{5,4},{6,7},{7,6},{8,9},{9,8},{10,11... | collective-permute-start | bytes 552968 | tf_op jit(solution)/shard_map/ppermute | solution.py:974
  399.3 13.7 %copy-start.25 = (bf16[1,1,2,2,72,640]{5,4,3,2,1,0:T(8,128)(2,1)S(1)}, bf16[1,1,2,2,72,640]{5,4,3,2,1,0:T(8,128)(2,1)}, u32[]{:S(2)}) copy-start(bf16[1,1,2,2,72,640]{5,4,3,2,1,0:T(8,128)(2,1)} %copy-done.24) | copy-start | bytes 1105924
  399.3 13.8 %copy-start.9 = (bf16[2,2,1,1,72,1152]{5,4,3,2,1,0:T(8,128)(2,1)S(1)}, bf16[2,2,1,1,72,1152]{5,4,3,2,1,0:T(8,128)(2,1)}, u32[]{:S(2)}) copy-start(bf16[2,2,1,1,72,1152]{5,4,3,2,1,0:T(8,128)(2,1)} %copy-done.8) | copy-start | bytes 1990660
  399.3 13.8 %copy-start.11 = (bf16[2,2,1,1,72,1152]{5,4,3,2,1,0:T(8,128)(2,1)S(1)}, bf16[2,2,1,1,72,1152]{5,4,3,2,1,0:T(8,128)(2,1)}, u32[]{:S(2)}) copy-start(bf16[2,2,1,1,72,1152]{5,4,3,2,1,0:T(8,128)(2,1)} %copy-done.10) | copy-start | bytes 1990660
  399.3 13.7 %collective-permute-start.26 = (bf16[2,2,1,1,72,768]{5,4,3,2,1,0:T(8,128)(2,1)S(1)}, bf16[2,2,1,1,72,768]{5,4,3,2,1,0:T(8,128)(2,1)S(1)}, u32[]{:S(2)}, u32[]{:S(2)}) collective-permute-start(bf16[2,2,1,1,72,768]{5,4,3,2,1,0:T(8,128)(2,1)S(1)} %constant_dynamic-slice_fusion.7), channel_id=1, source_target_pairs={{0,2},{1,3},{2,0},{3,1},{4,6},{5,7},{6,4},{7,5},{8,10},{9,11},{10,... | collective-permute-start | bytes 1327112 | tf_op jit(solution)/shard_map/ppermute | solution.py:974
  399.9 13.1 %collective-permute-start.27 = (bf16[2,2,1,1,72,768]{5,4,3,2,1,0:T(8,128)(2,1)}, bf16[2,2,1,1,72,768]{5,4,3,2,1,0:T(8,128)(2,1)S(1)}, u32[]{:S(2)}, u32[]{:S(2)}) collective-permute-start(bf16[2,2,1,1,72,768]{5,4,3,2,1,0:T(8,128)(2,1)} %constant_dynamic-slice_fusion.6), channel_id=1, source_target_pairs={{0,1},{1,0},{2,3},{3,2},{4,5},{5,4},{6,7},{7,6},{8,9},{9,8},{10,11... | collective-permute-start | bytes 1327112 | tf_op jit(solution)/shard_map/ppermute | solution.py:974
  400.5 2.6 collective-permute-start.25
  401.6 10.8 %collective-permute-start.28 = (bf16[2,2,1,1,72,256]{5,4,3,2,1,0:T(8,128)(2,1)S(1)}, bf16[2,2,1,1,72,256]{5,4,3,2,1,0:T(8,128)(2,1)S(1)}, u32[]{:S(2)}, u32[]{:S(2)}) collective-permute-start(bf16[2,2,1,1,72,256]{5,4,3,2,1,0:T(8,128)(2,1)S(1)} %constant_dynamic-slice_fusion.5), channel_id=1, source_target_pairs={{0,2},{1,3},{2,0},{3,1},{4,6},{5,7},{6,4},{7,5},{8,10},{9,11},{10,... | collective-permute-start | bytes 442376 | tf_op jit(solution)/shard_map/ppermute | solution.py:974
  403.2 9.8 %collective-permute-start.29 = (bf16[2,2,1,1,72,256]{5,4,3,2,1,0:T(8,128)(2,1)S(1)}, bf16[2,2,1,1,72,256]{5,4,3,2,1,0:T(8,128)(2,1)S(1)}, u32[]{:S(2)}, u32[]{:S(2)}) collective-permute-start(bf16[2,2,1,1,72,256]{5,4,3,2,1,0:T(8,128)(2,1)S(1)} %constant_dynamic-slice_fusion.4), channel_id=1, source_target_pairs={{0,1},{1,0},{2,3},{3,2},{4,5},{5,4},{6,7},{7,6},{8,9},{9,8},{10,11... | collective-permute-start | bytes 442376 | tf_op jit(solution)/shard_map/ppermute | solution.py:974
  412.4 34.1 %collective-permute-start.35 = (bf16[1120,512]{1,0:T(8,128)(2,1)}, bf16[1120,512]{1,0:T(8,128)(2,1)}, u32[]{:S(2)}, u32[]{:S(2)}) collective-permute-start(bf16[1120,512]{1,0:T(8,128)(2,1)} %get-tuple-element.192), channel_id=1, source_target_pairs={{0,16},{16,0},{1,17},{17,1},{2,18},{18,2},{3,19},{19,3},{4,20},{20... | collective-permute-start | bytes 3440648 | tf_op jit(solution)/shard_map/ppermute | solution.py:969
  412.9 48.4 %collective-permute-start.22 = (bf16[1120,512]{1,0:T(8,128)(2,1)S(1)}, bf16[1120,512]{1,0:T(8,128)(2,1)S(1)}, u32[]{:S(2)}, u32[]{:S(2)}) collective-permute-start(bf16[1120,512]{1,0:T(8,128)(2,1)S(1)} %copy-done.32), channel_id=1, source_target_pairs={{0,16},{16,0},{1,17},{17,1},{2,18},{18,2},{3,19},{19,3},{4,20},{20... | collective-permute-start | bytes 3440648 | tf_op jit(solution)/shard_map/ppermute | solution.py:969
  413.8 18.6 %collective-permute-start.40 = (bf16[1,1,1,1,72,2304]{5,4,3,2,1,0:T(8,128)(2,1)S(1)}, bf16[1,1,1,1,72,2304]{5,4,3,2,1,0:T(8,128)(2,1)S(1)}, u32[]{:S(2)}, u32[]{:S(2)}) collective-permute-start(bf16[1,1,1,1,72,2304]{5,4,3,2,1,0:T(8,128)(2,1)S(1)} %constant_dynamic-slice_fusion.3), channel_id=1, source_target_pairs={{0,8},{1,9},{2,10},{3,11},{4,12},{5,13},{6,14},{7,15},{8,0},{9,1},... | collective-permute-start | bytes 995336 | tf_op jit(solution)/shard_map/ppermute | solution.py:974
  416.4 13.5 %collective-permute-start.39 = (bf16[1,1,1,1,72,640]{5,4,3,2,1,0:T(8,128)(2,1)S(1)}, bf16[1,1,1,1,72,640]{5,4,3,2,1,0:T(8,128)(2,1)S(1)}, u32[]{:S(2)}, u32[]{:S(2)}) collective-permute-start(bf16[1,1,1,1,72,640]{5,4,3,2,1,0:T(8,128)(2,1)S(1)} %constant_dynamic-slice_fusion.2), channel_id=1, source_target_pairs={{0,2},{1,3},{2,0},{3,1},{4,6},{5,7},{6,4},{7,5},{8,10},{9,11},{10,... | collective-permute-start | bytes 276488 | tf_op jit(solution)/shard_map/ppermute | solution.py:974
  429.5 15.2 %collective-permute-start.31 = (bf16[2,1,1,1,72,1536]{5,4,3,2,1,0:T(8,128)(2,1)S(1)}, bf16[2,1,1,1,72,1536]{5,4,3,2,1,0:T(8,128)(2,1)S(1)}, u32[]{:S(2)}, u32[]{:S(2)}) collective-permute-start(bf16[2,1,1,1,72,1536]{5,4,3,2,1,0:T(8,128)(2,1)S(1)} %fusion.19), channel_id=1, source_target_pairs={{0,4},{1,5},{2,6},{3,7},{4,0},{5,1},{6,2},{7,3},{8,12},{9,13},{10,... | collective-permute-start | bytes 1327112 | tf_op jit(solution)/shard_map/ppermute | solution.py:974
  429.9 14.8 %collective-permute-start.32 = (bf16[2,1,1,1,72,512]{5,4,3,2,1,0:T(8,128)(2,1)S(1)}, bf16[2,1,1,1,72,512]{5,4,3,2,1,0:T(8,128)(2,1)S(1)}, u32[]{:S(2)}, u32[]{:S(2)}) collective-permute-start(bf16[2,1,1,1,72,512]{5,4,3,2,1,0:T(8,128)(2,1)S(1)} %fusion.21), channel_id=1, source_target_pairs={{0,4},{1,5},{2,6},{3,7},{4,0},{5,1},{6,2},{7,3},{8,12},{9,13},{10,... | collective-permute-start | bytes 442376 | tf_op jit(solution)/shard_map/ppermute | solution.py:974
  432.4 4.0 collective-permute-start.30
  444.9 7.6 %collective-permute-start.38 = (bf16[1,1,1,1,72,512]{5,4,3,2,1,0:T(8,128)(2,1)S(1)}, bf16[1,1,1,1,72,512]{5,4,3,2,1,0:T(8,128)(2,1)S(1)}, u32[]{:S(2)}, u32[]{:S(2)}) collective-permute-start(bf16[1,1,1,1,72,512]{5,4,3,2,1,0:T(8,128)(2,1)S(1)} %constant_dynamic-slice_fusion), channel_id=1, source_target_pairs={{0,8},{1,9},{2,10},{3,11},{4,12},{5,13},{6,14},{7,15},{8,0},{9,1},... | collective-permute-start | bytes 221192 | tf_op jit(solution)/shard_map/ppermute | solution.py:974
  448.6 12.7 %collective-permute-start.37 = (bf16[1,1,1,1,72,1536]{5,4,3,2,1,0:T(8,128)(2,1)S(1)}, bf16[1,1,1,1,72,1536]{5,4,3,2,1,0:T(8,128)(2,1)S(1)}, u32[]{:S(2)}, u32[]{:S(2)}) collective-permute-start(bf16[1,1,1,1,72,1536]{5,4,3,2,1,0:T(8,128)(2,1)S(1)} %constant_dynamic-slice_fusion.1), channel_id=1, source_target_pairs={{0,8},{1,9},{2,10},{3,11},{4,12},{5,13},{6,14},{7,15},{8,0},{9,1},... | collective-permute-start | bytes 663560 | tf_op jit(solution)/shard_map/ppermute | solution.py:974
  451.1 13.4 %collective-permute-start.33 = (f32[8,1120]{1,0:T(8,128)S(1)}, f32[8,1120]{1,0:T(8,128)S(1)}, u32[]{:S(2)}, u32[]{:S(2)}) collective-permute-start(f32[8,1120]{1,0:T(8,128)S(1)} %add.263), channel_id=1, source_target_pairs={{0,2},{1,3},{2,0},{3,1},{4,6},{5,7},{6,4},{7,5},{8,10},{9,11},{10,... | collective-permute-start | bytes 107528 | tf_op jit(solution)/shard_map/ppermute | solution.py:974
  464.5 4.0 collective-permute-start.34
  468.5 4.9 %collective-permute-start.36 = (f32[8,1120]{1,0:T(8,128)S(1)}, f32[8,1120]{1,0:T(8,128)S(1)}, u32[]{:S(2)}, u32[]{:S(2)}) collective-permute-start(f32[8,1120]{1,0:T(8,128)S(1)} %add.267), channel_id=1, source_target_pairs={{0,8},{1,9},{2,10},{3,11},{4,12},{5,13},{6,14},{7,15},{8,0},{9,1},... | collective-permute-start | bytes 107528 | tf_op jit(solution)/shard_map/ppermute | solution.py:974
  (43 other events, 192.5 us)
